TPU v7x, 32 devices: a whole 2x2x4 slice. The times are simulated.
32 devices in a mesh: dp: 4 (over y, core), fsdp: 8 (over z, x).
Axes of the slice: x: 2, y: 2, z: 4, core: 2. Of those that a mesh axis runs over, the one named last changes fastest.
Arguments:
- hidden_states: bfloat16 [16384, 1280], P(('dp', 'fsdp')), may hold values from -9 to 9
- clip_lengths: int32 [8], replicated, may hold values from 512 to 2048, as said below
- norm_gains: float32 [2, 1280], replicated, may hold values from 0.25 to 1.75
- norm_shifts: float32 [2, 1280], replicated, may hold values from -1.5 to 1.5
- proj_biases: float32 [4, 1280], replicated, may hold values from -1 to 1
- up_bias: float32 [5120], replicated, may hold values from -1.5 to 1.5
- in_proj: bfloat16 [3840, 1280], P('fsdp'), may hold values from -0.15625 to 0.15625
- out_proj: bfloat16 [1280, 1280], P('fsdp'), may hold values from -0.3125 to 0.3125
- up_proj: bfloat16 [5120, 1280], P('fsdp'), may hold values from -0.15625 to 0.15625
- down_proj: bfloat16 [1280, 5120], P('fsdp'), may hold values from -0.078125 to 0.078125
- cotangent: bfloat16 [16384, 1280], P(('dp', 'fsdp')), may hold values from -6 to 6
Outputs:
- layer_out: bfloat16 [16384, 1280], P(('dp', 'fsdp'))
- grad_hidden: bfloat16 [16384, 1280], P(('dp', 'fsdp'))
- grad_in_proj: float32 [3840, 1280], P('fsdp')
- grad_out_proj: float32 [1280, 1280], P('fsdp')
- grad_up_proj: float32 [5120, 1280], P('fsdp')
- grad_down_proj: float32 [1280, 5120], P('fsdp')
- grad_gains: float32 [2, 1280], replicated
- grad_shifts: float32 [2, 1280], replicated
- grad_biases: float32 [4, 1280], replicated
- grad_up_bias: float32 [5120], replicated
- root_means: float32 [3], replicated
Inputs may be any that keep to these rules, and one draw needn't show every extreme that they name: Clip c owns the 2048 slots from c * 2048 on; its first clip_lengths[c] slots hold frames, the rest padding. Some clip fills all its slots in every draw.
All inputs are finite; a program needn't handle non-finite values.
Results may differ from a plain program's by a relative error of at most 0.015.
Values may be sent and summed in bfloat16 or wider, within the bound.
No kernel may reach another device: no remote copies, remote signals or barrier semaphores. Data moves between devices by JAX's collectives and lax.ppermute only.
A program may use at most 384 MiB of HBM per device.

v0:
```python
import jax
import jax.numpy as jnp
from jax import lax
from jax.sharding import PartitionSpec as P

H = 16
HD = 80
CLIP_DEV = 4


epsilon = 1e-05
group_heads = 4


def partner(value, axis, stride):
    mask = 2**stride
    pairs = [(source, source ^ mask) for source in range(lax.axis_size(axis))]
    return lax.ppermute(value, axis, pairs)


def norm_rows(values, gain_row, shift_row):
    center = values - jnp.mean(values, axis=-1, keepdims=True)
    spread = jnp.mean(center * center, axis=-1, keepdims=True)
    return center * lax.rsqrt(spread + epsilon) * gain_row + shift_row


def gelu_exact(values):
    return jax.nn.gelu(values, approximate=False)


def times_rows(operand, weight):
    return lax.dot_general(
        operand, weight, (((1,), (1,)), ((), ())), preferred_element_type=jnp.float32
    )


def times_plain(operand, weight):
    return jnp.dot(operand, weight, preferred_element_type=jnp.float32)


def grad_terms(grad_rows, inputs):
    return lax.dot_general(
        grad_rows, inputs, (((0,), (0,)), ((), ())), preferred_element_type=jnp.float32
    )


def fold_rows(operand, block_rows):
    return times_plain(operand, block_rows)


def on_device(
    hidden_states,
    clip_lengths,
    norm_gains,
    norm_shifts,
    proj_biases,
    up_bias,
    in_proj,
    out_proj,
    up_proj,
    down_proj,
    cotangent,
):
    tokens_here = hidden_states.shape[0]
    model_width = hidden_states.shape[1]
    fsdp_count = lax.axis_size("fsdp")
    fsdp_index = lax.axis_index("fsdp")
    device = lax.axis_index("dp") * fsdp_count + fsdp_index
    levels = CLIP_DEV.bit_length() - 1
    region = device // CLIP_DEV
    region_place = device % CLIP_DEV
    length = lax.dynamic_index_in_dim(clip_lengths, region, keepdims=False)
    region_span = tokens_here * CLIP_DEV
    row_place = region_place * tokens_here + jnp.arange(tokens_here, dtype=jnp.int32)
    row_valid = (row_place < length).astype(jnp.float32)
    key_valid = jnp.arange(region_span, dtype=jnp.int32) < length
    scale_factor = HD ** (-0.5)
    head_span = group_heads * HD
    head_groups = H // group_heads
    inputs = hidden_states.astype(jnp.float32)
    normed_one, first_back = jax.vjp(norm_rows, inputs, norm_gains[0], norm_shifts[0])
    normed_low = normed_one.astype(jnp.bfloat16)
    projected = times_rows(normed_low, lax.all_gather(in_proj, "fsdp", axis=0, tiled=True))
    queries = (projected[:, :model_width] + proj_biases[0]).astype(jnp.bfloat16)
    region_keys = projected[:, model_width : 2 * model_width].astype(jnp.bfloat16)
    region_values = (projected[:, 2 * model_width :] + proj_biases[1]).astype(jnp.bfloat16)
    for level_bit in range(levels):
        other_keys, other_values = partner((region_keys, region_values), "fsdp", level_bit)
        upper_half = fsdp_index // 2**level_bit % 2 == 1
        region_keys = jnp.where(
            upper_half,
            jnp.concatenate([other_keys, region_keys]),
            jnp.concatenate([region_keys, other_keys]),
        )
        region_values = jnp.where(
            upper_half,
            jnp.concatenate([other_values, region_values]),
            jnp.concatenate([region_values, other_values]),
        )
    attended = []
    log_sums = []
    for head_group in range(head_groups):
        columns = slice(head_group * head_span, (head_group + 1) * head_span)
        query_group = queries[:, columns].reshape(tokens_here, group_heads, HD)
        key_group = region_keys[:, columns].reshape(region_span, group_heads, HD)
        value_group = region_values[:, columns].reshape(region_span, group_heads, HD)
        scores = (
            jnp.einsum("qhd,khd->hqk", query_group, key_group, preferred_element_type=jnp.float32)
            * scale_factor
        )
        scores = jnp.where(key_valid, scores, -1e30)
        largest = jnp.max(scores, axis=-1, keepdims=True)
        exponent = jnp.exp(scores - largest)
        summed = jnp.sum(exponent, axis=-1, keepdims=True)
        weights_soft = exponent / summed
        log_sums.append(largest + jnp.log(summed))
        attended.append(
            jnp.einsum(
                "hqk,khd->qhd",
                weights_soft.astype(jnp.bfloat16),
                value_group,
                preferred_element_type=jnp.float32,
            ).reshape(tokens_here, head_span)
        )
    context_low = jnp.concatenate(attended, axis=1).astype(jnp.bfloat16)
    attention = (
        times_rows(context_low, lax.all_gather(out_proj, "fsdp", axis=0, tiled=True))
        + proj_biases[2]
    )
    middle = inputs + attention
    normed_two, second_back = jax.vjp(norm_rows, middle, norm_gains[1], norm_shifts[1])
    normed_second = normed_two.astype(jnp.bfloat16)
    widened = (
        times_rows(normed_second, lax.all_gather(up_proj, "fsdp", axis=0, tiled=True)) + up_bias
    )
    activated, gelu_back = jax.vjp(gelu_exact, widened)
    activated_low = activated.astype(jnp.bfloat16)
    feedforward = (
        times_rows(activated_low, lax.all_gather(down_proj, "fsdp", axis=0, tiled=True))
        + proj_biases[3]
    )
    outputs = middle + feedforward
    stat_terms = jnp.stack(
        [
            jnp.sum(row_valid * jnp.sum(middle * middle, axis=1)),
            jnp.sum(row_valid * jnp.sum(attention * attention, axis=1)),
            jnp.sum(row_valid * jnp.sum(feedforward * feedforward, axis=1)),
        ]
    )
    grad_out = cotangent.astype(jnp.float32)
    grad_activated = fold_rows(cotangent, lax.all_gather(down_proj, "fsdp", axis=0, tiled=True))
    grad_widened = gelu_back(grad_activated)[0].astype(jnp.bfloat16)
    grad_up_bias = jnp.sum(grad_widened.astype(jnp.float32), axis=0)
    grad_normed_two = fold_rows(grad_widened, lax.all_gather(up_proj, "fsdp", axis=0, tiled=True))
    grad_middle_norm, grad_gain_two, grad_shift_two = second_back(grad_normed_two)
    grad_middle = grad_out + grad_middle_norm
    grad_attention = grad_middle.astype(jnp.bfloat16)
    grad_context = fold_rows(grad_attention, lax.all_gather(out_proj, "fsdp", axis=0, tiled=True))
    grad_context_low = grad_context.astype(jnp.bfloat16)
    query_parts = []
    key_parts = []
    value_parts = []
    for head_group in range(head_groups):
        columns = slice(head_group * head_span, (head_group + 1) * head_span)
        query_group = queries[:, columns].reshape(tokens_here, group_heads, HD)
        key_group = region_keys[:, columns].reshape(region_span, group_heads, HD)
        value_group = region_values[:, columns].reshape(region_span, group_heads, HD)
        grad_group = grad_context_low[:, columns].reshape(tokens_here, group_heads, HD)
        scores = (
            jnp.einsum("qhd,khd->hqk", query_group, key_group, preferred_element_type=jnp.float32)
            * scale_factor
        )
        scores = jnp.where(key_valid, scores, -1e30)
        weights_soft = jnp.exp(scores - log_sums[head_group])
        value_parts.append(
            jnp.einsum(
                "hqk,qhd->khd",
                weights_soft.astype(jnp.bfloat16),
                grad_group,
                preferred_element_type=jnp.float32,
            ).reshape(region_span, head_span)
        )
        grad_soft = jnp.einsum(
            "qhd,khd->hqk", grad_group, value_group, preferred_element_type=jnp.float32
        )
        grad_scores = (
            weights_soft * (grad_soft - jnp.sum(weights_soft * grad_soft, axis=-1, keepdims=True))
        ).astype(jnp.bfloat16)
        query_parts.append(
            jnp.einsum(
                "hqk,khd->qhd", grad_scores, key_group, preferred_element_type=jnp.float32
            ).reshape(tokens_here, head_span)
            * scale_factor
        )
        key_parts.append(
            jnp.einsum(
                "hqk,qhd->khd", grad_scores, query_group, preferred_element_type=jnp.float32
            ).reshape(region_span, head_span)
            * scale_factor
        )
    grad_keys = jnp.concatenate(key_parts, axis=1)
    grad_values = jnp.concatenate(value_parts, axis=1)
    for level_bit in reversed(range(levels)):
        half_rows = grad_keys.shape[0] // 2
        upper_half = fsdp_index // 2**level_bit % 2 == 1
        own_keys = jnp.where(upper_half, grad_keys[half_rows:], grad_keys[:half_rows])
        sent_keys = jnp.where(upper_half, grad_keys[:half_rows], grad_keys[half_rows:])
        own_values = jnp.where(upper_half, grad_values[half_rows:], grad_values[:half_rows])
        sent_values = jnp.where(upper_half, grad_values[:half_rows], grad_values[half_rows:])
        came_keys, came_values = (
            partner(sent_keys.astype(jnp.bfloat16), "fsdp", level_bit).astype(sent_keys.dtype),
            partner(sent_values.astype(jnp.bfloat16), "fsdp", level_bit).astype(sent_values.dtype),
        )
        grad_keys = own_keys + came_keys
        grad_values = own_values + came_values
    grad_query_low = jnp.concatenate(query_parts, axis=1).astype(jnp.bfloat16)
    grad_keys_low = grad_keys.astype(jnp.bfloat16)
    grad_values_low = grad_values.astype(jnp.bfloat16)
    grad_projected = jnp.concatenate([grad_query_low, grad_keys_low, grad_values_low], axis=1)
    grad_normed_one = fold_rows(grad_projected, lax.all_gather(in_proj, "fsdp", axis=0, tiled=True))
    grad_inputs_norm, grad_gain_one, grad_shift_one = first_back(grad_normed_one)
    grad_hidden = (grad_middle + grad_inputs_norm).astype(jnp.bfloat16)
    grad_entry = grad_terms(grad_projected, normed_low)
    grad_exit = grad_terms(grad_attention, context_low)
    grad_up = grad_terms(grad_widened, normed_second)
    grad_down = grad_terms(cotangent, activated_low)
    shard_grads = (
        lax.psum_scatter(
            grad_entry.astype(jnp.bfloat16), "fsdp", scatter_dimension=0, tiled=True
        ).astype(jnp.float32),
        lax.psum_scatter(
            grad_exit.astype(jnp.bfloat16), "fsdp", scatter_dimension=0, tiled=True
        ).astype(jnp.float32),
        lax.psum_scatter(
            grad_up.astype(jnp.bfloat16), "fsdp", scatter_dimension=0, tiled=True
        ).astype(jnp.float32),
        lax.psum_scatter(
            grad_down.astype(jnp.bfloat16), "fsdp", scatter_dimension=0, tiled=True
        ).astype(jnp.float32),
    )
    shard_grads = (
        lax.psum(shard_grads[0].astype(jnp.bfloat16), "dp").astype(jnp.float32),
        lax.psum(shard_grads[1].astype(jnp.bfloat16), "dp").astype(jnp.float32),
        lax.psum(shard_grads[2].astype(jnp.bfloat16), "dp").astype(jnp.float32),
        lax.psum(shard_grads[3].astype(jnp.bfloat16), "dp").astype(jnp.float32),
    )
    bias_terms = jnp.stack(
        [
            jnp.sum(grad_query_low.astype(jnp.float32), axis=0),
            jnp.sum(grad_values_low.astype(jnp.float32), axis=0),
            jnp.sum(grad_attention.astype(jnp.float32), axis=0),
            jnp.sum(grad_out, axis=0),
        ]
    )
    small_totals = lax.psum(
        (
            jnp.stack([grad_gain_one, grad_gain_two]),
            jnp.stack([grad_shift_one, grad_shift_two]),
            bias_terms,
            grad_up_bias,
            stat_terms,
        ),
        ("dp", "fsdp"),
    )
    valid_count = jnp.sum(clip_lengths).astype(jnp.float32) * model_width
    root_means = jnp.sqrt(small_totals[4] / valid_count)
    return (
        outputs.astype(jnp.bfloat16),
        grad_hidden,
        shard_grads[0],
        shard_grads[1],
        shard_grads[2],
        shard_grads[3],
        small_totals[0],
        small_totals[1],
        small_totals[2],
        small_totals[3],
        root_means,
    )


def solution(mesh):
    in_specs = (
        P(("dp", "fsdp"), None),
        P(),
        P(),
        P(),
        P(),
        P(),
        P("fsdp", None),
        P("fsdp", None),
        P("fsdp", None),
        P("fsdp", None),
        P(("dp", "fsdp"), None),
    )
    out_specs = (
        P(("dp", "fsdp"), None),
        P(("dp", "fsdp"), None),
        P("fsdp", None),
        P("fsdp", None),
        P("fsdp", None),
        P("fsdp", None),
        P(),
        P(),
        P(),
        P(),
        P(),
    )
    return jax.shard_map(
        on_device, mesh=mesh, in_specs=in_specs, out_specs=out_specs, check_vma=False
    )
```

profile of v0, /device:TPU:3, one launch (start us, length us, event | category | flops | bytes accessed | tf_op | source)
XLA Modules:
  0.0 1673.1 jit_solution(14728812984768785608)
XLA Ops:
  13.5 139.5 %all-gather.5.cloned.1.call-done = bf16[3840,1280]{1,0:T(8,128)(2,1)} async-done(((bf16[480,1280]{1,0:T(8,128)(2,1)}), bf16[3840,1280]{1,0:T(8,128)(2,1)}) %all-gather.5.cloned.1.call-update) | async-done | bytes 9830416 | tf_op jit(solution)/shard_map/all_gather | solution.py:83
  165.6 39.4 %collective-permute-done.2 = bf16[512,1280]{1,0:T(8,128)(2,1)} collective-permute-done((bf16[512,1280]{1,0:T(8,128)(2,1)S(1)}, bf16[512,1280]{1,0:T(8,128)(2,1)}, u32[]{:S(2)}, u32[]{:S(2)}) %collective-permute-start.2) | collective-permute-done | bytes 1310752 | tf_op jit(solution)/shard_map/ppermute | solution.py:18
  225.0 17.8 %collective-permute-done = bf16[512,1280]{1,0:T(8,128)(2,1)} collective-permute-done((bf16[512,1280]{1,0:T(8,128)(2,1)}, bf16[512,1280]{1,0:T(8,128)(2,1)}, u32[]{:S(2)}, u32[]{:S(2)}) %collective-permute-start) | collective-permute-done | bytes 1310752 | tf_op jit(solution)/shard_map/ppermute | solution.py:18
  246.9 77.6 %collective-permute-done.3 = bf16[1024,1280]{1,0:T(8,128)(2,1)} collective-permute-done((bf16[1024,1280]{1,0:T(8,128)(2,1)S(1)}, bf16[1024,1280]{1,0:T(8,128)(2,1)}, u32[]{:S(2)}, u32[]{:S(2)}) %collective-permute-start.3) | collective-permute-done | bytes 2621472 | tf_op jit(solution)/shard_map/ppermute | solution.py:18
  367.5 76.9 %collective-permute-done.1 = bf16[1024,1280]{1,0:T(8,128)(2,1)} collective-permute-done((bf16[1024,1280]{1,0:T(8,128)(2,1)}, bf16[1024,1280]{1,0:T(8,128)(2,1)}, u32[]{:S(2)}, u32[]{:S(2)}) %collective-permute-start.1) | collective-permute-done | bytes 2621472 | tf_op jit(solution)/shard_map/ppermute | solution.py:18
  462.8 23.8 %fusion.31 = (f32[4,512]{1,0:T(4,128)S(1)}, f32[4,512]{1,0:T(4,128)S(1)}, f32[4,512]{1,0:T(4,128)S(1)}, f32[4,512]{1,0:T(4,128)S(1)}, f32[4,512,2048]{2,1,0:T(8,128)}) fusion(pred[2048]{0:T(1024)(128)(4,1)S(1)} %iota_compare_fusion, f32[4,512,2048]{2,1,0:T(8,128)} %fusion.92, f32[4,512,2048]{2,1,0:T(8,128)} %fusion.93, f32[4,512,2048]{2,1,0:T(8,128)} %fusion.94, ...), kind=kOutput, calls=%fused_computation.69 | convolution fusion | flops 721412096 | bytes 68782080 | tf_op jit(solution)/shard_map/qhd,khd->hqk/dot_general | solution.py:108
  486.6 25.7 %fusion.1 = (f32[4,512]{1,0:T(4,128)S(1)}, f32[4,512]{1,0:T(4,128)S(1)}, f32[4,512]{1,0:T(4,128)S(1)}, f32[4,512]{1,0:T(4,128)S(1)}) fusion(f32[4,512]{1,0:T(4,128)S(1)} %get-tuple-element.68, f32[4,512,2048]{2,1,0:T(8,128)} %get-tuple-element.121, pred[2048]{0:T(1024)(128)(4,1)S(1)} %iota_compare_fusion, f32[4,512]{1,0:T(4,128)S(1)} %get-tuple-element.71, ...), kind=kLoop, calls=%fused_computation.29 | loop fusion | flops 67100672 | bytes 67176448 | tf_op jit(solution)/shard_map/reduce_sum | solution.py:114
  551.8 14.9 fusion.82
  566.7 112.4 %all-gather.11.cloned.1.call-done = bf16[1280,5120]{1,0:T(8,128)(2,1)} async-done(((bf16[160,5120]{1,0:T(8,128)(2,1)}), bf16[1280,5120]{1,0:T(8,128)(2,1)}) %all-gather.11.cloned.1.call-update) | async-done | bytes 13107216 | tf_op jit(solution)/shard_map/all_gather | solution.py:139
  679.1 35.2 %convert_reduce_fusion = (f32[5120]{0:T(1024)}, bf16[512,5120]{1,0:T(8,128)(2,1)}, f32[512,5120]{1,0:T(8,128)S(1)}) fusion(f32[512,5120]{1,0:T(8,128)} %fusion.82, f32[5120]{0:T(1024)S(1)} %copy-done.57, bf16[512,1280]{1,0:T(8,128)(2,1)S(1)} %copy-done.28, bf16[1280,5120]{1,0:T(8,128)(2,1)} %all-gather.11.cloned.1.call-done), kind=kOutput, calls=%fused_computation.40 | convolution fusion | flops 6907489280 | bytes 40673280 | tf_op jit(solution)/shard_map/dot_general | solution.py:38
  714.3 14.9 multiply_reduce_fusion.7
  743.5 17.6 %copy.89 = bf16[1280,5120]{1,0:T(8,128)(2,1)} copy(bf16[1280,5120]{0,1:T(8,128)(2,1)} %fusion) | data formatting | bytes 26214400
  761.8 16.1 multiply_reduce_fusion.4
  854.3 39.0 %multiply_reduce_fusion = (f32[4,512]{1,0:T(4,128)S(1)}, f32[4,512]{1,0:T(4,128)S(1)}, f32[4,512]{1,0:T(4,128)S(1)}, f32[4,512]{1,0:T(4,128)S(1)}, f32[4,512,2048]{2,1,0:T(8,128)}) fusion(f32[4,512]{1,0:T(4,128)S(1)} %copy-done.47, f32[4,512,2048]{2,1,0:T(8,128)} %fusion.94, pred[2048]{0:T(1024)(128)(4,1)S(1)} %copy-done.51, f32[4,512,2048]{2,1,0:T(8,128)} %fusion.97, ...), kind=kOutput, calls=%fused_computation.3 | convolution fusion | flops 754966528 | bytes 135923712 | tf_op jit(solution)/shard_map/qhd,khd->hqk/dot_general | solution.py:183
  893.3 53.1 %multiply_convert_fusion = (bf16[4,512,2048]{2,1,0:T(8,128)(2,1)S(1)}, bf16[4,512,2048]{2,1,0:T(8,128)(2,1)}, bf16[4,512,2048]{2,1,0:T(8,128)(2,1)}, bf16[4,512,2048]{2,1,0:T(8,128)(2,1)}) fusion(f32[4,512,2048]{2,1,0:T(8,128)} %get-tuple-element.123, f32[4,512]{1,0:T(4,128)S(1)} %get-tuple-element.60, f32[4,512]{1,0:T(4,128)S(1)} %copy-done.47, ...), kind=kLoop, calls=%fused_computation.2 | loop fusion | flops 100663296 | bytes 167839744 | tf_op jit(solution)/shard_map/convert_element_type | solution.py:188
  998.9 71.5 %collective-permute-done.4 = bf16[1024,1280]{0,1:T(8,128)(2,1)} collective-permute-done((bf16[1024,1280]{0,1:T(8,128)(2,1)}, bf16[1024,1280]{0,1:T(8,128)(2,1)}, u32[]{:S(2)}, u32[]{:S(2)}) %collective-permute-start.4) | collective-permute-done | bytes 2621472 | tf_op jit(solution)/shard_map/ppermute | solution.py:18
  1091.5 33.6 %collective-permute-done.5 = bf16[512,1280]{0,1:T(8,128)(2,1)S(1)} collective-permute-done((bf16[512,1280]{0,1:T(8,128)(2,1)S(1)}, bf16[512,1280]{0,1:T(8,128)(2,1)S(1)}, u32[]{:S(2)}, u32[]{:S(2)}) %collective-permute-start.5) | collective-permute-done | bytes 1310752 | tf_op jit(solution)/shard_map/ppermute | solution.py:18
  1128.2 11.4 convolution_convert_fusion.2
  1140.4 12.9 convolution_convert_fusion.1
  1165.3 156.9 %reduce-scatter.7.cloned.1.call-done = bf16[480,1280]{1,0:T(8,128)(2,1)} async-done(((bf16[3840,1280]{1,0:T(8,128)(2,1)}), bf16[480,1280]{1,0:T(8,128)(2,1)}) %reduce-scatter.7.cloned.1.call-update) | async-done | bytes 1228816 | tf_op jit(solution)/shard_map/reduce_scatter | solution.py:228
  1322.2 217.8 %reduce-scatter.11.cloned.1.call-done = bf16[640,1280]{1,0:T(8,128)(2,1)} async-done(((bf16[5120,1280]{1,0:T(8,128)(2,1)}), bf16[640,1280]{1,0:T(8,128)(2,1)}) %reduce-scatter.11.cloned.1.call-update) | async-done | bytes 1638416 | tf_op jit(solution)/shard_map/reduce_scatter | solution.py:234
  1540.0 11.0 fusion.83
  1555.1 41.3 %all-reduce = (f32[2,1280]{1,0:T(2,128)}, f32[2,1280]{1,0:T(2,128)}, f32[4,1280]{1,0:T(4,128)}, f32[5120]{0:T(1024)}, f32[3]{0:T(128)S(1)}) all-reduce(f32[2,1280]{1,0:T(2,128)S(1)} %pad_maximum_fusion.6, f32[2,1280]{1,0:T(2,128)S(1)} %pad_maximum_fusion.7, ...), channel_id=1, replica_groups=mesh['dp'=4,'fsdp'=8] {'dp','fsdp'}, use_global_device_ids=true, to_apply=%region_30.31 | all-reduce | flops 15363 | bytes 122904 | tf_op jit(solution)/shard_map/psum | solution.py:255
  1596.9 60.3 %all-reduce.4.cloned.1.call-done = (bf16[160,5120]{0,1:T(8,128)(2,1)}, bf16[480,1280]{1,0:T(8,128)(2,1)}, bf16[160,1280]{1,0:T(8,128)(2,1)}, bf16[640,1280]{1,0:T(8,128)(2,1)}) async-done(((bf16[160,5120]{0,1:T(8,128)(2,1)}, bf16[480,1280]{1,0:T(8,128)(2,1)}, bf16[160,1280]{1,0:T(8,128)(2,1)}, bf16[640,1280]{1,0:T(8,128)(2,1)}), (bf16[160,5120]{0,1:T(8,128)(2,1)}, bf16[480,1280]{1,0:T(8,128)(2,1)}, ...) | async-done | bytes 4915216 | tf_op jit(solution)/shard_map/psum | solution.py:245
  (381 shorter events, 336.2 us)
Async XLA Ops:
  7.2 145.8 %all-gather.5.cloned.1.call-start = ((), (), s32[]{:S(2)}) async-start(), calls=%async_computation.4 | async-start | bytes 11059200 | tf_op jit(solution)/shard_map/all_gather | solution.py:83
  7.9 534.7 %all-gather.7.cloned.1.call-start = ((), (), s32[]{:S(2)}) async-start(), calls=%async_computation.5 | async-start | bytes 3686400 | tf_op jit(solution)/shard_map/all_gather | solution.py:127
  8.7 543.1 %all-gather.9.cloned.1.call-start = ((), (), s32[]{:S(2)}) async-start(), calls=%async_computation.6 | async-start | bytes 14745600 | tf_op jit(solution)/shard_map/all_gather | solution.py:134
  9.4 669.7 %all-gather.11.cloned.1.call-start = ((), (), s32[]{:S(2)}) async-start(), calls=%async_computation.7 | async-start | bytes 14745600 | tf_op jit(solution)/shard_map/all_gather | solution.py:139
  10.9 150.2 %copy-start.52 = (f32[1280]{0:T(1024)}, f32[1280]{0:T(1024)S(1)}, u32[]{:S(2)}) copy-start(f32[1280]{0:T(1024)S(1)} %get-tuple-element.125) | copy-start | bytes 15364
  10.9 150.2 %copy-start.74 = (f32[1280]{0:T(1024)}, f32[1280]{0:T(1024)S(1)}, u32[]{:S(2)}) copy-start(f32[1280]{0:T(1024)S(1)} %get-tuple-element.59) | copy-start | bytes 15364
  12.5 148.6 %copy-start.54 = (f32[512]{0:T(512)}, f32[512]{0:T(512)S(1)}, u32[]{:S(2)}) copy-start(f32[512]{0:T(512)S(1)} %broadcast_multiply_fusion.1) | copy-start | bytes 6148
  164.3 40.7 %collective-permute-start.2 = (bf16[512,1280]{1,0:T(8,128)(2,1)S(1)}, bf16[512,1280]{1,0:T(8,128)(2,1)}, u32[]{:S(2)}, u32[]{:S(2)}) collective-permute-start(bf16[512,1280]{1,0:T(8,128)(2,1)S(1)} %slice.223), channel_id=1, source_target_pairs={{0,1},{1,0},{2,3},{3,2},{4,5},{5,4},{6,7},{7,6},{8,9},{9,8},{10,11... | collective-permute-start | bytes 3932168 | tf_op jit(solution)/shard_map/ppermute | solution.py:18
  207.9 116.6 %collective-permute-start.3 = (bf16[1024,1280]{1,0:T(8,128)(2,1)S(1)}, bf16[1024,1280]{1,0:T(8,128)(2,1)}, u32[]{:S(2)}, u32[]{:S(2)}) collective-permute-start(bf16[1024,1280]{1,0:T(8,128)(2,1)S(1)} %maximum_select_fusion.3), channel_id=1, source_target_pairs={{0,2},{1,3},{2,0},{3,1},{4,6},{5,7},{6,4},{7,5},{8,10},{9,11},{10,... | collective-permute-start | bytes 7864328 | tf_op jit(solution)/shard_map/ppermute | solution.py:18
  214.5 28.3 %collective-permute-start = (bf16[512,1280]{1,0:T(8,128)(2,1)}, bf16[512,1280]{1,0:T(8,128)(2,1)}, u32[]{:S(2)}, u32[]{:S(2)}) collective-permute-start(bf16[512,1280]{1,0:T(8,128)(2,1)} %get-tuple-element.93), channel_id=1, source_target_pairs={{0,1},{1,0},{2,3},{3,2},{4,5},{5,4},{6,7},{7,6},{8,9},{9,8},{10,11... | collective-permute-start | bytes 3932168 | tf_op jit(solution)/shard_map/ppermute | solution.py:18
  215.6 945.7 %reduce-scatter.13.cloned.1.call-start = ((), (), s32[]{:S(2)}) async-start(), calls=%async_computation.11 | async-start | bytes 14745600
  217.0 317.5 %copy-start.50 = (pred[2048]{0:T(1024)(128)(4,1)}, pred[2048]{0:T(1024)(128)(4,1)S(1)}, u32[]{:S(2)}) copy-start(pred[2048]{0:T(1024)(128)(4,1)S(1)} %iota_compare_fusion) | copy-start | bytes 6148
  225.0 237.8 %copy-start.30 = (bf16[512,320]{0,1:T(8,128)(2,1)}, bf16[512,320]{0,1:T(8,128)(2,1)S(1)}, u32[]{:S(2)}) copy-start(bf16[512,320]{0,1:T(8,128)(2,1)S(1)} %copy.73) | copy-start | bytes 983044
  246.8 197.5 %collective-permute-start.1 = (bf16[1024,1280]{1,0:T(8,128)(2,1)}, bf16[1024,1280]{1,0:T(8,128)(2,1)}, u32[]{:S(2)}, u32[]{:S(2)}) collective-permute-start(bf16[1024,1280]{1,0:T(8,128)(2,1)} %maximum_select_fusion.2), channel_id=1, source_target_pairs={{0,2},{1,3},{2,0},{3,1},{4,6},{5,7},{6,4},{7,5},{8,10},{9,11},{10,... | collective-permute-start | bytes 7864328 | tf_op jit(solution)/shard_map/ppermute | solution.py:18
  547.5 213.7 %copy-start.66 = (f32[512]{0:T(512)}, f32[512]{0:T(512)S(1)}, u32[]{:S(2)}) copy-start(f32[512]{0:T(512)S(1)} %broadcast_multiply_fusion) | copy-start | bytes 6148
  549.4 211.8 %copy-start.81 = (f32[512]{0:T(512)}, f32[512]{0:T(512)S(1)}, u32[]{:S(2)}) copy-start(f32[512]{0:T(512)S(1)} %fusion.59) | copy-start | bytes 6148
  761.1 404.2 %reduce-scatter.9.cloned.1.call-start = ((), (), s32[]{:S(2)}) async-start(), calls=%async_computation.9 | async-start | bytes 3686400 | tf_op jit(solution)/shard_map/reduce_scatter | solution.py:231
  829.7 160.7 %collective-permute-start.6 = (bf16[1024,1280]{0,1:T(8,128)(2,1)}, bf16[1024,1280]{0,1:T(8,128)(2,1)}, u32[]{:S(2)}, u32[]{:S(2)}) collective-permute-start(bf16[1024,1280]{0,1:T(8,128)(2,1)} %select_convert_fusion), channel_id=1, source_target_pairs={{0,2},{1,3},{2,0},{3,1},{4,6},{5,7},{6,4},{7,5},{8,10},{9,11},{10,... | collective-permute-start | bytes 7864328 | tf_op jit(solution)/shard_map/ppermute | solution.py:18
  970.1 100.4 %collective-permute-start.4 = (bf16[1024,1280]{0,1:T(8,128)(2,1)}, bf16[1024,1280]{0,1:T(8,128)(2,1)}, u32[]{:S(2)}, u32[]{:S(2)}) collective-permute-start(bf16[1024,1280]{0,1:T(8,128)(2,1)} %select_convert_fusion.1), channel_id=1, source_target_pairs={{0,2},{1,3},{2,0},{3,1},{4,6},{5,7},{6,4},{7,5},{8,10},{9,11},{10,... | collective-permute-start | bytes 7864328 | tf_op jit(solution)/shard_map/ppermute | solution.py:18
  974.9 347.2 %reduce-scatter.7.cloned.1.call-start = ((), (), s32[]{:S(2)}) async-start(), calls=%async_computation.8 | async-start | bytes 11059200 | tf_op jit(solution)/shard_map/reduce_scatter | solution.py:228
  995.6 93.7 %collective-permute-start.7 = (bf16[512,1280]{0,1:T(8,128)(2,1)}, bf16[512,1280]{0,1:T(8,128)(2,1)}, u32[]{:S(2)}, u32[]{:S(2)}) collective-permute-start(bf16[512,1280]{0,1:T(8,128)(2,1)} %select_convert_fusion.2), channel_id=1, source_target_pairs={{0,1},{1,0},{2,3},{3,2},{4,5},{5,4},{6,7},{7,6},{8,9},{9,8},{10,11... | collective-permute-start | bytes 3932168 | tf_op jit(solution)/shard_map/ppermute | solution.py:18
  1082.5 42.6 %collective-permute-start.5 = (bf16[512,1280]{0,1:T(8,128)(2,1)S(1)}, bf16[512,1280]{0,1:T(8,128)(2,1)S(1)}, u32[]{:S(2)}, u32[]{:S(2)}) collective-permute-start(bf16[512,1280]{0,1:T(8,128)(2,1)S(1)} %select_convert_fusion.3), channel_id=1, source_target_pairs={{0,1},{1,0},{2,3},{3,2},{4,5},{5,4},{6,7},{7,6},{8,9},{9,8},{10,11... | collective-permute-start | bytes 3932168 | tf_op jit(solution)/shard_map/ppermute | solution.py:18
  1139.7 400.3 %reduce-scatter.11.cloned.1.call-start = ((), (), s32[]{:S(2)}) async-start(), calls=%async_computation.10 | async-start | bytes 14745600 | tf_op jit(solution)/shard_map/reduce_scatter | solution.py:234
  1153.3 503.9 %all-reduce.4.cloned.1.call-start = ((), (), s32[]{:S(2)}) async-start(), calls=%async_computation.12 | async-start | bytes 11796480 | tf_op jit(solution)/shard_map/psum | solution.py:245
  (107 other events, 1807.3 us)
Sparse Core Ops, SparseCore 0:
  10.2 142.7 all-gather.4
  155.2 78.0 all-gather.6
  235.5 256.9 all-gather.8
  494.6 184.5 all-gather.10
  761.2 292.8 reduce-scatter.12
  1058.2 91.3 reduce-scatter.8
  1153.6 168.4 reduce-scatter.6
  1326.3 213.6 reduce-scatter.10
  1543.3 113.9 all-reduce.3
where the time goes:
time: 1680 us; the launch traced here: 1670 us
  waiting for transfers between devices  1010 us (60%)
  matrix products  342 us (20%)
  other arithmetic  163 us (10%)
  local copies, waits for them, and re-layouts  93.8 us (6%)
  blocking collectives  41.3 us (2%)
    ppermute x8, waiting for transfers between devices, partner(): return lax.ppermute(value, axis, pairs)  317 us
    reduce_scatter x1, waiting for transfers between devices, on_device(): lax.psum_scatter(grad_up.astype(jnp.bfloat16), 'fsdp', scatter_dimension=...  218 us
    reduce_scatter x1, waiting for transfers between devices, on_device(): lax.psum_scatter(grad_entry.astype(jnp.bfloat16), 'fsdp', scatter_dimensi...  157 us
    all_gather x1, waiting for transfers between devices, on_device(): lax.all_gather(in_proj, 'fsdp', axis=0, tiled=True)  139 us
    all_gather x1, waiting for transfers between devices, on_device(): lax.all_gather(down_proj, 'fsdp', axis=0, tiled=True)  112 us
    dot_general x4, matrix products, on_device(): jnp.einsum('qhd,khd->hqk', grad_group, value_group, preferred_element_typ...  63.5 us
    dot_general x4, matrix products, times_plain(): return jnp.dot(operand, weight, preferred_element_type=jnp.float32)  62.9 us
    psum x1, waiting for transfers between devices, on_device(): lax.psum(shard_grads[3].astype(jnp.bfloat16), 'dp').astype(jnp.float32)  60.3 us
  transfers between devices with their start and end apart: 17, of which 11 were waited for; matrix products, arithmetic and copies ran while one was open for 29% of the time, Pallas kernels for 0%

commit v1 on v0

v1 whole, which is shorter than its diff:
```python
import functools
import math

import jax
import jax.numpy as jnp
from jax import lax
from jax.experimental import pallas as pl
from jax.experimental.pallas import tpu as pltpu
from jax.sharding import PartitionSpec as P

H = 16
HD = 80
CLIP_DEV = 4
LANES = 128
GROUP_HEADS = H // CLIP_DEV
EPSILON = 1e-05
SCORE_SCALE = HD ** (-0.5) * math.log2(math.e)
LN2 = math.log(2.0)
LOW = jnp.bfloat16
QUERY_BLOCK = 256
GRAD_BLOCK = 256
VMEM_BYTES = 56 * 1024 * 1024


def swap(value, axis, mask):
    pairs = [(source, source ^ mask) for source in range(lax.axis_size(axis))]
    return lax.ppermute(value, axis, pairs)


def dot_nt(lhs, rhs):
    return lax.dot_general(
        lhs, rhs, (((1,), (1,)), ((), ())), preferred_element_type=jnp.float32
    )


def dot_nn(lhs, rhs):
    return jnp.dot(lhs, rhs, preferred_element_type=jnp.float32)


def dot_tn(lhs, rhs):
    return lax.dot_general(
        lhs, rhs, (((0,), (0,)), ((), ())), preferred_element_type=jnp.float32
    )


def split_three(value):
    high = value.astype(LOW).astype(jnp.float32)
    rest = value - high
    middle = rest.astype(LOW).astype(jnp.float32)
    return high, middle, rest - middle


def with_lanes(block, first, columns):
    lane = lax.broadcasted_iota(jnp.int32, block.shape, 1)
    for place, column in enumerate(columns):
        block = jnp.where(lane == first + place, column, block)
    return block


def attend_kernel(query_ref, key_ref, value_ref, context_ref, query_out_ref):
    queries = query_ref[...]
    scores = dot_nt(queries, key_ref[...])
    largest = jnp.max(scores, axis=1, keepdims=True)
    exponent = jnp.exp2(scores - largest)
    mixed = dot_nn(exponent.astype(LOW), value_ref[...])
    summed = mixed[:, HD : HD + 1]
    context_ref[...] = (mixed / summed).astype(LOW)
    log_parts = split_three(-(largest + jnp.log2(summed)))
    query_out_ref[...] = with_lanes(
        queries.astype(jnp.float32), HD + 1, log_parts
    ).astype(LOW)


def attend(projected):
    rows = projected.shape[0]
    block = min(QUERY_BLOCK, rows)
    out = jax.ShapeDtypeStruct((rows, GROUP_HEADS * LANES), LOW)
    whole = pl.BlockSpec((rows, LANES), lambda head, step: (0, GROUP_HEADS + head))
    return pl.pallas_call(
        attend_kernel,
        grid=(GROUP_HEADS, rows // block),
        in_specs=[
            pl.BlockSpec((block, LANES), lambda head, step: (step, head)),
            whole,
            pl.BlockSpec((rows, LANES), lambda head, step: (0, 2 * GROUP_HEADS + head)),
        ],
        out_specs=[pl.BlockSpec((block, LANES), lambda head, step: (step, head))] * 2,
        out_shape=[out, out],
        compiler_params=pltpu.CompilerParams(vmem_limit_bytes=VMEM_BYTES),
        cost_estimate=pl.CostEstimate(
            flops=8 * GROUP_HEADS * rows * rows * LANES,
            bytes_accessed=5 * rows * GROUP_HEADS * LANES * 2,
            transcendentals=GROUP_HEADS * rows * rows,
        ),
    )(projected, projected, projected)


def attend_back_kernel(
    query_ref,
    key_ref,
    value_ref,
    context_ref,
    grad_ref,
    grad_query_ref,
    grad_key_ref,
    grad_value_ref,
    key_turned,
    key_total,
    value_total,
):
    step = pl.program_id(1)

    @pl.when(step == 0)
    def _():
        key_turned[...] = key_ref[...].T
        key_total[...] = jnp.zeros_like(key_total)
        value_total[...] = jnp.zeros_like(value_total)

    queries = query_ref[...]
    grad = grad_ref[...]
    grad_float = grad.astype(jnp.float32)
    row_term = jnp.sum(grad_float * context_ref[...].astype(jnp.float32), axis=1, keepdims=True)
    grad = with_lanes(grad_float, HD, split_three(-row_term)).astype(LOW)
    soft = jnp.exp2(dot_nt(key_ref[...], queries))
    grad_soft = dot_nt(value_ref[...], grad)
    value_total[...] += dot_nn(soft.astype(LOW), grad)
    grad_scores = (soft * grad_soft).astype(LOW)
    key_total[...] += dot_nn(grad_scores, queries)
    grad_query = dot_nn(key_turned[...], grad_scores)
    grad_query_ref[...] = (grad_query * HD ** (-0.5)).T.astype(LOW)

    @pl.when(step == pl.num_programs(1) - 1)
    def _():
        grad_key_ref[...] = (key_total[...] * LN2).astype(LOW)
        grad_value_ref[...] = value_total[...].astype(LOW)


def attend_back(queries, projected, context, grad_context):
    rows = projected.shape[0]
    block = min(GRAD_BLOCK, rows)
    out = jax.ShapeDtypeStruct((rows, GROUP_HEADS * LANES), LOW)
    part = pl.BlockSpec((block, LANES), lambda head, step: (step, head))
    whole = pl.BlockSpec((rows, LANES), lambda head, step: (0, head))
    return pl.pallas_call(
        attend_back_kernel,
        grid=(GROUP_HEADS, rows // block),
        in_specs=[
            part,
            pl.BlockSpec((rows, LANES), lambda head, step: (0, GROUP_HEADS + head)),
            pl.BlockSpec((rows, LANES), lambda head, step: (0, 2 * GROUP_HEADS + head)),
            part,
            part,
        ],
        out_specs=[part, whole, whole],
        out_shape=[out] * 3,
        scratch_shapes=[
            pltpu.VMEM((LANES, rows), LOW),
            pltpu.VMEM((rows, LANES), jnp.float32),
            pltpu.VMEM((rows, LANES), jnp.float32),
        ],
        compiler_params=pltpu.CompilerParams(vmem_limit_bytes=VMEM_BYTES),
        cost_estimate=pl.CostEstimate(
            flops=20 * GROUP_HEADS * rows * rows * LANES,
            bytes_accessed=8 * rows * GROUP_HEADS * LANES * 2,
            transcendentals=GROUP_HEADS * rows * rows,
        ),
    )(queries, projected, projected, context, grad_context)


def normalise(values):
    center = values - jnp.mean(values, axis=-1, keepdims=True)
    spread = jnp.mean(center * center, axis=-1, keepdims=True)
    scale = lax.rsqrt(spread + EPSILON)
    return center * scale, scale


def norm_back(grad, gain, unit, scale):
    scaled = grad * gain
    return scale * (
        scaled
        - jnp.mean(scaled, axis=-1, keepdims=True)
        - unit * jnp.mean(scaled * unit, axis=-1, keepdims=True)
    )


def gelu_exact(values):
    return jax.nn.gelu(values, approximate=False)


def pick(blocks, index, axis=0):
    return lax.dynamic_index_in_dim(blocks, index, axis, keepdims=False)


def gather_bits(piece, bits):
    held = piece.reshape((1,) * len(bits) + piece.shape)
    for place in sorted(range(len(bits)), key=lambda i: bits[i][3]):
        axis, mask, mine, _ = bits[place]
        came = swap(held, axis, mask)
        held = jnp.where(
            mine == 1,
            jnp.concatenate([came, held], axis=place),
            jnp.concatenate([held, came], axis=place),
        )
    return held


def reduce_bits(held, bits):
    for place in sorted(range(len(bits)), key=lambda i: -bits[i][3]):
        axis, mask, mine, _ = bits[place]
        kept = lax.dynamic_slice_in_dim(held, mine, 1, place)
        sent = lax.dynamic_slice_in_dim(held, 1 - mine, 1, place)
        came = swap(sent, axis, mask)
        held = (kept.astype(jnp.float32) + came.astype(jnp.float32)).astype(LOW)
    return held.reshape(held.shape[len(bits) :])


def on_device(
    hidden_states,
    clip_lengths,
    norm_gains,
    norm_shifts,
    proj_biases,
    up_bias,
    in_proj,
    out_proj,
    up_proj,
    down_proj,
    cotangent,
):
    tokens_here, width = hidden_states.shape
    fsdp_count = lax.axis_size("fsdp")
    dp_count = lax.axis_size("dp")
    fsdp_index = lax.axis_index("fsdp")
    dp_index = lax.axis_index("dp")
    core = dp_index % 2
    copies = dp_count // 2
    copy_index = dp_index // 2
    region = (dp_index * fsdp_count + fsdp_index) // CLIP_DEV
    place = fsdp_index % CLIP_DEV
    length = lax.dynamic_index_in_dim(clip_lengths, region, keepdims=False)
    span = tokens_here * CLIP_DEV
    hidden_units = up_bias.shape[0]
    positions = jnp.arange(tokens_here, dtype=jnp.int32)
    row_valid = (place * tokens_here + positions < length).astype(jnp.float32)
    fsdp_levels = fsdp_count.bit_length() - 1
    copy_levels = copies.bit_length() - 1

    def bits_of(turn):
        bits = []
        for level in reversed(range(fsdp_levels)):
            when = fsdp_levels - level if level else (100 if turn else 300)
            bits.append(("fsdp", 1 << level, fsdp_index >> level & 1, when))
        for level in reversed(range(copy_levels)):
            bits.append(("dp", 2 << level, copy_index >> level & 1, 200 - level))
        return bits

    core_bit = ("dp", 1, core, 1000)

    with jax.named_scope("gather_tokens"):
        half = width // 2
        own_x = hidden_states
        near_a = swap(own_x[:, :half], "fsdp", 1)
        far_b = swap(own_x[:, half:], "fsdp", 2)
        far_a, both_a = swap((own_x[:, :half], near_a), "fsdp", 2)
        near_b, both_b = swap((own_x[:, half:], far_b), "fsdp", 1)
        clip_x = jnp.concatenate(
            [
                own_x,
                jnp.concatenate([near_a, near_b], axis=1),
                jnp.concatenate([far_a, far_b], axis=1),
                jnp.concatenate([both_a, both_b], axis=1),
            ]
        ).astype(jnp.float32)
    block_place = place ^ jnp.arange(CLIP_DEV, dtype=jnp.int32)
    clip_position = (block_place[:, None] * tokens_here + positions).reshape(span)
    key_mask = jnp.where(clip_position < length, 0.0, -1e30).astype(jnp.float32)

    with jax.named_scope("gather_in_proj"):
        rounds = fsdp_count // CLIP_DEV
        unit_rows = in_proj.shape[0] // 3
        half_rows = unit_rows // 2
        units = in_proj.reshape(3, 2, half_rows, width)
        own_units = pick(units, core, 1)

        def route(slot, turn):
            pairs = []
            for source in range(fsdp_count):
                unit = (3 * source + slot) % fsdp_count
                owner, spot = unit // rounds, unit % rounds
                pairs.append((source, owner + CLIP_DEV * ((spot + turn) % rounds)))
            return pairs

        came = jnp.stack(
            [
                jnp.stack([lax.ppermute(own_units[slot], "fsdp", route(slot, turn)) for turn in range(rounds)])
                for slot in range(3)
            ]
        )
        came = gather_bits(came, [core_bit])
        came = jnp.moveaxis(came, 0, 2).reshape(3, rounds, unit_rows, width)
        lap = fsdp_index // CLIP_DEV

        def slot_of(kind, spot):
            return (place * rounds + spot + kind * fsdp_count) % 3

        weight_rows = jnp.stack(
            [
                jnp.concatenate(
                    [
                        pick(pick(came, slot_of(kind, spot)), (lap - spot) % rounds)
                        for spot in range(rounds)
                    ]
                )
                for kind in range(3)
            ]
        )
        group_width = GROUP_HEADS * HD
        padded_width = 3 * GROUP_HEADS * LANES
        weight_in = jnp.pad(
            weight_rows.reshape(3 * GROUP_HEADS, HD, width), ((0, 0), (0, LANES - HD), (0, 0))
        ).reshape(padded_width, width)

    unit_one, scale_one = normalise(clip_x)
    normed_one = (unit_one * norm_gains[0] + norm_shifts[0]).astype(LOW)
    zeros = jnp.zeros((width,), jnp.float32)
    group_bias = jnp.stack([proj_biases[0], zeros, proj_biases[1]]).reshape(3, CLIP_DEV, GROUP_HEADS, HD)
    group_bias = jnp.pad(pick(group_bias, place, 1), ((0, 0), (0, 0), (0, LANES - HD)))
    lane = jnp.arange(LANES)
    kind_scale = jnp.array([SCORE_SCALE, 1.0, 1.0], jnp.float32)[:, None, None]
    spare = jnp.stack(
        [
            lane == HD,
            (lane > HD) & (lane <= HD + 3),
            (lane >= HD) & (lane < HD + 3),
        ]
    ).astype(jnp.float32)
    column_shift = (group_bias * kind_scale + spare[:, None]).reshape(padded_width)
    column_scale = jnp.broadcast_to(kind_scale, group_bias.shape).reshape(padded_width)
    mask_lane = jnp.broadcast_to(
        (jnp.arange(3)[:, None, None] == 1) & (lane == HD), group_bias.shape
    ).reshape(padded_width)
    projected = dot_nt(normed_one, weight_in) * column_scale + column_shift
    projected = jnp.where(mask_lane, key_mask[:, None], projected).astype(LOW)
    context_heads, queries_ready = attend(projected)

    def to_heads(blocks):
        return blocks

    with jax.named_scope("context_back"):
        compact = context_heads.reshape(CLIP_DEV, tokens_here, GROUP_HEADS, LANES)[..., :HD]
        compact = compact.reshape(CLIP_DEV, tokens_here, group_width)
        parts = [compact[0]] + [swap(compact[j], "fsdp", j) for j in range(1, CLIP_DEV)]
        parts = jnp.stack(parts)
        context_low = jnp.concatenate(
            [pick(parts, place ^ group) for group in range(CLIP_DEV)], axis=1
        )

    with jax.named_scope("gather_weights"):
        out_rows = out_proj.shape[0] // dp_count
        out_piece = pick(out_proj.reshape(copies, 2, out_rows, width), copy_index)
        out_piece = pick(out_piece, core)
        out_full = gather_bits(out_piece, bits_of(True) + [core_bit]).reshape(width, width)
        shard_units = up_proj.shape[0]
        half_units = shard_units // 2
        up_rows = half_units // copies
        up_piece = pick(up_proj.reshape(2, copies, up_rows, width), core)
        up_piece = pick(up_piece, copy_index)
        up_half = gather_bits(up_piece, bits_of(True)).reshape(hidden_units // 2, width)
        down_rows = down_proj.shape[0] // copies
        down_piece = pick(down_proj.reshape(copies, down_rows, fsdp_count, 2, half_units), copy_index)
        down_piece = pick(down_piece, core, 2).reshape(down_rows, hidden_units // 2)
        down_half = gather_bits(down_piece, bits_of(False)).reshape(width, hidden_units // 2)

    inputs = hidden_states.astype(jnp.float32)
    attention = dot_nt(context_low, out_full) + proj_biases[2]
    middle = inputs + attention
    unit_two, scale_two = normalise(middle)
    normed_two = (unit_two * norm_gains[1] + norm_shifts[1]).astype(LOW)
    normed_pair = jnp.concatenate([normed_two, swap(normed_two, "dp", 1)])
    grad_pair = jnp.concatenate([cotangent, swap(cotangent, "dp", 1)])
    half_bias = pick(up_bias.reshape(fsdp_count, 2, half_units), core, 1).reshape(hidden_units // 2)
    widened = dot_nt(normed_pair, up_half) + half_bias
    activated, gelu_back = jax.vjp(gelu_exact, widened)
    activated_low = activated.astype(LOW)
    grad_activated = dot_nn(grad_pair, down_half)
    grad_widened = gelu_back(grad_activated)[0].astype(LOW)

    def over_cores(partial):
        return partial[:tokens_here] + swap(partial[tokens_here:].astype(LOW), "dp", 1).astype(jnp.float32)

    feedforward = over_cores(dot_nt(activated_low, down_half)) + proj_biases[3]
    outputs = (middle + feedforward).astype(LOW)
    stat_terms = jnp.stack(
        [
            jnp.sum(row_valid * jnp.sum(middle * middle, axis=1)),
            jnp.sum(row_valid * jnp.sum(attention * attention, axis=1)),
            jnp.sum(row_valid * jnp.sum(feedforward * feedforward, axis=1)),
        ]
    )
    grad_normed_two = over_cores(dot_nn(grad_widened, up_half))
    grad_out = cotangent.astype(jnp.float32)
    grad_middle = grad_out + norm_back(grad_normed_two, norm_gains[1], unit_two, scale_two)
    grad_attention = grad_middle.astype(LOW)
    grad_context = dot_nn(grad_attention, out_full).astype(LOW)

    with jax.named_scope("grad_context_to_heads"):
        groups = jnp.moveaxis(grad_context.reshape(tokens_here, CLIP_DEV, group_width), 1, 0)
        sends = [pick(groups, place ^ j) for j in range(CLIP_DEV)]
        grad_heads = jnp.stack([sends[0]] + [swap(sends[j], "fsdp", j) for j in range(1, CLIP_DEV)])
        grad_heads = jnp.pad(
            grad_heads.reshape(span, GROUP_HEADS, HD), ((0, 0), (0, 0), (0, LANES - HD))
        ).reshape(span, GROUP_HEADS * LANES)

    grad_down = dot_tn(grad_pair, activated_low).astype(LOW)
    grad_up = dot_tn(grad_widened, normed_pair).astype(LOW)
    grad_exit = dot_tn(grad_attention, context_low).astype(LOW)

    def shape_of(bits):
        return (2,) * len(bits)

    with jax.named_scope("reduce_weights"):
        bits = bits_of(False)
        down_sum = reduce_bits(grad_down.reshape(shape_of(bits) + (down_rows, hidden_units // 2)), bits)
        bits = bits_of(True)
        up_sum = reduce_bits(grad_up.reshape(shape_of(bits) + (up_rows, width)), bits)
        bits = bits_of(True) + [core_bit]
        exit_sum = reduce_bits(grad_exit.reshape(shape_of(bits) + (out_rows, width)), bits)
        copy_bits = [bit for bit in bits_of(False) if bit[0] == "dp"]
        down_sum = gather_bits(down_sum, copy_bits + [core_bit])
        down_sum = down_sum.reshape(copies, 2, down_rows, fsdp_count, half_units)
        down_sum = jnp.moveaxis(down_sum, 1, 3).reshape(down_proj.shape).astype(jnp.float32)
        up_sum = gather_bits(up_sum, [core_bit] + copy_bits).reshape(up_proj.shape).astype(jnp.float32)
        exit_sum = gather_bits(exit_sum, copy_bits + [core_bit]).reshape(out_proj.shape).astype(jnp.float32)

    grad_query, grad_key, grad_value = attend_back(queries_ready, projected, context_heads, grad_heads)
    grad_projected = jnp.concatenate([grad_query, grad_key, grad_value], axis=1)
    partial_one = dot_nn(grad_projected, weight_in)
    gain_one = jnp.sum(partial_one * unit_one, axis=0)
    shift_one = jnp.sum(partial_one, axis=0)
    grad_entry = dot_tn(grad_projected, normed_one)
    grad_entry = grad_entry.reshape(3, GROUP_HEADS, LANES, width)[:, :, :HD].astype(LOW)

    with jax.named_scope("reduce_tokens"):
        blocks = partial_one.reshape(CLIP_DEV, tokens_here, width)
        first, second = blocks[:, :, :half], blocks[:, :, half:]
        came = swap(first[1::2].astype(LOW), "fsdp", 1)
        first = first[0::2] + came.astype(jnp.float32)
        first = first[0] + swap(first[1].astype(LOW), "fsdp", 2).astype(jnp.float32)
        came = swap(second[2:].astype(LOW), "fsdp", 2)
        second = second[:2] + came.astype(jnp.float32)
        second = second[0] + swap(second[1].astype(LOW), "fsdp", 1).astype(jnp.float32)
        grad_normed_one = jnp.concatenate([first, second], axis=1)

    with jax.named_scope("reduce_in_proj"):
        entry_bits = [core_bit] + copy_bits
        entry = grad_entry.reshape(3, rounds, 2, copies, half_rows // copies, width)
        entry = jnp.moveaxis(entry, (2, 3), (0, 1))
        entry = entry.reshape((2,) * len(entry_bits) + (3, rounds, half_rows // copies, width))
        entry = reduce_bits(entry, entry_bits)
        totals = []
        for slot in range(3):
            total = 0.0
            for turn in range(rounds):
                spot = (lap - turn) % rounds
                kind = ((slot - place * rounds - spot) * pow(fsdp_count, -1, 3)) % 3
                sent = pick(pick(entry, kind), spot)
                back = [(target, source) for source, target in route(slot, turn)]
                total = total + lax.ppermute(sent, "fsdp", back).astype(jnp.float32)
            totals.append(total.astype(LOW))
        entry_sum = gather_bits(jnp.stack(totals), entry_bits)
        entry_sum = entry_sum.reshape(2, copies, 3, half_rows // copies, width)
        entry_sum = jnp.moveaxis(entry_sum, 2, 0).reshape(in_proj.shape).astype(jnp.float32)

    grad_hidden = grad_middle + norm_back(grad_normed_one, norm_gains[0], unit_one[:tokens_here], scale_one[:tokens_here])

    def place_heads(grads):
        columns = jnp.sum(grads.astype(jnp.float32), axis=0).reshape(GROUP_HEADS, LANES)[:, :HD]
        rows = jnp.zeros((CLIP_DEV, group_width), jnp.float32)
        return lax.dynamic_update_index_in_dim(rows, columns.reshape(group_width), place, 0).reshape(width)

    bias_terms = jnp.stack(
        [
            place_heads(grad_query),
            place_heads(grad_value),
            jnp.sum(grad_attention.astype(jnp.float32), axis=0),
            jnp.sum(grad_out, axis=0),
        ]
    )
    half_up = jnp.sum(grad_widened.astype(jnp.float32), axis=0).reshape(fsdp_count, half_units)
    up_terms = jnp.zeros((fsdp_count, 2, half_units), jnp.float32)
    up_terms = lax.dynamic_update_index_in_dim(up_terms, half_up, core, 1).reshape(hidden_units)
    small_totals = lax.psum(
        (
            jnp.stack([gain_one, jnp.sum(grad_normed_two * unit_two, axis=0)]),
            jnp.stack([shift_one, jnp.sum(grad_normed_two, axis=0)]),
            bias_terms,
            up_terms,
            stat_terms,
        ),
        ("dp", "fsdp"),
    )
    valid_count = jnp.sum(clip_lengths).astype(jnp.float32) * width
    root_means = jnp.sqrt(small_totals[4] / valid_count)
    return (
        outputs,
        grad_hidden.astype(LOW),
        entry_sum,
        exit_sum,
        up_sum,
        down_sum,
        small_totals[0],
        small_totals[1],
        small_totals[2],
        small_totals[3],
        root_means,
    )


def solution(mesh):
    in_specs = (
        P(("dp", "fsdp"), None),
        P(),
        P(),
        P(),
        P(),
        P(),
        P("fsdp", None),
        P("fsdp", None),
        P("fsdp", None),
        P("fsdp", None),
        P(("dp", "fsdp"), None),
    )
    out_specs = (
        P(("dp", "fsdp"), None),
        P(("dp", "fsdp"), None),
        P("fsdp", None),
        P("fsdp", None),
        P("fsdp", None),
        P("fsdp", None),
        P(),
        P(),
        P(),
        P(),
        P(),
    )
    return jax.shard_map(
        on_device, mesh=mesh, in_specs=in_specs, out_specs=out_specs, check_vma=False
    )
```

time: 1680 us -> 931 us (0.55)
  waiting for transfers between devices: 1010 us -> 329 us
  matrix products: 342 us -> 127 us
  starting transfers between devices: 10.1 us -> 110 us
  Pallas kernels: 0 us -> 88.3 us
  other arithmetic: 163 us -> 119 us
    reduce_scatter x3 -> x0, waiting for transfers between devices: 375 us -> none  [the longest x1 218 us: on_device(): lax.psum_scatter(grad_up.astype(jnp.bfloat16), 'fsdp', scatter_dimension=...]
    all_gather x4 -> x0, waiting for transfers between devices: 252 us -> none  [the longest x1 139 us: on_device(): lax.all_gather(in_proj, 'fsdp', axis=0, tiled=True)]
    dot_general x36 -> x12, matrix products: 342 us -> 127 us  [the longest x4 61.7 us: dot_nn(): return jnp.dot(lhs, rhs, preferred_element_type=jnp.float32)]
    ppermute x8 -> x69, starting transfers between devices: 9.33 us -> 110 us  [the longest x57 79.6 us: swap(): return lax.ppermute(value, axis, pairs)]
    pallas_call x0 -> x2, Pallas kernels: none -> 88.3 us  [the longest x1 53.3 us: attend_back(): pl.pallas_call(attend_back_kernel, grid=(GROUP_HEADS, rows // block), in_...]
    psum x1 -> x0, waiting for transfers between devices: 60.3 us -> none  [on_device(): lax.psum(shard_grads[3].astype(jnp.bfloat16), 'dp').astype(jnp.float32)]
    convert_element_type x10 -> x21, other arithmetic: 76.5 us -> 37.1 us  [the longest x13 12.8 us: reduce_bits(): held = (kept.astype(jnp.float32) + came.astype(jnp.float32)).astype(LOW)]
    unnamed x235 -> x181, local copies, waits for them, and re-layouts: 52.2 us -> 22.1 us
  transfers between devices with their start and end apart: 17 -> 69, of which waited for: 11 -> 23; matrix products, arithmetic and copies ran while one was open for 29% -> 27% of each run, Pallas kernels for 0% -> 10%
where the time goes in v1:
time: 931 us; the launch traced here: 920 us
  waiting for transfers between devices  329 us (35%)
  matrix products  127 us (14%)
  other arithmetic  119 us (13%)
  starting transfers between devices  110 us (12%)
  local copies, waits for them, and re-layouts  101 us (11%)
  Pallas kernels  88.3 us (9%)
  blocking collectives  42.7 us (5%)
    ppermute x57, waiting for transfers between devices, swap(): return lax.ppermute(value, axis, pairs)  320 us
    ppermute x57, starting transfers between devices, swap(): return lax.ppermute(value, axis, pairs)  79.6 us
    dot_general x4, matrix products, dot_nn(): return jnp.dot(lhs, rhs, preferred_element_type=jnp.float32)  61.7 us
    pallas_call x1, Pallas kernels, attend_back(): pl.pallas_call(attend_back_kernel, grid=(GROUP_HEADS, rows // block), in_...  53.3 us
    psum x1, blocking collectives, on_device(): lax.psum((jnp.stack([gain_one, jnp.sum(grad_normed_two * unit_two, axis=0...  42.7 us
    pallas_call x1, Pallas kernels, attend(): pl.pallas_call(attend_kernel, grid=(GROUP_HEADS, rows // block), in_specs...  35 us
    dot_general x4, matrix products, dot_nt(): lax.dot_general(lhs, rhs, (((1,), (1,)), ((), ())), preferred_element_typ...  33.5 us
    dot_general x4, matrix products, dot_tn(): lax.dot_general(lhs, rhs, (((0,), (0,)), ((), ())), preferred_element_typ...  31.4 us
  transfers between devices with their start and end apart: 69, of which 23 were waited for; matrix products, arithmetic and copies ran while one was open for 27% of the time, Pallas kernels for 10%

profile of v1, /device:TPU:3, one launch (start us, length us, event | category | flops | bytes accessed | tf_op | source)
XLA Modules:
  0.0 920.3 jit_solution(13576629045663528531)
XLA Ops:
  55.2 28.2 %collective-permute-done.17 = bf16[2,1,1,1,1,40,1280]{6,5,0,1,2,4,3:T(8,128)(2,1)S(1)} collective-permute-done((bf16[2,1,1,1,1,40,1280]{6,5,0,1,2,4,3:T(8,128)(2,1)S(1)}, bf16[2,1,1,1,1,40,1280]{6,5,0,1,2,4,3:T(8,128)(2,1)S(1)}, u32[]{:S(2)}, u32[]{:S(2)}) %collective-permute-start.17) | collective-permute-done | bytes 204832 | tf_op jit(solution)/shard_map/gather_weights/ppermute | solution.py:27
  93.6 9.7 %collective-permute-done.23 = bf16[2,1,1,1,160,1280]{5,4,0,3,2,1:T(8,128)(2,1)S(1)} collective-permute-done((bf16[2,1,1,1,160,1280]{5,4,0,3,2,1:T(8,128)(2,1)S(1)}, bf16[2,1,1,1,160,1280]{5,4,0,3,2,1:T(8,128)(2,1)S(1)}, u32[]{:S(2)}, u32[]{:S(2)}) %collective-permute-start.23) | collective-permute-done | bytes 819232 | tf_op jit(solution)/shard_map/gather_weights/ppermute | solution.py:27
  111.2 23.7 %collective-permute-done.3 = bf16[512,640]{1,0:T(8,128)(2,1)S(1)} collective-permute-done((bf16[512,640]{1,0:T(8,128)(2,1)S(1)}, bf16[512,640]{1,0:T(8,128)(2,1)S(1)}, u32[]{:S(2)}, u32[]{:S(2)}) %collective-permute-start.3) | collective-permute-done | bytes 655392 | tf_op jit(solution)/shard_map/gather_tokens/ppermute | solution.py:27
  147.7 9.3 %collective-permute-done.5 = bf16[512,640]{1,0:T(8,128)(2,1)S(1)} collective-permute-done((bf16[512,640]{1,0:T(8,128)(2,1)S(1)}, bf16[512,640]{1,0:T(8,128)(2,1)S(1)}, u32[]{:S(2)}, u32[]{:S(2)}) %collective-permute-start.5) | collective-permute-done | bytes 655392 | tf_op jit(solution)/shard_map/gather_tokens/ppermute | solution.py:27
  159.4 14.9 %convert_reduce_fusion = (f32[2048]{0:T(1024)S(1)}, bf16[2048,1280]{1,0:T(8,128)(2,1)S(1)}) fusion(bf16[512,640]{1,0:T(8,128)(2,1)S(1)} %collective-permute-done.5, bf16[512,640]{1,0:T(8,128)(2,1)S(1)} %collective-permute-done.4, bf16[512,640]{1,0:T(8,128)(2,1)S(1)} %collective-permute-done.3, bf16[512,640]{1,0:T(8,128)(2,1)S(1)} %collective-permute-done.2, ...), kind=kLoop, calls=%fused_computation.2 | loop fusion | flops 41940992 | bytes 10493952 | tf_op jit(solution)/shard_map/reduce_sum | solution.py:171
  180.8 11.0 %select_convert_fusion.query_ref.key_ref.value_ref = bf16[2048,1536]{1,0:T(8,128)(2,1)} fusion(bf16[1536,1280]{1,0:T(8,128)(2,1)S(1)} %bitcast.270, f32[1536]{0:T(1024)S(1)} %copy-done.62, f32[1536]{0:T(1024)S(1)} %copy-done.63, bf16[2048]{0:T(1024)(128)(2,1)S(1)} %bitcast.302, pred[1536]{0:T(1024)(128)(4,1)S(1)} %reshape.2301, f32[1280]{0:T(1024)S(1)} %copy-done.64, ...), kind=kOutput, calls=%fused_computation.3 | convolution fusion | flops 8078229504 | bytes 15511040 | tf_op jit(solution)/shard_map/dot_general | solution.py:31
  194.6 35.0 %shard_map.203 = (bf16[2048,512]{1,0:T(8,128)(2,1)}, bf16[2048,512]{1,0:T(8,128)(2,1)}) custom-call(bf16[2048,1536]{1,0:T(8,128)(2,1)} %select_convert_fusion.query_ref.key_ref.value_ref, bf16[2048,1536]{1,0:T(8,128)(2,1)} %select_convert_fusion.query_ref.key_ref.value_ref, bf16[2048,1536]{1,0:T(8,128)(2,1)} %select_convert_fusion.query_ref.key_ref.value_ref), custom_call_target="tpu_custom_call" | custom-call | flops 17179869184 | bytes 10485760 | tf_op jit(solution)/shard_map/pallas_call | solution.py:79
  268.5 55.8 %collective-permute-done.29 = bf16[2,2,1,2,80,2560]{5,4,0,1,3,2:T(8,128)(2,1)S(1)} collective-permute-done((bf16[2,2,1,2,80,2560]{5,4,0,1,3,2:T(8,128)(2,1)S(1)}, bf16[2,2,1,2,80,2560]{5,4,0,1,3,2:T(8,128)(2,1)S(1)}, u32[]{:S(2)}, u32[]{:S(2)}) %collective-permute-start.29) | collective-permute-done | bytes 3276832 | tf_op jit(solution)/shard_map/gather_weights/ppermute | solution.py:27
  334.5 9.3 %fusion.11 = f32[1024,2560]{1,0:T(8,128)S(1)} fusion(bf16[2560,1280]{1,0:T(8,128)(2,1)S(1)} %bitcast.263, bf16[512,1280]{1,0:T(8,128)(2,1)} %collective-permute-done.21, bf16[512,1280]{1,0:T(8,128)(2,1)S(1)} %add_convert_fusion.9), kind=kOutput, calls=%fused_computation.78 | convolution fusion | flops 6716129280 | bytes 19660800 | tf_op jit(solution)/shard_map/dot_general | solution.py:31
  343.8 34.1 %convert_reduce_fusion.1 = (f32[2560]{0:T(1024)S(1)}, bf16[1024,2560]{1,0:T(8,128)(2,1)}, f32[1024,2560]{1,0:T(8,128)S(1)}) fusion(f32[1024,2560]{1,0:T(8,128)S(1)} %fusion.11, f32[2560]{0:T(1024)S(1)} %add.588, bf16[1024,1280]{1,0:T(8,128)(2,1)} %copy-done.34, bf16[1280,2560]{1,0:T(8,128)(2,1)} %bitcast.267), kind=kOutput, calls=%fused_computation.10 | convolution fusion | flops 6907491840 | bytes 35409920 | tf_op jit(solution)/shard_map/dot_general | solution.py:37
  382.0 11.0 %fusion.51 = f32[1024,1280]{1,0:T(8,128)S(1)} fusion(bf16[1024,2560]{1,0:T(8,128)(2,1)} %multiply_convert_fusion, bf16[1280,2560]{1,0:T(8,128)(2,1)} %bitcast.268), kind=kOutput, calls=%fused_computation.251 | convolution fusion | flops 6710886400 | bytes 17039360 | tf_op jit(solution)/shard_map/dot_general | solution.py:31
  403.0 11.0 %fusion.52 = f32[1024,1280]{1,0:T(8,128)} fusion(bf16[1024,2560]{1,0:T(8,128)(2,1)} %get-tuple-element.42, bf16[2560,1280]{1,0:T(8,128)(2,1)S(1)} %bitcast.266), kind=kOutput, calls=%fused_computation.252 | convolution fusion | flops 6710886400 | bytes 17039360 | tf_op jit(solution)/shard_map/dot_general | solution.py:37
  418.5 8.7 convolution_convert_fusion.1
  466.0 53.5 %collective-permute-done.33 = bf16[512,320]{0,1:T(8,128)(2,1)S(1)} collective-permute-done((bf16[512,320]{0,1:T(8,128)(2,1)S(1)}, bf16[512,320]{0,1:T(8,128)(2,1)S(1)}, u32[]{:S(2)}, u32[]{:S(2)}) %collective-permute-start.33) | collective-permute-done | bytes 327712 | tf_op jit(solution)/shard_map/grad_context_to_heads/ppermute | solution.py:27
  526.7 53.3 %shard_map.204 = (bf16[2048,512]{1,0:T(8,128)(2,1)}, bf16[2048,512]{1,0:T(8,128)(2,1)}, bf16[2048,512]{1,0:T(8,128)(2,1)}) custom-call(bf16[2048,512]{1,0:T(8,128)(2,1)} %get-tuple-element.17.query_ref, bf16[2048,1536]{1,0:T(8,128)(2,1)} %select_convert_fusion.query_ref.key_ref.value_ref, bf16[2048,1536]{1,0:T(8,128)(2,1)} %select_convert_fusion.query_ref.key_ref.value_ref, ...), custom_call_target="tpu_custom_call" | custom-call | flops 42949672960 | bytes 16777216 | tf_op jit(solution)/shard_map/pallas_call | solution.py:144
  587.5 14.7 %fusion.46 = (f32[1280]{0:T(1024)S(1)}, f32[1280]{0:T(1024)S(1)}, f32[2048,1280]{1,0:T(8,128)}, f32[2048,1280]{1,0:T(8,128)}) fusion(f32[2048]{0:T(1024)S(1)} %copy-done.59, f32[2048]{0:T(1024)S(1)} %copy-done.52, bf16[2048,1280]{1,0:T(8,128)(2,1)S(1)} %bitcast.243, bf16[2048,1536]{1,0:T(8,128)(2,1)} %constant_dynamic-update-slice_fusion.2, ...), kind=kOutput, calls=%fused_computation.247 | convolution fusion | flops 8068790272 | bytes 36464640 | tf_op jit(solution)/shard_map/dot_general | solution.py:37
  602.2 11.8 %convolution_convert_fusion.3 = bf16[1536,1280]{1,0:T(8,128)(2,1)S(1)} fusion(bf16[2048,1536]{1,0:T(8,128)(2,1)} %constant_dynamic-update-slice_fusion.2, f32[1280]{0:T(1024)S(1)} %copy-done.65, f32[1280]{0:T(1024)S(1)} %copy-done.48, bf16[2048,1280]{1,0:T(8,128)(2,1)S(1)} %bitcast.243, f32[2048]{0:T(1024)S(1)} %copy-done.59, f32[2048]{0:T(1024)S(1)} %copy-done.52), kind=kOutput, calls=%fused_computation.29 | convolution fusion | flops 8070758400 | bytes 15493120 | tf_op jit(solution)/shard_map/dot_general | solution.py:41
  631.3 42.7 %all-reduce.3 = (f32[2,1280]{1,0:T(2,128)}, f32[2,1280]{1,0:T(2,128)}, f32[4,1280]{1,0:T(4,128)}, f32[5120]{0:T(1024)}, f32[3]{0:T(128)S(1)}) all-reduce(f32[2,1280]{1,0:T(2,128)S(1)} %pad_maximum_fusion.11, f32[2,1280]{1,0:T(2,128)S(1)} %pad_maximum_fusion.12, ...), channel_id=1, replica_groups=mesh['dp'=4,'fsdp'=8] {'dp','fsdp'}, use_global_device_ids=true, to_apply=%region_10.11 | all-reduce | flops 15363 | bytes 122904 | tf_op jit(solution)/shard_map/psum | solution.py:492
  681.5 22.1 %collective-permute-done.36 = bf16[2,512,640]{2,1,0:T(8,128)(2,1)S(1)} collective-permute-done((bf16[2,512,640]{2,1,0:T(8,128)(2,1)}, bf16[2,512,640]{2,1,0:T(8,128)(2,1)S(1)}, u32[]{:S(2)}, u32[]{:S(2)}) %collective-permute-start.36) | collective-permute-done | bytes 1310752 | tf_op jit(solution)/shard_map/reduce_tokens/ppermute | solution.py:27
  745.4 31.5 %collective-permute-done.52 = bf16[2,2,1,1,1,40,1280]{6,5,4,3,2,1,0:T(8,128)(2,1)S(1)} collective-permute-done((bf16[2,2,1,1,1,40,1280]{6,5,4,3,2,1,0:T(8,128)(2,1)S(1)}, bf16[2,2,1,1,1,40,1280]{6,5,4,3,2,1,0:T(8,128)(2,1)S(1)}, u32[]{:S(2)}, u32[]{:S(2)}) %collective-permute-start.52) | collective-permute-done | bytes 409632 | tf_op jit(solution)/shard_map/reduce_weights/ppermute | solution.py:27
  805.5 18.0 %collective-permute-done.59 = bf16[2,1,1,1,160,1280]{5,4,3,2,1,0:T(8,128)(2,1)S(1)} collective-permute-done((bf16[2,1,1,1,160,1280]{5,4,3,2,1,0:T(8,128)(2,1)S(1)}, bf16[2,1,1,1,160,1280]{5,4,3,2,1,0:T(8,128)(2,1)S(1)}, u32[]{:S(2)}, u32[]{:S(2)}) %collective-permute-start.59) | collective-permute-done | bytes 819232 | tf_op jit(solution)/shard_map/reduce_weights/ppermute | solution.py:27
  825.1 24.7 %collective-permute-done.65 = bf16[2,1,1,1,80,2560]{5,4,3,2,1,0:T(8,128)(2,1)S(1)} collective-permute-done((bf16[2,1,1,1,80,2560]{5,4,3,2,1,0:T(8,128)(2,1)S(1)}, bf16[2,1,1,1,80,2560]{5,4,3,2,1,0:T(8,128)(2,1)S(1)}, u32[]{:S(2)}, u32[]{:S(2)}) %collective-permute-start.65) | collective-permute-done | bytes 819232 | tf_op jit(solution)/shard_map/reduce_weights/ppermute | solution.py:27
  851.1 20.0 %collective-permute-done.66 = bf16[1,1,1,1,80,2560]{5,4,3,2,1,0:T(8,128)(2,1)S(1)} collective-permute-done((bf16[1,1,1,1,80,2560]{5,4,3,2,1,0:T(8,128)(2,1)S(1)}, bf16[1,1,1,1,80,2560]{5,4,3,2,1,0:T(8,128)(2,1)S(1)}, u32[]{:S(2)}, u32[]{:S(2)}) %collective-permute-start.66) | collective-permute-done | bytes 409632 | tf_op jit(solution)/shard_map/reduce_weights/ppermute | solution.py:27
  902.1 11.7 %convert_bitcast_fusion = f32[2,80,8,2,320]{4,3,2,1,0:T(2,128)} fusion(pred[]{:T(512)S(6)} %eq.88, bf16[2,1,80,8,320]{4,1,3,2,0:T(2,128)(2,1)} %broadcast_select_fusion, bf16[2,1,80,8,320]{4,1,3,2,0:T(2,128)(2,1)} %concatenate.888), kind=kLoop, calls=%fused_computation.37 | loop fusion | flops 8192000 | bytes 4915201 | tf_op jit(solution)/shard_map/reduce_weights/convert_element_type | solution.py:431
  (508 shorter events, 351.3 us)
Async XLA Ops:
  6.0 38.6 %collective-permute-start.10 = (bf16[80,1280]{1,0:T(8,128)(2,1)}, bf16[80,1280]{1,0:T(8,128)(2,1)}, u32[]{:S(2)}, u32[]{:S(2)}) collective-permute-start(bf16[80,1280]{1,0:T(8,128)(2,1)} %get-tuple-element.79), channel_id=1, source_target_pairs={{0,1},{1,6},{2,0},{3,5},{4,3},{5,4},{6,2},{7,7},{8,9},{9,14},{10,8... | collective-permute-start | bytes 614408 | tf_op jit(solution)/shard_map/gather_in_proj/ppermute | solution.py:295
  44.5 93.3 %collective-permute-start = (bf16[512,640]{1,0:T(8,128)(2,1)}, bf16[512,640]{1,0:T(8,128)(2,1)S(1)}, u32[]{:S(2)}, u32[]{:S(2)}) collective-permute-start(bf16[512,640]{1,0:T(8,128)(2,1)} %get-tuple-element.75), channel_id=1, source_target_pairs={{0,1},{1,0},{2,3},{3,2},{4,5},{5,4},{6,7},{7,6},{8,9},{9,8},{10,11... | collective-permute-start | bytes 1966088 | tf_op jit(solution)/shard_map/gather_tokens/ppermute | solution.py:27
  46.2 99.9 %collective-permute-start.2 = (bf16[512,640]{1,0:T(8,128)(2,1)}, bf16[512,640]{1,0:T(8,128)(2,1)S(1)}, u32[]{:S(2)}, u32[]{:S(2)}) collective-permute-start(bf16[512,640]{1,0:T(8,128)(2,1)} %get-tuple-element.75), channel_id=1, source_target_pairs={{0,2},{1,3},{2,0},{3,1},{4,6},{5,7},{6,4},{7,5},{8,10},{9,11},{10,... | collective-permute-start | bytes 1966088 | tf_op jit(solution)/shard_map/gather_tokens/ppermute | solution.py:27
  86.2 55.7 %collective-permute-start.27 = (bf16[2,1,1,1,80,2560]{5,4,3,2,1,0:T(8,128)(2,1)S(1)}, bf16[2,1,1,1,80,2560]{5,4,3,2,1,0:T(8,128)(2,1)S(1)}, u32[]{:S(2)}, u32[]{:S(2)}) collective-permute-start(bf16[2,1,1,1,80,2560]{5,4,3,2,1,0:T(8,128)(2,1)S(1)} %maximum_select_fusion.16), channel_id=1, source_target_pairs={{0,2},{1,3},{2,0},{3,1},{4,6},{5,7},{6,4},{7,5},{8,10},{9,11},{10,... | collective-permute-start | bytes 2457608 | tf_op jit(solution)/shard_map/gather_weights/ppermute | solution.py:27
  91.2 43.6 %collective-permute-start.3 = (bf16[512,640]{1,0:T(8,128)(2,1)S(1)}, bf16[512,640]{1,0:T(8,128)(2,1)S(1)}, u32[]{:S(2)}, u32[]{:S(2)}) collective-permute-start(bf16[512,640]{1,0:T(8,128)(2,1)S(1)} %copy-done.32), channel_id=1, source_target_pairs={{0,2},{1,3},{2,0},{3,1},{4,6},{5,7},{6,4},{7,5},{8,10},{9,11},{10,... | collective-permute-start | bytes 1966088 | tf_op jit(solution)/shard_map/gather_tokens/ppermute | solution.py:27
  103.2 43.2 %collective-permute-start.1 = (bf16[512,640]{1,0:T(8,128)(2,1)S(1)}, bf16[512,640]{1,0:T(8,128)(2,1)S(1)}, u32[]{:S(2)}, u32[]{:S(2)}) collective-permute-start(bf16[512,640]{1,0:T(8,128)(2,1)S(1)} %copy-done.32), channel_id=1, source_target_pairs={{0,1},{1,0},{2,3},{3,2},{4,5},{5,4},{6,7},{7,6},{8,9},{9,8},{10,11... | collective-permute-start | bytes 1966088 | tf_op jit(solution)/shard_map/gather_tokens/ppermute | solution.py:27
  134.8 41.1 %collective-permute-start.31 = (bf16[512,1280]{1,0:T(8,128)(2,1)S(1)}, bf16[512,1280]{1,0:T(8,128)(2,1)S(1)}, u32[]{:S(2)}, u32[]{:S(2)}) collective-permute-start(bf16[512,1280]{1,0:T(8,128)(2,1)S(1)} %copy-done.15), channel_id=1, source_target_pairs={{0,8},{8,0},{16,24},{24,16},{1,9},{9,1},{17,25},{25,17},{2,10},{10... | collective-permute-start | bytes 3932168 | tf_op jit(solution)/shard_map/ppermute | solution.py:27
  146.4 45.4 %collective-permute-start.19 = (bf16[2,2,2,1,1,40,1280]{6,5,0,1,2,4,3:T(8,128)(2,1)S(1)}, bf16[2,2,2,1,1,40,1280]{6,5,0,1,2,4,3:T(8,128)(2,1)S(1)}, u32[]{:S(2)}, u32[]{:S(2)}) collective-permute-start(bf16[2,2,2,1,1,40,1280]{6,5,0,1,2,4,3:T(8,128)(2,1)S(1)} %maximum_select_fusion.13), channel_id=1, source_target_pairs={{0,16},{8,24},{16,0},{24,8},{1,17},{9,25},{17,1},{25,9},{2,18},{10... | collective-permute-start | bytes 2457608 | tf_op jit(solution)/shard_map/gather_weights/ppermute | solution.py:27
  156.9 98.5 %collective-permute-start.24 = (bf16[2,2,1,1,160,1280]{5,4,3,2,1,0:T(8,128)(2,1)}, bf16[2,2,1,1,160,1280]{5,4,3,2,1,0:T(8,128)(2,1)}, u32[]{:S(2)}, u32[]{:S(2)}) collective-permute-start(bf16[2,2,1,1,160,1280]{5,4,3,2,1,0:T(8,128)(2,1)} %copy.68), channel_id=1, source_target_pairs={{0,1},{1,0},{2,3},{3,2},{4,5},{5,4},{6,7},{7,6},{8,9},{9,8},{10,11... | collective-permute-start | bytes 4915208 | tf_op jit(solution)/shard_map/gather_weights/ppermute | solution.py:27
  158.2 84.5 %collective-permute-start.28 = (bf16[2,2,1,1,80,2560]{5,4,0,1,3,2:T(8,128)(2,1)}, bf16[2,2,1,1,80,2560]{5,4,0,1,3,2:T(8,128)(2,1)}, u32[]{:S(2)}, u32[]{:S(2)}) collective-permute-start(bf16[2,2,1,1,80,2560]{5,4,0,1,3,2:T(8,128)(2,1)} %maximum_select_fusion.9), channel_id=1, source_target_pairs={{0,16},{8,24},{16,0},{24,8},{1,17},{9,25},{17,1},{25,9},{2,18},{10... | collective-permute-start | bytes 4915208 | tf_op jit(solution)/shard_map/gather_weights/ppermute | solution.py:27
  193.2 65.1 %collective-permute-start.20 = (bf16[2,2,2,2,1,40,1280]{6,5,0,1,2,4,3:T(8,128)(2,1)}, bf16[2,2,2,2,1,40,1280]{6,5,0,1,2,4,3:T(8,128)(2,1)}, u32[]{:S(2)}, u32[]{:S(2)}) collective-permute-start(bf16[2,2,2,2,1,40,1280]{6,5,0,1,2,4,3:T(8,128)(2,1)} %maximum_select_fusion.6), channel_id=1, source_target_pairs={{0,8},{8,0},{16,24},{24,16},{1,9},{9,1},{17,25},{25,17},{2,10},{10... | collective-permute-start | bytes 4915208 | tf_op jit(solution)/shard_map/gather_weights/ppermute | solution.py:27
  247.1 77.2 %collective-permute-start.29 = (bf16[2,2,1,2,80,2560]{5,4,0,1,3,2:T(8,128)(2,1)S(1)}, bf16[2,2,1,2,80,2560]{5,4,0,1,3,2:T(8,128)(2,1)S(1)}, u32[]{:S(2)}, u32[]{:S(2)}) collective-permute-start(bf16[2,2,1,2,80,2560]{5,4,0,1,3,2:T(8,128)(2,1)S(1)} %maximum_select_fusion.4), channel_id=1, source_target_pairs={{0,1},{1,0},{2,3},{3,2},{4,5},{5,4},{6,7},{7,6},{8,9},{9,8},{10,11... | collective-permute-start | bytes 9830408 | tf_op jit(solution)/shard_map/gather_weights/ppermute | solution.py:27
  258.0 72.0 %collective-permute-start.25 = (bf16[2,2,2,1,160,1280]{5,4,3,2,1,0:T(8,128)(2,1)S(1)}, bf16[2,2,2,1,160,1280]{5,4,3,2,1,0:T(8,128)(2,1)}, u32[]{:S(2)}, u32[]{:S(2)}) collective-permute-start(bf16[2,2,2,1,160,1280]{5,4,3,2,1,0:T(8,128)(2,1)S(1)} %maximum_select_fusion.3), channel_id=1, source_target_pairs={{0,16},{8,24},{16,0},{24,8},{1,17},{9,25},{17,1},{25,9},{2,18},{10... | collective-permute-start | bytes 9830408 | tf_op jit(solution)/shard_map/gather_weights/ppermute | solution.py:27
  266.3 68.2 %collective-permute-start.21 = (bf16[512,1280]{1,0:T(8,128)(2,1)S(1)}, bf16[512,1280]{1,0:T(8,128)(2,1)}, u32[]{:S(2)}, u32[]{:S(2)}) collective-permute-start(bf16[512,1280]{1,0:T(8,128)(2,1)S(1)} %add_convert_fusion.9), channel_id=1, source_target_pairs={{0,8},{8,0},{16,24},{24,16},{1,9},{9,1},{17,25},{25,17},{2,10},{10... | collective-permute-start | bytes 3932168 | tf_op jit(solution)/shard_map/ppermute | solution.py:27
  430.9 280.3 %collective-permute-start.57 = (bf16[2,2,2,1,160,1280]{5,4,3,2,1,0:T(8,128)(2,1)}, bf16[2,2,2,1,160,1280]{5,4,3,2,1,0:T(8,128)(2,1)}, u32[]{:S(2)}, u32[]{:S(2)}) collective-permute-start(bf16[2,2,2,1,160,1280]{5,4,3,2,1,0:T(8,128)(2,1)} %constant_dynamic-slice_fusion.7), channel_id=1, source_target_pairs={{0,16},{8,24},{16,0},{24,8},{1,17},{9,25},{17,1},{25,9},{2,18},{10... | collective-permute-start | bytes 9830408 | tf_op jit(solution)/shard_map/reduce_weights/ppermute | solution.py:27
  433.1 273.4 %collective-permute-start.63 = (bf16[2,2,1,2,80,2560]{5,4,3,2,1,0:T(8,128)(2,1)}, bf16[2,2,1,2,80,2560]{5,4,3,2,1,0:T(8,128)(2,1)}, u32[]{:S(2)}, u32[]{:S(2)}) collective-permute-start(bf16[2,2,1,2,80,2560]{5,4,3,2,1,0:T(8,128)(2,1)} %constant_dynamic-slice_fusion.3), channel_id=1, source_target_pairs={{0,1},{1,0},{2,3},{3,2},{4,5},{5,4},{6,7},{7,6},{8,9},{9,8},{10,11... | collective-permute-start | bytes 9830408 | tf_op jit(solution)/shard_map/reduce_weights/ppermute | solution.py:27
  451.6 68.0 %collective-permute-start.33 = (bf16[512,320]{0,1:T(8,128)(2,1)S(1)}, bf16[512,320]{0,1:T(8,128)(2,1)S(1)}, u32[]{:S(2)}, u32[]{:S(2)}) collective-permute-start(bf16[512,320]{0,1:T(8,128)(2,1)S(1)} %get-tuple-element.70), channel_id=1, source_target_pairs={{0,1},{1,0},{2,3},{3,2},{4,5},{5,4},{6,7},{7,6},{8,9},{9,8},{10,11... | collective-permute-start | bytes 983048 | tf_op jit(solution)/shard_map/grad_context_to_heads/ppermute | solution.py:27
  459.6 244.7 %collective-permute-start.50 = (bf16[2,2,2,2,1,40,1280]{6,5,4,3,2,1,0:T(8,128)(2,1)}, bf16[2,2,2,2,1,40,1280]{6,5,4,3,2,1,0:T(8,128)(2,1)}, u32[]{:S(2)}, u32[]{:S(2)}) collective-permute-start(bf16[2,2,2,2,1,40,1280]{6,5,4,3,2,1,0:T(8,128)(2,1)} %constant_dynamic-slice_fusion.12), channel_id=1, source_target_pairs={{0,8},{8,0},{16,24},{24,16},{1,9},{9,1},{17,25},{25,17},{2,10},{10... | collective-permute-start | bytes 4915208 | tf_op jit(solution)/shard_map/reduce_weights/ppermute | solution.py:27
  616.9 60.4 %collective-permute-start.38 = (bf16[2,512,640]{2,1,0:T(8,128)(2,1)}, bf16[2,512,640]{2,1,0:T(8,128)(2,1)}, u32[]{:S(2)}, u32[]{:S(2)}) collective-permute-start(bf16[2,512,640]{2,1,0:T(8,128)(2,1)} %slice.235), channel_id=1, source_target_pairs={{0,2},{1,3},{2,0},{3,1},{4,6},{5,7},{6,4},{7,5},{8,10},{9,11},{10,... | collective-permute-start | bytes 3932168 | tf_op jit(solution)/shard_map/reduce_tokens/ppermute | solution.py:27
  618.2 56.4 %collective-permute-start.40 = (bf16[1,2,3,2,40,1280]{5,4,1,0,3,2:T(8,128)(2,1)}, bf16[1,2,3,2,40,1280]{5,4,1,0,3,2:T(8,128)(2,1)}, u32[]{:S(2)}, u32[]{:S(2)}) collective-permute-start(bf16[1,2,3,2,40,1280]{5,4,1,0,3,2:T(8,128)(2,1)} %dynamic-slice_bitcast_fusion), channel_id=1, source_target_pairs={{0,8},{8,0},{16,24},{24,16},{1,9},{9,1},{17,25},{25,17},{2,10},{10... | collective-permute-start | bytes 3686408 | tf_op jit(solution)/shard_map/reduce_in_proj/ppermute | solution.py:27
  736.6 65.5 %collective-permute-start.58 = (bf16[2,2,1,1,160,1280]{5,4,3,2,1,0:T(8,128)(2,1)S(1)}, bf16[2,2,1,1,160,1280]{5,4,3,2,1,0:T(8,128)(2,1)S(1)}, u32[]{:S(2)}, u32[]{:S(2)}) collective-permute-start(bf16[2,2,1,1,160,1280]{5,4,3,2,1,0:T(8,128)(2,1)S(1)} %constant_dynamic-slice_fusion.6), channel_id=1, source_target_pairs={{0,1},{1,0},{2,3},{3,2},{4,5},{5,4},{6,7},{7,6},{8,9},{9,8},{10,11... | collective-permute-start | bytes 4915208 | tf_op jit(solution)/shard_map/reduce_weights/ppermute | solution.py:27
  739.7 65.1 %collective-permute-start.64 = (bf16[2,2,1,1,80,2560]{5,4,3,2,1,0:T(8,128)(2,1)S(1)}, bf16[2,2,1,1,80,2560]{5,4,3,2,1,0:T(8,128)(2,1)S(1)}, u32[]{:S(2)}, u32[]{:S(2)}) collective-permute-start(bf16[2,2,1,1,80,2560]{5,4,3,2,1,0:T(8,128)(2,1)S(1)} %constant_dynamic-slice_fusion.2), channel_id=1, source_target_pairs={{0,16},{8,24},{16,0},{24,8},{1,17},{9,25},{17,1},{25,9},{2,18},{10... | collective-permute-start | bytes 4915208 | tf_op jit(solution)/shard_map/reduce_weights/ppermute | solution.py:27
  740.1 43.8 %collective-permute-start.48 = (bf16[1,1,3,40,1280]{4,3,1,0,2:T(8,128)(2,1)S(1)}, bf16[1,1,3,40,1280]{4,3,1,0,2:T(8,128)(2,1)S(1)}, u32[]{:S(2)}, u32[]{:S(2)}) collective-permute-start(bf16[1,1,3,40,1280]{4,3,1,0,2:T(8,128)(2,1)S(1)} %maximum_bitcast_fusion.9), channel_id=1, source_target_pairs={{0,16},{8,24},{16,0},{24,8},{1,17},{9,25},{17,1},{25,9},{2,18},{10... | collective-permute-start | bytes 921608 | tf_op jit(solution)/shard_map/reduce_in_proj/ppermute | solution.py:27
  805.3 44.4 %collective-permute-start.65 = (bf16[2,1,1,1,80,2560]{5,4,3,2,1,0:T(8,128)(2,1)S(1)}, bf16[2,1,1,1,80,2560]{5,4,3,2,1,0:T(8,128)(2,1)S(1)}, u32[]{:S(2)}, u32[]{:S(2)}) collective-permute-start(bf16[2,1,1,1,80,2560]{5,4,3,2,1,0:T(8,128)(2,1)S(1)} %constant_dynamic-slice_fusion.1), channel_id=1, source_target_pairs={{0,2},{1,3},{2,0},{3,1},{4,6},{5,7},{6,4},{7,5},{8,10},{9,11},{10,... | collective-permute-start | bytes 2457608 | tf_op jit(solution)/shard_map/reduce_weights/ppermute | solution.py:27
  (132 other events, 2217.1 us)

commit v2 on v1

v2 whole, which is shorter than its diff:
```python
import functools
import math

import jax
import jax.numpy as jnp
from jax import lax
from jax.experimental import pallas as pl
from jax.experimental.pallas import tpu as pltpu
from jax.sharding import PartitionSpec as P

H = 16
HD = 80
CLIP_DEV = 4
LANES = 128
GROUP_HEADS = H // CLIP_DEV
EPSILON = 1e-05
SCORE_SCALE = HD ** (-0.5) * math.log2(math.e)
LN2 = math.log(2.0)
LOW = jnp.bfloat16
TOKEN_BLOCK = 256
QUERY_BLOCK = 256
GRAD_BLOCK = 256
UNIT_BLOCK = 512
GROUP_LANES = GROUP_HEADS * LANES
GROUP_WIDTH = GROUP_HEADS * HD
VMEM_BYTES = 56 * 1024 * 1024


def swap(value, axis, mask):
    pairs = [(source, source ^ mask) for source in range(lax.axis_size(axis))]
    return lax.ppermute(value, axis, pairs)


def dot_nt(lhs, rhs):
    return lax.dot_general(
        lhs, rhs, (((1,), (1,)), ((), ())), preferred_element_type=jnp.float32
    )


def dot_nn(lhs, rhs):
    return jnp.dot(lhs, rhs, preferred_element_type=jnp.float32)


def dot_tn(lhs, rhs):
    return lax.dot_general(
        lhs, rhs, (((0,), (0,)), ((), ())), preferred_element_type=jnp.float32
    )


def split_three(value):
    high = value.astype(LOW).astype(jnp.float32)
    rest = value - high
    middle = rest.astype(LOW).astype(jnp.float32)
    return high, middle, rest - middle


def with_lanes(block, first, columns):
    lane = lax.broadcasted_iota(jnp.int32, block.shape, 1)
    for place, column in enumerate(columns):
        block = jnp.where(lane == first + place, column, block)
    return block


def divisor(size, most):
    block = min(size, most)
    while size % block:
        block //= 2
    return block


ANYWHERE = pl.BlockSpec(memory_space=pl.ANY)


def call(body, grid, scalars, inputs, outputs, held=None, scratch=(), cost=(0, 0, 0), after=()):
    held = () if held is None else tuple(held)
    passive = held + tuple(after)
    n_scalar, n_in, n_passive, n_out = len(scalars), len(inputs), len(passive), len(outputs)

    def kernel(*refs):
        first = n_scalar + n_in
        body(*refs[:first], *refs[first + n_passive :])

    flops, moved, special = cost
    return pl.pallas_call(
        kernel,
        grid_spec=pltpu.PrefetchScalarGridSpec(
            num_scalar_prefetch=n_scalar,
            grid=grid,
            in_specs=[spec for _, spec in inputs] + [ANYWHERE] * n_passive,
            out_specs=[spec for _, spec in outputs],
            scratch_shapes=list(scratch),
        ),
        out_shape=[shape for shape, _ in outputs],
        input_output_aliases={n_scalar + n_in + i: i for i in range(len(held))},
        compiler_params=pltpu.CompilerParams(vmem_limit_bytes=VMEM_BYTES),
        cost_estimate=pl.CostEstimate(flops=int(flops), bytes_accessed=int(moved), transcendentals=int(special)),
    )(*scalars, *(array for array, _ in inputs), *passive)


def like(rows, columns, kind=LOW):
    return jax.ShapeDtypeStruct((rows, columns), kind)


def whole_block(array):
    return pl.BlockSpec(array.shape, lambda *_: (0,) * len(array.shape))


def unit_rows_of(values):
    center = values - jnp.mean(values, axis=-1, keepdims=True)
    spread = jnp.mean(center * center, axis=-1, keepdims=True)
    return center * lax.rsqrt(spread + EPSILON)


def project_kernel(limit_ref, x_ref, weight_ref, gain_ref, shift_ref, column_ref, query_ref, pair_ref, normed_ref):
    rows = x_ref.shape[0]
    unit = unit_rows_of(x_ref[...].astype(jnp.float32))
    normed = (unit * gain_ref[...] + shift_ref[...]).astype(LOW)
    normed_ref[...] = normed
    columns = column_ref[...]
    queries = dot_nt(normed, weight_ref[:GROUP_LANES, :])
    query_ref[...] = (queries * SCORE_SCALE + columns[:, :GROUP_LANES]).astype(LOW)
    pair = dot_nt(normed, weight_ref[GROUP_LANES:, :]) + columns[:, GROUP_LANES:]
    row = pl.program_id(0) * rows + lax.broadcasted_iota(jnp.int32, pair.shape, 0)
    lane = lax.broadcasted_iota(jnp.int32, pair.shape, 1)
    masked = (row >= limit_ref[0]) & (lane % LANES == HD) & (lane < GROUP_LANES)
    pair_ref[...] = jnp.where(masked, -1e30, pair).astype(LOW)


def project(number, x_block, weight, gain, shift, columns, limit, held, after=()):
    tokens, width = x_block.shape
    block = divisor(tokens, TOKEN_BLOCK)
    steps = tokens // block
    rows = CLIP_DEV * tokens

    def out(columns_out):
        return like(rows, columns_out), pl.BlockSpec((block, columns_out), lambda i, _: (number * steps + i, 0))

    return call(
        project_kernel,
        (steps,),
        (limit,),
        [(x_block, pl.BlockSpec((block, width), lambda i, _: (i, 0)))]
        + [(array, whole_block(array)) for array in (weight, gain, shift, columns)],
        [out(GROUP_LANES), out(2 * GROUP_LANES), out(width)],
        held,
        cost=(2 * tokens * weight.size, tokens * width * 8 + weight.size * 2, tokens),
        after=after,
    )


def attend_kernel(query_ref, pair_ref, context_ref, ready_ref):
    contexts = []
    for head in range(GROUP_HEADS):
        lanes = slice(head * LANES, (head + 1) * LANES)
        queries = query_ref[:, lanes]
        scores = dot_nt(queries, pair_ref[:, lanes])
        largest = jnp.max(scores, axis=1, keepdims=True)
        exponent = jnp.exp2(scores - largest)
        values = pair_ref[:, GROUP_LANES + head * LANES : GROUP_LANES + (head + 1) * LANES]
        mixed = dot_nn(exponent.astype(LOW), values)
        summed = mixed[:, HD : HD + 1]
        contexts.append((mixed / summed)[:, :HD])
        log_parts = split_three(-(largest + jnp.log2(summed)))
        ready_ref[:, lanes] = with_lanes(queries.astype(jnp.float32), HD + 1, log_parts).astype(LOW)
    context_ref[...] = jnp.concatenate(contexts, axis=1).astype(LOW)


def attend(number, queries, pair, after=()):
    rows = queries.shape[0]
    tokens = rows // CLIP_DEV
    block = divisor(tokens, QUERY_BLOCK)
    steps = tokens // block
    spot = pl.BlockSpec((block, GROUP_LANES), lambda i: (number * steps + i, 0))
    context, ready = call(
        attend_kernel,
        (steps,),
        (),
        [(queries, spot), (pair, whole_block(pair))],
        [
            (like(tokens, GROUP_WIDTH), pl.BlockSpec((block, GROUP_WIDTH), lambda i: (i, 0))),
            (like(tokens, GROUP_LANES), pl.BlockSpec((block, GROUP_LANES), lambda i: (i, 0))),
        ],
        cost=(4 * tokens * rows * GROUP_LANES * 2, rows * GROUP_LANES * 6, tokens * rows * GROUP_HEADS),
        after=after,
    )
    return context, ready


def attend_back_kernel(
    head,
    query_ref,
    key_ref,
    value_ref,
    context_ref,
    grad_ref,
    grad_query_ref,
    grad_key_ref,
    grad_value_ref,
    key_turned,
    key_total,
    value_total,
):
    step = pl.program_id(0)

    @pl.when(step == 0)
    def _():
        key_turned[...] = key_ref[...].T
        key_total[...] = jnp.zeros_like(key_total)
        value_total[...] = jnp.zeros_like(value_total)

    lanes = slice(head * HD, (head + 1) * HD)
    queries = query_ref[...]
    grad = grad_ref[:, lanes].astype(jnp.float32)
    row_term = jnp.sum(grad * context_ref[:, lanes].astype(jnp.float32), axis=1, keepdims=True)
    grad = jnp.concatenate([grad, jnp.zeros((grad.shape[0], LANES - HD), jnp.float32)], axis=1)
    grad = with_lanes(grad, HD, split_three(-row_term)).astype(LOW)
    soft = jnp.exp2(dot_nt(key_ref[...], queries))
    grad_soft = dot_nt(value_ref[...], grad)
    value_total[...] += dot_nn(soft.astype(LOW), grad)
    grad_scores = (soft * grad_soft).astype(LOW)
    key_total[...] += dot_nn(grad_scores, queries)
    grad_query = dot_nn(key_turned[...], grad_scores)
    grad_query_ref[...] = (grad_query * HD ** (-0.5)).T.astype(LOW)

    @pl.when(step == pl.num_programs(0) - 1)
    def _():
        grad_key_ref[...] = (key_total[...] * LN2).astype(LOW)
        grad_value_ref[...] = value_total[...].astype(LOW)


def attend_back(head, queries, pair, context, grad_context, held, after=()):
    rows = queries.shape[0]
    block = divisor(rows, GRAD_BLOCK)
    part = pl.BlockSpec((block, LANES), lambda i: (i, head))
    compact = pl.BlockSpec((block, GROUP_WIDTH), lambda i: (i, 0))
    out = like(rows, GROUP_LANES)
    whole = pl.BlockSpec((rows, LANES), lambda i: (0, head))
    return call(
        functools.partial(attend_back_kernel, head),
        (rows // block,),
        (),
        [
            (queries, part),
            (pair, whole),
            (pair, pl.BlockSpec((rows, LANES), lambda i: (0, GROUP_HEADS + head))),
            (context, compact),
            (grad_context, compact),
        ],
        [(out, part), (out, whole), (out, whole)],
        held,
        scratch=[
            pltpu.VMEM((LANES, rows), LOW),
            pltpu.VMEM((rows, LANES), jnp.float32),
            pltpu.VMEM((rows, LANES), jnp.float32),
        ],
        cost=(20 * rows * rows * LANES, 10 * rows * LANES * 2, rows * rows),
        after=after,
    )


def entry_back_kernel(x_ref, query_ref, key_ref, value_ref, weight_ref, partial_ref, sums_ref):
    partial = dot_nn(query_ref[...], weight_ref[:GROUP_LANES, :])
    partial += dot_nn(key_ref[...], weight_ref[GROUP_LANES : 2 * GROUP_LANES, :])
    partial += dot_nn(value_ref[...], weight_ref[2 * GROUP_LANES :, :])
    partial_ref[...] = partial.astype(LOW)
    unit = unit_rows_of(x_ref[...].astype(jnp.float32))

    @pl.when(pl.program_id(0) == 0)
    def _():
        sums_ref[...] = jnp.zeros_like(sums_ref)

    sums_ref[0:1, :] += jnp.sum(partial * unit, axis=0, keepdims=True)
    sums_ref[1:2, :] += jnp.sum(partial, axis=0, keepdims=True)


def entry_back(number, x_block, grads, weight, after=()):
    tokens, width = x_block.shape
    block = divisor(tokens, TOKEN_BLOCK)
    steps = tokens // block
    spot = pl.BlockSpec((block, width), lambda i: (i, 0))
    return call(
        entry_back_kernel,
        (steps,),
        (),
        [(x_block, spot)]
        + [(grad, pl.BlockSpec((block, GROUP_LANES), lambda i: (number * steps + i, 0))) for grad in grads]
        + [(weight, whole_block(weight))],
        [(like(tokens, width), spot), (like(8, width, jnp.float32), pl.BlockSpec((8, width), lambda i: (0, 0)))],
        cost=(2 * tokens * weight.size, tokens * width * 8 + weight.size * 2, tokens),
        after=after,
    )


def widen_kernel(normed_ref, weight_ref, bias_ref, activated_ref, slope_ref):
    widened = dot_nt(normed_ref[...], weight_ref[...]) + bias_ref[...]
    below = 0.5 + 0.5 * lax.erf(widened * math.sqrt(0.5))
    activated_ref[...] = (widened * below).astype(LOW)
    density = jnp.exp2(widened * widened * (-0.5 * math.log2(math.e))) * (1.0 / math.sqrt(2.0 * math.pi))
    slope_ref[...] = (below + widened * density).astype(LOW)


def widen(number, normed, weight, bias, held, after=()):
    tokens, width = normed.shape
    units = weight.shape[0]
    block = divisor(units, UNIT_BLOCK)
    spot = pl.BlockSpec((tokens, block), lambda i: (number, i))
    out = like(2 * tokens, units)
    return call(
        widen_kernel,
        (units // block,),
        (),
        [
            (normed, whole_block(normed)),
            (weight, pl.BlockSpec((block, width), lambda i: (i, 0))),
            (bias.reshape(1, units), pl.BlockSpec((1, block), lambda i: (0, i))),
        ],
        [(out, spot), (out, spot)],
        held,
        cost=(2 * tokens * weight.size + 40 * tokens * units, weight.size * 2 + tokens * units * 4, 2 * tokens * units),
        after=after,
    )


def split_columns(piece, core, shards):
    rows, columns = piece.shape
    span = columns // shards // 2

    def body(core_ref, piece_ref, out_ref):
        for shard in range(shards):
            low = piece_ref[:, 2 * shard * span : (2 * shard + 1) * span]
            high = piece_ref[:, (2 * shard + 1) * span : (2 * shard + 2) * span]
            out_ref[:, shard * span : (shard + 1) * span] = jnp.where(core_ref[0] == 0, low, high)

    spec = pl.BlockSpec((rows, columns // 2), lambda *_: (0, 0))
    return call(body, (1,), (core.reshape(1),), [(piece, whole_block(piece))], [(like(rows, columns // 2), spec)])[0]


def merge_columns(mine, other, core, shards):
    rows, columns = mine.shape
    span = columns // shards

    def body(core_ref, mine_ref, other_ref, out_ref):
        for shard in range(shards):
            a = mine_ref[:, shard * span : (shard + 1) * span].astype(jnp.float32)
            b = other_ref[:, shard * span : (shard + 1) * span].astype(jnp.float32)
            first = core_ref[0] == 0
            out_ref[:, 2 * shard * span : (2 * shard + 1) * span] = jnp.where(first, a, b)
            out_ref[:, (2 * shard + 1) * span : (2 * shard + 2) * span] = jnp.where(first, b, a)

    spec = pl.BlockSpec((rows, 2 * columns), lambda *_: (0, 0))
    return call(
        body,
        (1,),
        (core.reshape(1),),
        [(mine, whole_block(mine)), (other, whole_block(other))],
        [(like(rows, 2 * columns, jnp.float32), spec)],
    )[0]


def normalise(values):
    center = values - jnp.mean(values, axis=-1, keepdims=True)
    spread = jnp.mean(center * center, axis=-1, keepdims=True)
    scale = lax.rsqrt(spread + EPSILON)
    return center * scale, scale


def norm_back(grad, gain, unit, scale):
    scaled = grad * gain
    return scale * (
        scaled
        - jnp.mean(scaled, axis=-1, keepdims=True)
        - unit * jnp.mean(scaled * unit, axis=-1, keepdims=True)
    )


def pick(blocks, index, axis=0):
    return lax.dynamic_index_in_dim(blocks, index, axis, keepdims=False)


def widen_bit(held, place, axis, mask, mine):
    came = swap(held, axis, mask)
    return jnp.where(
        mine == 1,
        jnp.concatenate([came, held], axis=place),
        jnp.concatenate([held, came], axis=place),
    )


def gather_bits(piece, bits):
    held = piece.reshape((1,) * len(bits) + piece.shape)
    for place in sorted(range(len(bits)), key=lambda i: bits[i][3]):
        axis, mask, mine, _ = bits[place]
        held = widen_bit(held, place, axis, mask, mine)
    return held


def halve(held, place, axis, mask, mine):
    kept = pick(held, mine, place)
    came = swap(pick(held, 1 - mine, place), axis, mask)
    return (kept.astype(jnp.float32) + came.astype(jnp.float32)).astype(LOW)


def gather_near(held, turn):
    blocks = held.shape[0]
    held = held.reshape(-1, held.shape[2])
    masks = [(i, 0, 0) for i in range(blocks)]
    copies = lax.axis_size("dp") // 2
    steps = [("dp", 1 << level) for level in range(copies.bit_length() - 1)]
    steps = [("fsdp", 1)] + steps if turn else steps + [("fsdp", 1)]
    parts, stages = [], []
    for number, (axis, mask) in enumerate(steps):
        came = swap(held, axis, 2 * mask if axis == "dp" else mask)
        stages.append(came)
        came_masks = [
            (far, near ^ (mask if axis == "fsdp" else 0), copy ^ (mask if axis == "dp" else 0))
            for far, near, copy in masks
        ]
        if number == len(steps) - 1:
            parts = [(held, masks), (came, came_masks)]
        else:
            held, masks = jnp.concatenate([held, came]), masks + came_masks
    return parts, stages


def assemble(low, high, shape, block_rows, axis):
    copies = lax.axis_size("dp") // 2
    near, copy = lax.axis_index("fsdp") % 2, lax.axis_index("dp") // 2
    columns = low[0][0].shape[1]

    def target(mask):
        return ((2 * mask[0] + (near ^ mask[1])) * copies + (copy ^ mask[2])).astype(jnp.int32)

    order = [mask for _, masks in low for mask in masks]
    out_rows = shape[0] // len(order)
    if block_rows % 16:
        out = jnp.zeros(shape, LOW)
        for offset, parts in ((0, low), (1, high)):
            for array, masks in parts:
                for number, mask in enumerate(masks):
                    block = array[number * block_rows : (number + 1) * block_rows]
                    start = target(mask) * out_rows
                    shift = (0, offset * columns) if axis else (offset * block_rows, 0)
                    out = lax.dynamic_update_slice(out, block, (start + shift[0], shift[1]))
        return out

    sources = low + high
    tables, uses = [], []
    for _, masks in sources:
        at, table = 0, []
        for mask in order:
            at = masks.index(mask) if mask in masks else at
            table.append(at)
        tables.append(table)
        uses.append([int(mask in masks) for mask in order])
    steps = len(order)
    flat = [target(mask) for mask in order]
    fixed = jnp.array([x for table in tables + uses for x in table], jnp.int32)
    scalars = jnp.concatenate([jnp.stack(flat), fixed])

    def body(table_ref, *refs):
        step = pl.program_id(0)
        out_ref = refs[-1]
        for part, source in enumerate(refs[:-1]):
            first = part < len(low)
            if axis:
                spot = (slice(None), slice(0, columns) if first else slice(columns, 2 * columns))
            else:
                spot = (slice(0, block_rows) if first else slice(block_rows, 2 * block_rows), slice(None))

            @pl.when(table_ref[steps * (1 + len(sources) + part) + step] == 1)
            def _(source=source, spot=spot):
                out_ref[spot] = source[...]

    def source_spec(part):
        return pl.BlockSpec((block_rows, columns), lambda i, t: (t[steps * (1 + part) + i], 0))

    out_block = (block_rows, 2 * columns) if axis else (2 * block_rows, columns)
    return call(
        body,
        (steps,),
        (scalars,),
        [(array, source_spec(part)) for part, (array, _) in enumerate(sources)],
        [(like(*shape), pl.BlockSpec(out_block, lambda i, t: (t[i], 0)))],
        cost=(0, 4 * shape[0] * shape[1], 0),
    )[0]


def zero_after(*arrays):
    zero = jnp.int32(0)
    for array in arrays:
        first = array[(0,) * array.ndim].astype(jnp.float32)
        zero += (jnp.abs(first) * 2.0 < -1.0).astype(jnp.int32)
    return zero


def on_device(
    hidden_states,
    clip_lengths,
    norm_gains,
    norm_shifts,
    proj_biases,
    up_bias,
    in_proj,
    out_proj,
    up_proj,
    down_proj,
    cotangent,
):
    tokens_here, width = hidden_states.shape
    fsdp_count = lax.axis_size("fsdp")
    dp_count = lax.axis_size("dp")
    fsdp_index = lax.axis_index("fsdp")
    dp_index = lax.axis_index("dp")
    core = dp_index % 2
    copies = dp_count // 2
    copy_index = dp_index // 2
    region = (dp_index * fsdp_count + fsdp_index) // CLIP_DEV
    place = fsdp_index % CLIP_DEV
    length = lax.dynamic_index_in_dim(clip_lengths, region, keepdims=False)
    span = tokens_here * CLIP_DEV
    hidden_units = up_bias.shape[0]
    positions = jnp.arange(tokens_here, dtype=jnp.int32)
    row_valid = (place * tokens_here + positions < length).astype(jnp.float32)
    copy_levels = copies.bit_length() - 1
    fsdp_levels = fsdp_count.bit_length() - 1
    far_count = fsdp_count // 2
    half = width // 2

    core_bit = ("dp", 1, core, 1000)
    copy_bits = [("dp", 2 << level, copy_index >> level & 1, 200 - level) for level in reversed(range(copy_levels))]
    fsdp_bits = [
        ("fsdp", 1 << level, fsdp_index >> level & 1, fsdp_count - level)
        for level in reversed(range(fsdp_levels))
    ]

    with jax.named_scope("gather_tokens"):
        near = swap(hidden_states, "fsdp", 1)
        far = swap(hidden_states, "fsdp", 2)
        both = jnp.concatenate([swap(near[:, :half], "fsdp", 2), swap(far[:, half:], "fsdp", 1)], axis=1)
        clip_blocks = [hidden_states, near, far, both]

    with jax.named_scope("gather_in_proj"):
        rounds = fsdp_count // CLIP_DEV
        unit_rows = in_proj.shape[0] // 3
        piece_rows = unit_rows // dp_count
        own_units = in_proj.reshape(3, 2, copies, piece_rows, width)
        own_units = pick(pick(own_units, core, 1), copy_index, 1)

        def route(slot, turn):
            pairs = []
            for source in range(fsdp_count):
                unit = (3 * source + slot) % fsdp_count
                owner, spot = unit // rounds, unit % rounds
                pairs.append((source, owner + CLIP_DEV * ((spot + turn) % rounds)))
            return pairs

        entry_bits = [core_bit] + copy_bits
        came = jnp.stack(
            [
                jnp.stack([lax.ppermute(own_units[slot], "fsdp", route(slot, turn)) for turn in range(rounds)])
                for slot in range(3)
            ]
        )
        came = gather_bits(came, entry_bits)
        came = came.reshape(dp_count, 3, rounds, piece_rows, width)
        came = jnp.moveaxis(came, 0, 2).reshape(3, rounds, unit_rows, width)
        lap = fsdp_index // CLIP_DEV

        def slot_of(kind, spot):
            return (place * rounds + spot + kind * fsdp_count) % 3

        weight_rows = jnp.stack(
            [
                jnp.concatenate(
                    [
                        pick(pick(came, slot_of(kind, spot)), (lap - spot) % rounds)
                        for spot in range(rounds)
                    ]
                )
                for kind in range(3)
            ]
        )
        padded_width = 3 * GROUP_LANES
        weight_in = jnp.pad(
            weight_rows.reshape(3 * GROUP_HEADS, HD, width), ((0, 0), (0, LANES - HD), (0, 0))
        ).reshape(padded_width, width)

    zeros = jnp.zeros((width,), jnp.float32)
    group_bias = jnp.stack([proj_biases[0] * SCORE_SCALE, zeros, proj_biases[1]])
    group_bias = pick(group_bias.reshape(3, CLIP_DEV, GROUP_HEADS, HD), place, 1)
    group_bias = jnp.pad(group_bias, ((0, 0), (0, 0), (0, LANES - HD)))
    lane = jnp.arange(LANES)
    spare = jnp.stack(
        [
            lane == HD,
            (lane > HD) & (lane <= HD + 3),
            (lane >= HD) & (lane < HD + 3),
        ]
    ).astype(jnp.float32)
    columns = (group_bias + spare[:, None]).reshape(1, padded_width)
    held = None
    for number in range(CLIP_DEV):
        limit = (length - (place ^ number) * tokens_here).reshape(1)
        held = project(
            number, clip_blocks[number], weight_in, norm_gains[0:1], norm_shifts[0:1], columns, limit, held
        )
    queries, pair, normed_one = held

    with jax.named_scope("gather_up_and_out_proj"):
        out_rows = out_proj.shape[0] // dp_count
        shard_units = up_proj.shape[0]
        half_units = shard_units // 2
        up_rows = half_units // copies
        up_part = up_rows // 2
        zero = zero_after(near, far, came)
        out_piece = pick(pick(out_proj.reshape(copies, 2, out_rows, width), copy_index + zero), core)
        up_piece = pick(pick(up_proj.reshape(2, copies, up_rows, width), core + zero), copy_index)
        up_far = gather_bits(jnp.concatenate([up_piece, out_piece]), fsdp_bits[:-1])
        up_far = up_far.reshape(far_count, up_rows + out_rows, width)
    with jax.named_scope("gather_out_proj"):
        out_full = up_far[:, up_rows:].reshape((far_count, 1) + (1,) * copy_levels + (1, out_rows, width))
        out_stages = []
        for number, bit in enumerate([fsdp_bits[-1]] + copy_bits + [core_bit]):
            out_full = widen_bit(out_full, number + 1, *bit[:3])
            out_stages.append(out_full)
        out_full = out_full.reshape(width, width)
    with jax.named_scope("gather_up_proj"):
        low, low_stages = gather_near(up_far[:, :up_part], True)
        high, high_stages = gather_near(up_far[:, up_part:up_rows], False)
        up_stages = [low_stages, high_stages]
        up_half = assemble(low, high, (hidden_units // 2, width), up_part, 0)
    with jax.named_scope("gather_down_proj"):
        down_rows = down_proj.shape[0] // copies
        quarter = hidden_units // 4
        down_piece = pick(down_proj.reshape(copies, down_rows, hidden_units), copy_index + zero_after(up_far))
        down_piece = split_columns(down_piece, core, fsdp_count)
        down_piece = jnp.concatenate([down_piece[:, :quarter], down_piece[:, quarter:]])
        down_far = gather_bits(down_piece, fsdp_bits[:-1]).reshape(far_count, 2 * down_rows, quarter)
        low, low_stages = gather_near(down_far[:, :down_rows], True)
        high, high_stages = gather_near(down_far[:, down_rows:], False)
        down_half = assemble(low, high, (width, hidden_units // 2), down_rows, 1)

    contexts, ready = [None] * CLIP_DEV, [None] * CLIP_DEV
    gates = [[up_far], out_stages[:1], [up_stages[0][0], up_stages[1][0], out_stages[1]], [down_far, out_stages[-1]]]
    for number, gate in zip((3, 1, 2, 0), gates, strict=True):
        contexts[number], ready[number] = attend(number, queries, pair, gate)
    with jax.named_scope("context_back"):
        parts = [contexts[0]] + [swap(contexts[j], "fsdp", j) for j in range(1, CLIP_DEV)]
        parts = jnp.stack(parts)
        context_low = jnp.concatenate([pick(parts, place ^ group) for group in range(CLIP_DEV)], axis=1)
    context_heads = jnp.concatenate(contexts)
    queries_ready = jnp.concatenate(ready)

    inputs = hidden_states.astype(jnp.float32)
    grad_other = swap(cotangent, "dp", 1)
    grad_pair = jnp.concatenate([cotangent, grad_other])
    attention = dot_nt(context_low, out_full) + proj_biases[2]
    middle = inputs + attention
    unit_two, scale_two = normalise(middle)
    normed_two = (unit_two * norm_gains[1] + norm_shifts[1]).astype(LOW)
    normed_other = swap(normed_two, "dp", 1)
    half_bias = pick(up_bias.reshape(fsdp_count, 2, half_units), core, 1).reshape(hidden_units // 2)
    held = widen(0, normed_two, up_half, half_bias, None)
    activated, slope = widen(1, normed_other, up_half, half_bias, held)
    normed_pair = jnp.concatenate([normed_two, normed_other])
    grad_activated = dot_nn(grad_pair, down_half)
    grad_widened = (grad_activated * slope.astype(jnp.float32)).astype(LOW)

    def over_cores(rows, product):
        sent = product(rows[tokens_here:]).astype(LOW)
        return product(rows[:tokens_here]) + swap(sent, "dp", 1).astype(jnp.float32)

    grad_normed_two = over_cores(grad_widened, lambda rows: dot_nn(rows, up_half))
    feedforward = over_cores(activated, lambda rows: dot_nt(rows, down_half)) + proj_biases[3]
    outputs = (middle + feedforward).astype(LOW)
    stat_terms = jnp.stack(
        [
            jnp.sum(row_valid * jnp.sum(middle * middle, axis=1)),
            jnp.sum(row_valid * jnp.sum(attention * attention, axis=1)),
            jnp.sum(row_valid * jnp.sum(feedforward * feedforward, axis=1)),
        ]
    )
    grad_out = cotangent.astype(jnp.float32)
    grad_middle = grad_out + norm_back(grad_normed_two, norm_gains[1], unit_two, scale_two)
    grad_attention = grad_middle.astype(LOW)
    grad_context = dot_nn(grad_attention, out_full).astype(LOW)

    with jax.named_scope("grad_context_to_heads"):
        groups = [grad_context[:, i * GROUP_WIDTH : (i + 1) * GROUP_WIDTH] for i in range(CLIP_DEV)]
        groups = jnp.stack(groups)
        sends = [pick(groups, place ^ j) for j in range(CLIP_DEV)]
        grad_heads = jnp.concatenate([sends[0]] + [swap(sends[j], "fsdp", j) for j in range(1, CLIP_DEV)])

    grad_down = dot_tn(grad_pair, activated).astype(LOW)
    grad_up = dot_tn(grad_widened, normed_pair).astype(LOW)
    grad_exit = dot_tn(grad_attention, context_low).astype(LOW)

    def reduce_copies(grad, axis):
        grad = grad.reshape(grad.shape[:axis] + (2,) * copy_levels + grad.shape[axis + 1 :])
        for level in reversed(range(copy_levels)):
            grad = halve(grad, axis, "dp", 2 << level, copy_index >> level & 1)
        return grad

    def reduce_near(grad, turn):
        if turn:
            first = reduce_copies(grad, 2)
            return halve(first, 1, "fsdp", 1, fsdp_index % 2), first
        first = halve(grad, 1, "fsdp", 1, fsdp_index % 2)
        return reduce_copies(first, 1), first

    def reduce_far(grad):
        stages = []
        grad = grad.reshape((2,) * (fsdp_levels - 1) + grad.shape[1:])
        for axis, mask, mine, _ in fsdp_bits[:-1]:
            grad = halve(grad, 0, axis, mask, mine)
            stages.append(grad)
        return grad, stages

    with jax.named_scope("reduce_down_proj"):
        grad = grad_down.reshape(far_count, 2, copies, down_rows, hidden_units // 2)
        low_half, low_first = reduce_near(grad[..., :quarter], True)
        high_half, high_first = reduce_near(grad[..., quarter:], False)
        down_first = [low_first, high_first]
        down_second = jnp.concatenate([low_half, high_half], axis=1)
        down_sum, down_stages = reduce_far(down_second)
        down_sum = jnp.concatenate([down_sum[:down_rows], down_sum[down_rows:]], axis=1)
        down_sum = gather_bits(down_sum, copy_bits).reshape(down_rows * copies, hidden_units // 2)
        down_sum = merge_columns(down_sum, swap(down_sum, "dp", 1), core, fsdp_count)
    with jax.named_scope("reduce_up_proj"):
        grad = grad_up.reshape(far_count, 2, copies, 2, up_part, width)
        low_half, low_first = reduce_near(grad[:, :, :, 0], True)
        high_half, high_first = reduce_near(grad[:, :, :, 1], False)
        up_first = [low_first, high_first]
        exit_core = halve(grad_exit.reshape(far_count, 2, copies, 2, out_rows, width), 3, "dp", 1, core)
        exit_grad, exit_first = reduce_near(exit_core, True)
        up_second = jnp.concatenate([low_half, high_half, exit_grad], axis=1)
        sums, far_stages = reduce_far(up_second)
        sums = gather_bits(sums, [core_bit] + copy_bits).reshape(2, copies, up_rows + out_rows, width)
        up_sum = sums[:, :, :up_rows].reshape(up_proj.shape).astype(jnp.float32)
        exit_sum = jnp.moveaxis(sums[:, :, up_rows:], 0, 1).reshape(out_proj.shape).astype(jnp.float32)

    held = None
    gates = [[], down_first, up_first + [exit_core], [down_second, exit_first]]
    for head in range(GROUP_HEADS):
        held = attend_back(head, queries_ready, pair, context_heads, grad_heads, held, gates[head])
    grad_query, grad_key, grad_value = held
    kinds = (grad_query, grad_key, grad_value)

    with jax.named_scope("reduce_tokens"):
        partial = [None] * CLIP_DEV
        entry_sums = 0.0
        gates = {3: [up_second], 1: [], 2: [down_stages[0]], 0: []}
        for number in (3, 1, 2, 0):
            partial[number], sums = entry_back(number, clip_blocks[number], kinds, weight_in, gates[number])
            entry_sums += sums[:2]
        came_a = swap(partial[3][:, :half], "fsdp", 2)
        came_b = swap(partial[3][:, half:], "fsdp", 1)
        near_sum = jnp.concatenate(
            [
                (partial[1][:, :half].astype(jnp.float32) + came_a.astype(jnp.float32)).astype(LOW),
                partial[1][:, half:],
            ],
            axis=1,
        )
        far_sum = jnp.concatenate(
            [
                partial[2][:, :half],
                (partial[2][:, half:].astype(jnp.float32) + came_b.astype(jnp.float32)).astype(LOW),
            ],
            axis=1,
        )
        grad_normed_one = partial[0].astype(jnp.float32)
        grad_normed_one += swap(near_sum, "fsdp", 1).astype(jnp.float32)
        grad_normed_one += swap(far_sum, "fsdp", 2).astype(jnp.float32)

    with jax.named_scope("reduce_in_proj"):
        entry = jnp.stack([dot_tn(grad, normed_one).astype(LOW) for grad in kinds])
        entry = entry.reshape(3, GROUP_HEADS, LANES, width)[:, :, :HD]
        entry = entry.reshape(3, rounds, 2, copies, piece_rows, width)
        entry = halve(entry, 2, "dp", 1, core)
        entry = reduce_copies(entry, 2)
        totals = []
        for slot in range(3):
            total = 0.0
            for turn in range(rounds):
                spot = (lap - turn) % rounds
                kind = ((slot - place * rounds - spot) * pow(fsdp_count, -1, 3)) % 3
                sent = pick(pick(entry, kind), spot)
                back = [(target, source) for source, target in route(slot, turn)]
                total = total + lax.ppermute(sent, "fsdp", back).astype(jnp.float32)
            totals.append(total.astype(LOW))
        entry_sum = gather_bits(jnp.stack(totals), entry_bits)
        entry_sum = entry_sum.reshape(dp_count, 3, piece_rows, width)
        entry_sum = jnp.moveaxis(entry_sum, 1, 0).reshape(in_proj.shape).astype(jnp.float32)

    unit_one, scale_one = normalise(inputs)
    grad_hidden = grad_middle + norm_back(grad_normed_one, norm_gains[0], unit_one, scale_one)

    def place_heads(grads):
        sums = jnp.sum(grads.astype(jnp.float32), axis=0).reshape(GROUP_HEADS, LANES)[:, :HD]
        rows = jnp.zeros((CLIP_DEV, GROUP_WIDTH), jnp.float32)
        return lax.dynamic_update_index_in_dim(rows, sums.reshape(GROUP_WIDTH), place, 0).reshape(width)

    with jax.named_scope("small_sums"):
        half_up = jnp.sum(grad_widened.astype(jnp.float32), axis=0).reshape(fsdp_count, half_units)
        up_terms = jnp.zeros((fsdp_count, 2, half_units), jnp.float32)
        up_terms = lax.dynamic_update_index_in_dim(up_terms, half_up, core, 1).reshape(hidden_units // width, width)
        small = jnp.concatenate(
            [
                jnp.stack(
                    [
                        jnp.sum(grad_normed_two * unit_two, axis=0),
                        jnp.sum(grad_normed_two, axis=0),
                        place_heads(grad_query),
                        place_heads(grad_value),
                        jnp.sum(grad_attention.astype(jnp.float32), axis=0),
                        jnp.sum(grad_out, axis=0),
                        jnp.pad(stat_terms, (0, width - 3)),
                    ]
                ),
                up_terms,
                entry_sums,
            ]
        )
        for axis in ("dp", "fsdp"):
            for level in range(lax.axis_size(axis).bit_length() - 1):
                small = small + swap(small, axis, 1 << level)
    valid_count = jnp.sum(clip_lengths).astype(jnp.float32) * width
    root_means = jnp.sqrt(small[6, :3] / valid_count)
    return (
        outputs,
        grad_hidden.astype(LOW),
        entry_sum,
        exit_sum,
        up_sum,
        down_sum,
        jnp.stack([small[-2], small[0]]),
        jnp.stack([small[-1], small[1]]),
        small[2:6],
        small[7:-2].reshape(hidden_units),
        root_means,
    )


def solution(mesh):
    in_specs = (
        P(("dp", "fsdp"), None),
        P(),
        P(),
        P(),
        P(),
        P(),
        P("fsdp", None),
        P("fsdp", None),
        P("fsdp", None),
        P("fsdp", None),
        P(("dp", "fsdp"), None),
    )
    out_specs = (
        P(("dp", "fsdp"), None),
        P(("dp", "fsdp"), None),
        P("fsdp", None),
        P("fsdp", None),
        P("fsdp", None),
        P("fsdp", None),
        P(),
        P(),
        P(),
        P(),
        P(),
    )
    return jax.shard_map(
        on_device, mesh=mesh, in_specs=in_specs, out_specs=out_specs, check_vma=False
    )
```

time: 931 us -> 769 us (0.83)
  waiting for transfers between devices: 329 us -> 201 us
  Pallas kernels: 88.3 us -> 206 us
  matrix products: 127 us -> 79.1 us
  other arithmetic: 119 us -> 75.2 us
  blocking collectives: 42.7 us -> 0 us
  local copies, waits for them, and re-layouts: 101 us -> 84.7 us
    ppermute x57 -> x63, waiting for transfers between devices: 320 us -> 154 us  [swap(): return lax.ppermute(value, axis, pairs)]
    pallas_call x2 -> x22, Pallas kernels: 88.3 us -> 206 us  [call(): pl.pallas_call(kernel, grid_spec=pltpu.PrefetchScalarGridSpec(num_scalar_...]
    psum x1 -> x0, blocking collectives: 42.7 us -> none  [on_device(): lax.psum((jnp.stack([gain_one, jnp.sum(grad_normed_two * unit_two, axis=0...]
    dot_general x4, matrix products: 61.7 us -> 29 us  [dot_nn(): return jnp.dot(lhs, rhs, preferred_element_type=jnp.float32)]
    ppermute x6, waiting for transfers between devices: 0.02 us -> 21.1 us  [on_device(): lax.ppermute(own_units[slot], 'fsdp', route(slot, turn))]
    select_n x21 -> x14, other arithmetic: 29.3 us -> 11.6 us  [widen_bit(): jnp.where(mine == 1, jnp.concatenate([came, held], axis=place), jnp.conca...]
    ppermute x6, waiting for transfers between devices: 9.18 us -> 25.6 us  [on_device(): total = total + lax.ppermute(sent, 'fsdp', back).astype(jnp.float32)]
    dot_general x4 -> x3, matrix products: 33.5 us -> 19.3 us  [dot_nt(): lax.dot_general(lhs, rhs, (((1,), (1,)), ((), ())), preferred_element_typ...]
  transfers between devices with their start and end apart: 69 -> 75, of which waited for: 23 -> 21; matrix products, arithmetic and copies ran while one was open for 27% -> 25% of each run, Pallas kernels for 10% -> 26%
where the time goes in v2:
time: 769 us; the launch traced here: 761 us
  Pallas kernels  206 us (27%)
  waiting for transfers between devices  201 us (26%)
  starting transfers between devices  107 us (14%)
  local copies, waits for them, and re-layouts  84.7 us (11%)
  matrix products  79.1 us (10%)
  other arithmetic  75.2 us (10%)
  between operations  8.7 us (1%)
    pallas_call x22, Pallas kernels, call(): pl.pallas_call(kernel, grid_spec=pltpu.PrefetchScalarGridSpec(num_scalar_...  206 us
    ppermute x63, waiting for transfers between devices, swap(): return lax.ppermute(value, axis, pairs)  154 us
    ppermute x63, starting transfers between devices, swap(): return lax.ppermute(value, axis, pairs)  82.3 us
    dot_general x6, matrix products, dot_tn(): lax.dot_general(lhs, rhs, (((0,), (0,)), ((), ())), preferred_element_typ...  30.8 us
    dot_general x4, matrix products, dot_nn(): return jnp.dot(lhs, rhs, preferred_element_type=jnp.float32)  29 us
    ppermute x6, waiting for transfers between devices, on_device(): total = total + lax.ppermute(sent, 'fsdp', back).astype(jnp.float32)  25.6 us
    convert_element_type x16, other arithmetic, halve(): return (kept.astype(jnp.float32) + came.astype(jnp.float32)).astype(LOW)  23.5 us
    ppermute x6, waiting for transfers between devices, on_device(): lax.ppermute(own_units[slot], 'fsdp', route(slot, turn))  21.1 us
  transfers between devices with their start and end apart: 75, of which 21 were waited for; matrix products, arithmetic and copies ran while one was open for 25% of the time, Pallas kernels for 26%

profile of v2, /device:TPU:3, one launch (start us, length us, event | category | flops | bytes accessed | tf_op | source)
XLA Modules:
  0.0 761.4 jit_solution(16867049191446297678)
XLA Ops:
  17.8 17.3 %collective-permute-done.9 = bf16[40,1280]{1,0:T(8,128)(2,1)S(1)} collective-permute-done((bf16[40,1280]{1,0:T(8,128)(2,1)S(1)}, bf16[40,1280]{1,0:T(8,128)(2,1)S(1)}, u32[]{:S(2)}, u32[]{:S(2)}) %collective-permute-start.9) | collective-permute-done | bytes 102432 | tf_op jit(solution)/shard_map/gather_in_proj/ppermute | solution.py:560
  91.8 22.3 %collective-permute-done.12 = bf16[1,1,200,1280]{3,2,1,0:T(8,128)(2,1)S(1)} collective-permute-done((bf16[1,1,200,1280]{3,2,1,0:T(8,128)(2,1)S(1)}, bf16[1,1,200,1280]{3,2,1,0:T(8,128)(2,1)S(1)}, u32[]{:S(2)}, u32[]{:S(2)}) %collective-permute-start.12) | collective-permute-done | bytes 512032 | tf_op jit(solution)/shard_map/gather_up_and_out_proj/ppermute | solution.py:31
  158.7 12.4 %collective-permute-done.16 = bf16[4,1,1,1,40,1280]{5,4,0,1,3,2:T(8,128)(2,1)S(1)} collective-permute-done((bf16[4,1,1,1,40,1280]{5,4,0,1,3,2:T(8,128)(2,1)}, bf16[4,1,1,1,40,1280]{5,4,0,1,3,2:T(8,128)(2,1)S(1)}, u32[]{:S(2)}, u32[]{:S(2)}) %collective-permute-start.16) | collective-permute-done | bytes 409632 | tf_op jit(solution)/shard_map/gather_out_proj/ppermute | solution.py:31
  178.6 14.9 %collective-permute-done.17 = bf16[4,2,1,1,40,1280]{5,4,0,1,3,2:T(8,128)(2,1)S(1)} collective-permute-done((bf16[4,2,1,1,40,1280]{5,4,0,1,3,2:T(8,128)(2,1)S(1)}, bf16[4,2,1,1,40,1280]{5,4,0,1,3,2:T(8,128)(2,1)S(1)}, u32[]{:S(2)}, u32[]{:S(2)}) %collective-permute-start.17) | collective-permute-done | bytes 819232 | tf_op jit(solution)/shard_map/gather_out_proj/ppermute | solution.py:31
  201.1 10.1 %shard_map.219 = (bf16[512,320]{1,0:T(8,128)(2,1)}, bf16[512,512]{1,0:T(8,128)(2,1)}) custom-call(bf16[2048,512]{1,0:T(8,128)(2,1)} %get-tuple-element.64.refs_0_, bf16[2048,1024]{1,0:T(8,128)(2,1)} %get-tuple-element.65.refs_1_.refs_2_, bf16[4,200,1280]{2,1,0:T(8,128)(2,1)} %bitcast.326), custom_call_target="tpu_custom_call" | custom-call | flops 4294967296 | bytes 6291456 | tf_op jit(solution)/shard_map/pallas_call | solution.py:84
  213.4 9.9 %shard_map.217 = (bf16[512,320]{1,0:T(8,128)(2,1)}, bf16[512,512]{1,0:T(8,128)(2,1)}) custom-call(bf16[2048,512]{1,0:T(8,128)(2,1)} %get-tuple-element.64.refs_0_, bf16[2048,1024]{1,0:T(8,128)(2,1)} %get-tuple-element.65.refs_1_.refs_2_, bf16[4,2,1,1,40,1280]{5,4,3,2,1,0:T(8,128)(2,1)} %copy.55.refs_2_), custom_call_target="tpu_custom_call" | custom-call | flops 4294967296 | bytes 6291456 | tf_op jit(solution)/shard_map/pallas_call | solution.py:84
  224.7 10.0 %shard_map.218 = (bf16[512,320]{1,0:T(8,128)(2,1)}, bf16[512,512]{1,0:T(8,128)(2,1)}) custom-call(bf16[2048,512]{1,0:T(8,128)(2,1)} %get-tuple-element.64.refs_0_, bf16[2048,1024]{1,0:T(8,128)(2,1)} %get-tuple-element.65.refs_1_.refs_2_, bf16[320,1280]{1,0:T(8,128)(2,1)} %collective-permute-done.20.refs_2_, bf16[320,1280]{1,0:T(8,128)(2,1)} %copy-done.51, ...), custom_call_target="tpu_custom_call" | custom-call | flops 4294967296 | bytes 6291456 | tf_op jit(solution)/shard_map/pallas_call | solution.py:84
  236.9 9.2 %collective-permute-done.29 = bf16[320,1280]{1,0:T(8,128)(2,1)S(1)} collective-permute-done((bf16[320,1280]{1,0:T(8,128)(2,1)}, bf16[320,1280]{1,0:T(8,128)(2,1)S(1)}, u32[]{:S(2)}, u32[]{:S(2)}) %collective-permute-start.29) | collective-permute-done | bytes 819232 | tf_op jit(solution)/shard_map/gather_down_proj/ppermute | solution.py:31
  251.0 12.4 %gather_up_proj.1.refs_1_ = bf16[2560,1280]{1,0:T(8,128)(2,1)} custom-call(s32[144]{0:T(256)} %concatenate.348.refs_0_, bf16[640,1280]{1,0:T(8,128)(2,1)} %copy-done.26, bf16[640,1280]{1,0:T(8,128)(2,1)} %collective-permute-done.25.refs_2_, bf16[640,1280]{1,0:T(8,128)(2,1)} %pad_maximum_fusion.5.refs_3_, bf16[640,1280]{1,0:T(8,128)(2,1)} %collective-permute-done.26.refs_4_), custom_call_target="tpu_custom_call" | custom-call | bytes 13107200 | tf_op jit(solution)/shard_map/gather_up_proj/pallas_call | solution.py:84
  268.2 10.3 %shard_map.216 = (bf16[512,320]{1,0:T(8,128)(2,1)}, bf16[512,512]{1,0:T(8,128)(2,1)}) custom-call(bf16[2048,512]{1,0:T(8,128)(2,1)} %get-tuple-element.64.refs_0_, bf16[2048,1024]{1,0:T(8,128)(2,1)} %get-tuple-element.65.refs_1_.refs_2_, bf16[4,160,1280]{2,1,0:T(8,128)(2,1)} %bitcast.332, bf16[4,2,2,2,40,1280]{5,4,3,2,1,0:T(8,128)(2,1)} %copy.54.refs_3_), custom_call_target="tpu_custom_call" | custom-call | flops 4294967296 | bytes 6291456 | tf_op jit(solution)/shard_map/pallas_call | solution.py:84
  300.5 9.8 %shard_map.220 = (bf16[1024,2560]{1,0:T(8,128)(2,1)}, bf16[1024,2560]{1,0:T(8,128)(2,1)}) custom-call(bf16[512,1280]{1,0:T(8,128)(2,1)} %copy-done.43, bf16[2560,1280]{1,0:T(8,128)(2,1)} %gather_up_proj.1.refs_1_, f32[1,2560]{1,0:T(1,128)} %reshape_reshape.4.refs_2_), custom_call_target="tpu_custom_call" | custom-call | flops 3407872000 | bytes 11796480 | tf_op jit(solution)/shard_map/pallas_call | solution.py:84
  310.3 12.4 %gather_down_proj.3 = bf16[1280,2560]{1,0:T(8,128)(2,1)} custom-call(s32[144]{0:T(256)} %concatenate.348.refs_0_, bf16[640,1280]{1,0:T(8,128)(2,1)} %copy-done.25, bf16[640,1280]{1,0:T(8,128)(2,1)} %collective-permute-done.28.refs_2_, bf16[640,1280]{1,0:T(8,128)(2,1)} %pad_maximum_fusion.7.refs_3_, bf16[640,1280]{1,0:T(8,128)(2,1)} %collective-permute-done.30.refs_4_), custom_call_target="tpu_custom_call" | custom-call | bytes 13107200 | tf_op jit(solution)/shard_map/gather_down_proj/pallas_call | solution.py:84
  323.8 10.0 %shard_map.221 = (bf16[1024,2560]{1,0:T(8,128)(2,1)}, bf16[1024,2560]{1,0:T(8,128)(2,1)}) custom-call(bf16[512,1280]{1,0:T(8,128)(2,1)} %copy-done.40, bf16[2560,1280]{1,0:T(8,128)(2,1)} %gather_up_proj.1.refs_1_, f32[1,2560]{1,0:T(1,128)} %reshape_reshape.4.refs_2_, ...), custom_call_target="tpu_custom_call", output_to_operand_aliasing={{0}: (3, {}), {1}: (4, {})} | custom-call | flops 3407872000 | bytes 11796480 | tf_op jit(solution)/shard_map/pallas_call | solution.py:84
  347.8 9.0 %convert_reduce_fusion = (f32[2560]{0:T(1024)S(1)}, bf16[1024,2560]{1,0:T(8,128)(2,1)S(1)}) fusion(bf16[1024,2560]{1,0:T(8,128)(2,1)} %get-tuple-element.73, bf16[1024,1280]{1,0:T(8,128)(2,1)S(1)} %copy-done.54, bf16[1280,2560]{1,0:T(8,128)(2,1)S(1)} %copy-done.24), kind=kOutput, calls=%fused_computation.2 | convolution fusion | flops 6723991040 | bytes 19671040 | tf_op jit(solution)/shard_map/dot_general | solution.py:41
  386.2 10.7 %multiply_reduce_fusion.3 = (f32[1280]{0:T(1024)S(1)}, f32[512]{0:T(512)S(1)}, f32[512]{0:T(512)S(1)}, f32[512]{0:T(512)S(1)}, f32[1280]{0:T(1024)S(1)}, /*index=5*/f32[512,1280]{1,0:T(8,128)}) fusion(f32[512,1280]{1,0:T(8,128)} %copy-done.9, f32[512]{0:T(512)S(1)} %add_rsqrt_fusion.1, f32[512]{0:T(512)S(1)} %broadcast_multiply_fusion.5, ...), kind=kOutput, calls=%fused_computation.52 | convolution fusion | flops 3363958784 | bytes 15754240 | tf_op jit(solution)/shard_map/dot_general | solution.py:41
  460.1 15.0 %shard_map.222 = (bf16[2048,512]{1,0:T(8,128)(2,1)}, bf16[2048,512]{1,0:T(8,128)(2,1)}, bf16[2048,512]{1,0:T(8,128)(2,1)}) custom-call(bf16[2048,512]{1,0:T(8,128)(2,1)} %copy-done.63, bf16[2048,1024]{1,0:T(8,128)(2,1)} %get-tuple-element.65.refs_1_.refs_2_, bf16[2048,1024]{1,0:T(8,128)(2,1)} %get-tuple-element.65.refs_1_.refs_2_, ...), custom_call_target="tpu_custom_call" | custom-call | flops 10737418240 | bytes 5242880 | tf_op jit(solution)/shard_map/pallas_call | solution.py:84
  475.0 16.1 %shard_map.223 = (bf16[2048,512]{1,0:T(8,128)(2,1)}, bf16[2048,512]{1,0:T(8,128)(2,1)}, bf16[2048,512]{1,0:T(8,128)(2,1)}) custom-call(bf16[2048,512]{1,0:T(8,128)(2,1)} %copy-done.63, bf16[2048,1024]{1,0:T(8,128)(2,1)} %get-tuple-element.65.refs_1_.refs_2_, ...), custom_call_target="tpu_custom_call", output_to_operand_aliasing={{0}: (5, {}), {1}: (6, {}), {2}: (7, {})} | custom-call | flops 10737418240 | bytes 5242880 | tf_op jit(solution)/shard_map/pallas_call | solution.py:84
  507.3 26.8 %collective-permute-done.50 = bf16[2,160,1280]{2,1,0:T(8,128)(2,1)S(1)} collective-permute-done((bf16[2,160,1280]{2,1,0:T(8,128)(2,1)S(1)}, bf16[2,160,1280]{2,1,0:T(8,128)(2,1)S(1)}, u32[]{:S(2)}, u32[]{:S(2)}) %collective-permute-start.50) | collective-permute-done | bytes 819232 | tf_op jit(solution)/shard_map/reduce_down_proj/ppermute | solution.py:31
  534.4 15.8 %shard_map.224 = (bf16[2048,512]{1,0:T(8,128)(2,1)}, bf16[2048,512]{1,0:T(8,128)(2,1)}, bf16[2048,512]{1,0:T(8,128)(2,1)}) custom-call(bf16[2048,512]{1,0:T(8,128)(2,1)} %copy-done.63, bf16[2048,1024]{1,0:T(8,128)(2,1)} %get-tuple-element.65.refs_1_.refs_2_, ...), custom_call_target="tpu_custom_call", output_to_operand_aliasing={{0}: (5, {}), {1}: (6, {}), {2}: (7, {})} | custom-call | flops 10737418240 | bytes 5242880 | tf_op jit(solution)/shard_map/pallas_call | solution.py:84
  554.8 16.1 %shard_map.225 = (bf16[2048,512]{1,0:T(8,128)(2,1)}, bf16[2048,512]{1,0:T(8,128)(2,1)}, bf16[2048,512]{1,0:T(8,128)(2,1)}) custom-call(bf16[2048,512]{1,0:T(8,128)(2,1)} %copy-done.63, bf16[2048,1024]{1,0:T(8,128)(2,1)} %get-tuple-element.65.refs_1_.refs_2_, ...), custom_call_target="tpu_custom_call", output_to_operand_aliasing={{0}: (5, {}), {1}: (6, {}), {2}: (7, {})} | custom-call | flops 10737418240 | bytes 5242880 | tf_op jit(solution)/shard_map/pallas_call | solution.py:84
  634.0 12.6 %collective-permute-done.74 = f32[13,1280]{1,0:T(8,128)S(1)} collective-permute-done((f32[13,1280]{1,0:T(8,128)S(1)}, f32[13,1280]{1,0:T(8,128)S(1)}, u32[]{:S(2)}, u32[]{:S(2)}) %collective-permute-start.74) | collective-permute-done | bytes 66592 | tf_op jit(solution)/shard_map/small_sums/ppermute | solution.py:31
  664.7 28.5 %collective-permute-done.63 = bf16[2,200,1280]{2,1,0:T(8,128)(2,1)} collective-permute-done((bf16[2,200,1280]{2,1,0:T(8,128)(2,1)}, bf16[2,200,1280]{2,1,0:T(8,128)(2,1)}, u32[]{:S(2)}, u32[]{:S(2)}) %collective-permute-start.63) | collective-permute-done | bytes 1024032 | tf_op jit(solution)/shard_map/reduce_up_proj/ppermute | solution.py:31
  708.3 9.4 %collective-permute-done.58 = bf16[40,1280]{1,0:T(8,128)(2,1)S(1)} collective-permute-done((bf16[40,1280]{1,0:T(8,128)(2,1)S(1)}, bf16[40,1280]{1,0:T(8,128)(2,1)S(1)}, u32[]{:S(2)}, u32[]{:S(2)}) %collective-permute-start.58) | collective-permute-done | bytes 102432 | tf_op jit(solution)/shard_map/reduce_in_proj/ppermute | solution.py:790
  738.4 9.3 %collective-permute-start.62 = (bf16[1,2,3,40,1280]{4,3,1,0,2:T(8,128)(2,1)S(1)}, bf16[1,2,3,40,1280]{4,3,1,0,2:T(8,128)(2,1)S(1)}, u32[]{:S(2)}, u32[]{:S(2)}) collective-permute-start(bf16[1,2,3,40,1280]{4,3,1,0,2:T(8,128)(2,1)S(1)} %maximum_select_fusion.14), channel_id=1, source_target_pairs={{0,8},{8,0},{16,24},{24,16},{1,9},{9,1},{17,25},{25,17},{2,10},{10... | collective-permute-start | bytes 1843208 | tf_op jit(solution)/shard_map/reduce_in_proj/ppermute | solution.py:31
  (546 shorter events, 422.7 us)
Async XLA Ops:
  0.7 70.3 %collective-permute-start = (bf16[512,1280]{1,0:T(8,128)(2,1)}, bf16[512,1280]{1,0:T(8,128)(2,1)}, u32[]{:S(2)}, u32[]{:S(2)}) collective-permute-start(bf16[512,1280]{1,0:T(8,128)(2,1)} %refs_0_.1), channel_id=1, source_target_pairs={{0,1},{1,0},{2,3},{3,2},{4,5},{5,4},{6,7},{7,6},{8,9},{9,8},{10,11... | collective-permute-start | bytes 3932168 | tf_op jit(solution)/shard_map/gather_tokens/ppermute | solution.py:31
  0.7 73.5 %collective-permute-start.2 = (bf16[512,1280]{1,0:T(8,128)(2,1)}, bf16[512,1280]{1,0:T(8,128)(2,1)S(1)}, u32[]{:S(2)}, u32[]{:S(2)}) collective-permute-start(bf16[512,1280]{1,0:T(8,128)(2,1)} %refs_0_.1), channel_id=1, source_target_pairs={{0,2},{1,3},{2,0},{3,1},{4,6},{5,7},{6,4},{7,5},{8,10},{9,11},{10,... | collective-permute-start | bytes 3932168 | tf_op jit(solution)/shard_map/gather_tokens/ppermute | solution.py:31
  73.0 63.5 %collective-permute-start.1 = (bf16[512,640]{1,0:T(8,128)(2,1)}, bf16[512,640]{1,0:T(8,128)(2,1)}, u32[]{:S(2)}, u32[]{:S(2)}) collective-permute-start(bf16[512,640]{1,0:T(8,128)(2,1)} %slice.254), channel_id=1, source_target_pairs={{0,2},{1,3},{2,0},{3,1},{4,6},{5,7},{6,4},{7,5},{8,10},{9,11},{10,... | collective-permute-start | bytes 1966088 | tf_op jit(solution)/shard_map/gather_tokens/ppermute | solution.py:31
  75.2 62.4 %collective-permute-start.3 = (bf16[512,640]{1,0:T(8,128)(2,1)}, bf16[512,640]{1,0:T(8,128)(2,1)}, u32[]{:S(2)}, u32[]{:S(2)}) collective-permute-start(bf16[512,640]{1,0:T(8,128)(2,1)} %slice.255), channel_id=1, source_target_pairs={{0,1},{1,0},{2,3},{3,2},{4,5},{5,4},{6,7},{7,6},{8,9},{9,8},{10,11... | collective-permute-start | bytes 1966088 | tf_op jit(solution)/shard_map/gather_tokens/ppermute | solution.py:31
  175.3 74.2 %collective-permute-start.25 = (bf16[640,1280]{1,0:T(8,128)(2,1)S(1)}, bf16[640,1280]{1,0:T(8,128)(2,1)}, u32[]{:S(2)}, u32[]{:S(2)}) collective-permute-start(bf16[640,1280]{1,0:T(8,128)(2,1)S(1)} %pad_maximum_fusion.4.refs_1_), channel_id=1, source_target_pairs={{0,16},{8,24},{16,0},{24,8},{1,17},{9,25},{17,1},{25,9},{2,18},{10... | collective-permute-start | bytes 4915208 | tf_op jit(solution)/shard_map/gather_up_proj/ppermute | solution.py:31
  177.2 72.6 %collective-permute-start.26 = (bf16[640,1280]{1,0:T(8,128)(2,1)}, bf16[640,1280]{1,0:T(8,128)(2,1)}, u32[]{:S(2)}, u32[]{:S(2)}) collective-permute-start(bf16[640,1280]{1,0:T(8,128)(2,1)} %pad_maximum_fusion.5.refs_3_), channel_id=1, source_target_pairs={{0,1},{1,0},{2,3},{3,2},{4,5},{5,4},{6,7},{7,6},{8,9},{9,8},{10,11... | collective-permute-start | bytes 4915208 | tf_op jit(solution)/shard_map/gather_up_proj/ppermute | solution.py:31
  193.7 69.6 %collective-permute-start.18 = (bf16[4,2,2,1,40,1280]{5,4,0,1,3,2:T(8,128)(2,1)S(1)}, bf16[4,2,2,1,40,1280]{5,4,0,1,3,2:T(8,128)(2,1)}, u32[]{:S(2)}, u32[]{:S(2)}) collective-permute-start(bf16[4,2,2,1,40,1280]{5,4,0,1,3,2:T(8,128)(2,1)S(1)} %maximum_select_fusion.5), channel_id=1, source_target_pairs={{0,8},{8,0},{16,24},{24,16},{1,9},{9,1},{17,25},{25,17},{2,10},{10... | collective-permute-start | bytes 4915208 | tf_op jit(solution)/shard_map/gather_out_proj/ppermute | solution.py:31
  235.6 43.0 %collective-permute-start.23 = (bf16[512,320]{1,0:T(8,128)(2,1)S(1)}, bf16[512,320]{1,0:T(8,128)(2,1)S(1)}, u32[]{:S(2)}, u32[]{:S(2)}) collective-permute-start(bf16[512,320]{1,0:T(8,128)(2,1)S(1)} %copy-done.59), channel_id=1, source_target_pairs={{0,3},{1,2},{2,1},{3,0},{4,7},{5,6},{6,5},{7,4},{8,11},{9,10},{10,... | collective-permute-start | bytes 983048 | tf_op jit(solution)/shard_map/context_back/ppermute | solution.py:31
  249.8 60.5 %collective-permute-start.28 = (bf16[640,1280]{1,0:T(8,128)(2,1)S(1)}, bf16[640,1280]{1,0:T(8,128)(2,1)}, u32[]{:S(2)}, u32[]{:S(2)}) collective-permute-start(bf16[640,1280]{1,0:T(8,128)(2,1)S(1)} %pad_maximum_fusion.6.refs_1_), channel_id=1, source_target_pairs={{0,16},{8,24},{16,0},{24,8},{1,17},{9,25},{17,1},{25,9},{2,18},{10... | collective-permute-start | bytes 4915208 | tf_op jit(solution)/shard_map/gather_down_proj/ppermute | solution.py:31
  263.4 46.9 %collective-permute-start.30 = (bf16[640,1280]{1,0:T(8,128)(2,1)}, bf16[640,1280]{1,0:T(8,128)(2,1)}, u32[]{:S(2)}, u32[]{:S(2)}) collective-permute-start(bf16[640,1280]{1,0:T(8,128)(2,1)} %pad_maximum_fusion.7.refs_3_), channel_id=1, source_target_pairs={{0,1},{1,0},{2,3},{3,2},{4,5},{5,4},{6,7},{7,6},{8,9},{9,8},{10,11... | collective-permute-start | bytes 4915208 | tf_op jit(solution)/shard_map/gather_down_proj/ppermute | solution.py:31
  365.7 55.5 %collective-permute-start.37 = (bf16[4,2,80,1280]{3,2,0,1:T(8,128)(2,1)}, bf16[4,2,80,1280]{3,2,0,1:T(8,128)(2,1)}, u32[]{:S(2)}, u32[]{:S(2)}) collective-permute-start(bf16[4,2,80,1280]{3,2,0,1:T(8,128)(2,1)} %bitcast.299), channel_id=1, source_target_pairs={{0,16},{8,24},{16,0},{24,8},{1,17},{9,25},{17,1},{25,9},{2,18},{10... | collective-permute-start | bytes 4915208 | tf_op jit(solution)/shard_map/reduce_down_proj/ppermute | solution.py:31
  368.8 57.1 %collective-permute-start.38 = (bf16[4,2,80,1280]{3,2,0,1:T(8,128)(2,1)}, bf16[4,2,80,1280]{3,2,0,1:T(8,128)(2,1)}, u32[]{:S(2)}, u32[]{:S(2)}) collective-permute-start(bf16[4,2,80,1280]{3,2,0,1:T(8,128)(2,1)} %bitcast.298), channel_id=1, source_target_pairs={{0,1},{1,0},{2,3},{3,2},{4,5},{5,4},{6,7},{7,6},{8,9},{9,8},{10,11... | collective-permute-start | bytes 4915208 | tf_op jit(solution)/shard_map/reduce_down_proj/ppermute | solution.py:31
  380.9 57.1 %collective-permute-start.39 = (bf16[4,2,80,1280]{3,2,0,1:T(8,128)(2,1)}, bf16[4,2,80,1280]{3,2,0,1:T(8,128)(2,1)}, u32[]{:S(2)}, u32[]{:S(2)}) collective-permute-start(bf16[4,2,80,1280]{3,2,0,1:T(8,128)(2,1)} %bitcast.297), channel_id=1, source_target_pairs={{0,16},{8,24},{16,0},{24,8},{1,17},{9,25},{17,1},{25,9},{2,18},{10... | collective-permute-start | bytes 4915208 | tf_op jit(solution)/shard_map/reduce_up_proj/ppermute | solution.py:31
  385.2 64.1 %collective-permute-start.40 = (bf16[4,2,80,1280]{3,2,0,1:T(8,128)(2,1)}, bf16[4,2,80,1280]{3,2,0,1:T(8,128)(2,1)}, u32[]{:S(2)}, u32[]{:S(2)}) collective-permute-start(bf16[4,2,80,1280]{3,2,0,1:T(8,128)(2,1)} %bitcast.296), channel_id=1, source_target_pairs={{0,1},{1,0},{2,3},{3,2},{4,5},{5,4},{6,7},{7,6},{8,9},{9,8},{10,11... | collective-permute-start | bytes 4915208 | tf_op jit(solution)/shard_map/reduce_up_proj/ppermute | solution.py:31
  410.5 43.5 %collective-permute-start.36 = (bf16[512,320]{1,0:T(8,128)(2,1)S(1)}, bf16[512,320]{1,0:T(8,128)(2,1)S(1)}, u32[]{:S(2)}, u32[]{:S(2)}) collective-permute-start(bf16[512,320]{1,0:T(8,128)(2,1)S(1)} %get-tuple-element.148), channel_id=1, source_target_pairs={{0,3},{1,2},{2,1},{3,0},{4,7},{5,6},{6,5},{7,4},{8,11},{9,10},{10,... | collective-permute-start | bytes 983048 | tf_op jit(solution)/shard_map/grad_context_to_heads/ppermute | solution.py:31
  438.0 64.8 %collective-permute-start.41 = (bf16[4,2,2,40,1280]{4,3,0,1,2:T(8,128)(2,1)}, bf16[4,2,2,40,1280]{4,3,0,1,2:T(8,128)(2,1)}, u32[]{:S(2)}, u32[]{:S(2)}) collective-permute-start(bf16[4,2,2,40,1280]{4,3,0,1,2:T(8,128)(2,1)} %bitcast.300), channel_id=1, source_target_pairs={{0,8},{8,0},{16,24},{24,16},{1,9},{9,1},{17,25},{25,17},{2,10},{10... | collective-permute-start | bytes 4915208 | tf_op jit(solution)/shard_map/reduce_up_proj/ppermute | solution.py:31
  449.2 44.5 %collective-permute-start.43 = (bf16[4,80,1280]{2,1,0:T(8,128)(2,1)}, bf16[4,80,1280]{2,1,0:T(8,128)(2,1)}, u32[]{:S(2)}, u32[]{:S(2)}) collective-permute-start(bf16[4,80,1280]{2,1,0:T(8,128)(2,1)} %dynamic-slice_bitcast_fusion.6), channel_id=1, source_target_pairs={{0,16},{8,24},{16,0},{24,8},{1,17},{9,25},{17,1},{25,9},{2,18},{10... | collective-permute-start | bytes 2457608 | tf_op jit(solution)/shard_map/reduce_down_proj/ppermute | solution.py:31
  455.3 43.1 %collective-permute-start.46 = (bf16[4,80,1280]{2,1,0:T(8,128)(2,1)}, bf16[4,80,1280]{2,1,0:T(8,128)(2,1)}, u32[]{:S(2)}, u32[]{:S(2)}) collective-permute-start(bf16[4,80,1280]{2,1,0:T(8,128)(2,1)} %dynamic-slice_bitcast_fusion.3), channel_id=1, source_target_pairs={{0,16},{8,24},{16,0},{24,8},{1,17},{9,25},{17,1},{25,9},{2,18},{10... | collective-permute-start | bytes 2457608 | tf_op jit(solution)/shard_map/reduce_up_proj/ppermute | solution.py:31
  457.6 43.0 %collective-permute-start.45 = (bf16[4,80,1280]{2,1,0:T(8,128)(2,1)}, bf16[4,80,1280]{2,1,0:T(8,128)(2,1)}, u32[]{:S(2)}, u32[]{:S(2)}) collective-permute-start(bf16[4,80,1280]{2,1,0:T(8,128)(2,1)} %dynamic-slice_bitcast_fusion.4), channel_id=1, source_target_pairs={{0,1},{1,0},{2,3},{3,2},{4,5},{5,4},{6,7},{7,6},{8,9},{9,8},{10,11... | collective-permute-start | bytes 2457608 | tf_op jit(solution)/shard_map/reduce_up_proj/ppermute | solution.py:31
  506.0 45.7 %collective-permute-start.44 = (bf16[4,2,40,1280]{3,2,0,1:T(8,128)(2,1)S(1)}, bf16[4,2,40,1280]{3,2,0,1:T(8,128)(2,1)}, u32[]{:S(2)}, u32[]{:S(2)}) collective-permute-start(bf16[4,2,40,1280]{3,2,0,1:T(8,128)(2,1)S(1)} %dynamic-slice_bitcast_fusion.5), channel_id=1, source_target_pairs={{0,16},{8,24},{16,0},{24,8},{1,17},{9,25},{17,1},{25,9},{2,18},{10... | collective-permute-start | bytes 2457608 | tf_op jit(solution)/shard_map/reduce_up_proj/ppermute | solution.py:31
  550.4 74.8 %collective-permute-start.68 = (bf16[1,80,2560]{2,1,0:T(8,128)(2,1)S(1)}, bf16[1,80,2560]{2,1,0:T(8,128)(2,1)}, u32[]{:S(2)}, u32[]{:S(2)}) collective-permute-start(bf16[1,80,2560]{2,1,0:T(8,128)(2,1)S(1)} %maximum_bitcast_fusion.6), channel_id=1, source_target_pairs={{0,16},{8,24},{16,0},{24,8},{1,17},{9,25},{17,1},{25,9},{2,18},{10... | collective-permute-start | bytes 1228808 | tf_op jit(solution)/shard_map/reduce_down_proj/ppermute | solution.py:31
  646.5 46.7 %collective-permute-start.63 = (bf16[2,200,1280]{2,1,0:T(8,128)(2,1)}, bf16[2,200,1280]{2,1,0:T(8,128)(2,1)}, u32[]{:S(2)}, u32[]{:S(2)}) collective-permute-start(bf16[2,200,1280]{2,1,0:T(8,128)(2,1)} %dynamic-slice_bitcast_fusion.1), channel_id=1, source_target_pairs={{0,4},{1,5},{2,6},{3,7},{4,0},{5,1},{6,2},{7,3},{8,12},{9,13},{10,... | collective-permute-start | bytes 3072008 | tf_op jit(solution)/shard_map/reduce_up_proj/ppermute | solution.py:31
  655.1 92.6 %collective-permute-start.52 = (bf16[512,1280]{1,0:T(8,128)(2,1)}, bf16[512,1280]{1,0:T(8,128)(2,1)S(1)}, u32[]{:S(2)}, u32[]{:S(2)}) collective-permute-start(bf16[512,1280]{1,0:T(8,128)(2,1)} %pad_maximum_fusion.13), channel_id=1, source_target_pairs={{0,2},{1,3},{2,0},{3,1},{4,6},{5,7},{6,4},{7,5},{8,10},{9,11},{10,... | collective-permute-start | bytes 3932168 | tf_op jit(solution)/shard_map/reduce_tokens/ppermute | solution.py:31
  660.6 87.1 %collective-permute-start.49 = (bf16[512,1280]{1,0:T(8,128)(2,1)}, bf16[512,1280]{1,0:T(8,128)(2,1)S(1)}, u32[]{:S(2)}, u32[]{:S(2)}) collective-permute-start(bf16[512,1280]{1,0:T(8,128)(2,1)} %pad_maximum_fusion.12), channel_id=1, source_target_pairs={{0,1},{1,0},{2,3},{3,2},{4,5},{5,4},{6,7},{7,6},{8,9},{9,8},{10,11... | collective-permute-start | bytes 3932168 | tf_op jit(solution)/shard_map/reduce_tokens/ppermute | solution.py:31
  (141 other events, 2472.4 us)

commit v3 on v2

v3 whole, which is shorter than its diff:
```python
import functools
import math

import jax
import jax.numpy as jnp
from jax import lax
from jax.experimental import pallas as pl
from jax.experimental.pallas import tpu as pltpu
from jax.sharding import PartitionSpec as P

H = 16
HD = 80
CLIP_DEV = 4
LANES = 128
GROUP_HEADS = H // CLIP_DEV
EPSILON = 1e-05
SCORE_SCALE = HD ** (-0.5) * math.log2(math.e)
LN2 = math.log(2.0)
LOW = jnp.bfloat16
TOKEN_BLOCK = 256
QUERY_BLOCK = 512
GRAD_BLOCK = 512
UNIT_BLOCK = 1280
GROUP_LANES = GROUP_HEADS * LANES
GROUP_WIDTH = GROUP_HEADS * HD
VMEM_BYTES = 56 * 1024 * 1024


def swap(value, axis, mask):
    pairs = [(source, source ^ mask) for source in range(lax.axis_size(axis))]
    return lax.ppermute(value, axis, pairs)


def swap_by_core(value, first, second):
    fsdp = lax.axis_size("fsdp")
    pairs = []
    for dp in range(lax.axis_size("dp")):
        axis, mask = second if dp % 2 else first
        for index in range(fsdp):
            target = (dp ^ mask) * fsdp + index if axis == "dp" else dp * fsdp + (index ^ mask)
            pairs.append((dp * fsdp + index, target))
    return lax.ppermute(value, ("dp", "fsdp"), pairs)


def dot_nt(lhs, rhs):
    return lax.dot_general(
        lhs, rhs, (((1,), (1,)), ((), ())), preferred_element_type=jnp.float32
    )


def dot_nn(lhs, rhs):
    return jnp.dot(lhs, rhs, preferred_element_type=jnp.float32)


def dot_tn(lhs, rhs):
    return lax.dot_general(
        lhs, rhs, (((0,), (0,)), ((), ())), preferred_element_type=jnp.float32
    )


def split_three(value):
    high = value.astype(LOW).astype(jnp.float32)
    rest = value - high
    middle = rest.astype(LOW).astype(jnp.float32)
    return high, middle, rest - middle


def with_lanes(block, first, columns):
    lane = lax.broadcasted_iota(jnp.int32, block.shape, 1)
    for place, column in enumerate(columns):
        block = jnp.where(lane == first + place, column, block)
    return block


def divisor(size, most):
    block = min(size, most)
    while size % block:
        block //= 2
    return block


ANYWHERE = pl.BlockSpec(memory_space=pl.ANY)


def call(body, grid, scalars, inputs, outputs, held=None, scratch=(), cost=(0, 0, 0), after=()):
    held = () if held is None else tuple(held)
    passive = held + tuple(after)
    n_scalar, n_in, n_passive, n_out = len(scalars), len(inputs), len(passive), len(outputs)

    def kernel(*refs):
        first = n_scalar + n_in
        body(*refs[:first], *refs[first + n_passive :])

    flops, moved, special = cost
    return pl.pallas_call(
        kernel,
        grid_spec=pltpu.PrefetchScalarGridSpec(
            num_scalar_prefetch=n_scalar,
            grid=grid,
            in_specs=[spec for _, spec in inputs] + [ANYWHERE] * n_passive,
            out_specs=[spec for _, spec in outputs],
            scratch_shapes=list(scratch),
        ),
        out_shape=[shape for shape, _ in outputs],
        input_output_aliases={n_scalar + n_in + i: i for i in range(len(held))},
        compiler_params=pltpu.CompilerParams(vmem_limit_bytes=VMEM_BYTES),
        cost_estimate=pl.CostEstimate(flops=int(flops), bytes_accessed=int(moved), transcendentals=int(special)),
    )(*scalars, *(array for array, _ in inputs), *passive)


def like(rows, columns, kind=LOW):
    return jax.ShapeDtypeStruct((rows, columns), kind)


def whole_block(array):
    return pl.BlockSpec(array.shape, lambda *_: (0,) * len(array.shape))


def fence(token, reads, *arrays):
    def body(*refs):
        pass

    carried = (token, *arrays)
    return pl.pallas_call(
        body,
        in_specs=[ANYWHERE] * (len(carried) + len(reads)),
        out_specs=[ANYWHERE] * len(carried),
        out_shape=[jax.ShapeDtypeStruct(array.shape, array.dtype) for array in carried],
        input_output_aliases={i: i for i in range(len(carried))},
        cost_estimate=pl.CostEstimate(flops=0, bytes_accessed=0, transcendentals=0),
    )(*carried, *reads)


def unit_rows_of(values):
    center = values - jnp.mean(values, axis=-1, keepdims=True)
    spread = jnp.mean(center * center, axis=-1, keepdims=True)
    return center * lax.rsqrt(spread + EPSILON)


def project_kernel(limit_ref, x_ref, weight_ref, gain_ref, shift_ref, column_ref, query_ref, pair_ref, normed_ref):
    rows = x_ref.shape[0]
    unit = unit_rows_of(x_ref[...].astype(jnp.float32))
    normed = (unit * gain_ref[...] + shift_ref[...]).astype(LOW)
    normed_ref[...] = normed
    columns = column_ref[...]
    queries = dot_nt(normed, weight_ref[:GROUP_LANES, :])
    query_ref[...] = (queries * SCORE_SCALE + columns[:, :GROUP_LANES]).astype(LOW)
    pair = dot_nt(normed, weight_ref[GROUP_LANES:, :]) + columns[:, GROUP_LANES:]
    row = pl.program_id(0) * rows + lax.broadcasted_iota(jnp.int32, pair.shape, 0)
    lane = lax.broadcasted_iota(jnp.int32, pair.shape, 1)
    masked = (row >= limit_ref[0]) & (lane % LANES == HD) & (lane < GROUP_LANES)
    pair_ref[...] = jnp.where(masked, -1e30, pair).astype(LOW)


def project(number, x_block, weight, gain, shift, columns, limit, held, after=()):
    tokens, width = x_block.shape
    block = divisor(tokens, TOKEN_BLOCK)
    steps = tokens // block
    rows = CLIP_DEV * tokens

    def out(columns_out):
        return like(rows, columns_out), pl.BlockSpec((block, columns_out), lambda i, _: (number * steps + i, 0))

    return call(
        project_kernel,
        (steps,),
        (limit,),
        [(x_block, pl.BlockSpec((block, width), lambda i, _: (i, 0)))]
        + [(array, whole_block(array)) for array in (weight, gain, shift, columns)],
        [out(GROUP_LANES), out(2 * GROUP_LANES), out(width)],
        held,
        cost=(0, 0, 0),
        after=after,
    )


def attend_kernel(query_ref, pair_ref, context_ref, ready_ref):
    contexts = []
    for head in range(GROUP_HEADS):
        lanes = slice(head * LANES, (head + 1) * LANES)
        queries = query_ref[:, lanes]
        scores = dot_nt(queries, pair_ref[:, lanes])
        largest = jnp.max(scores, axis=1, keepdims=True)
        exponent = jnp.exp2(scores - largest)
        values = pair_ref[:, GROUP_LANES + head * LANES : GROUP_LANES + (head + 1) * LANES]
        mixed = dot_nn(exponent.astype(LOW), values)
        summed = mixed[:, HD : HD + 1]
        contexts.append((mixed / summed)[:, :HD])
        log_parts = split_three(-(largest + jnp.log2(summed)))
        ready_ref[:, lanes] = with_lanes(queries.astype(jnp.float32), HD + 1, log_parts).astype(LOW)
    context_ref[...] = jnp.concatenate(contexts, axis=1).astype(LOW)


def attend(number, queries, pair, after=()):
    rows = queries.shape[0]
    tokens = rows // CLIP_DEV
    block = divisor(tokens, QUERY_BLOCK)
    steps = tokens // block
    spot = pl.BlockSpec((block, GROUP_LANES), lambda i: (number * steps + i, 0))
    context, ready = call(
        attend_kernel,
        (steps,),
        (),
        [(queries, spot), (pair, whole_block(pair))],
        [
            (like(tokens, GROUP_WIDTH), pl.BlockSpec((block, GROUP_WIDTH), lambda i: (i, 0))),
            (like(tokens, GROUP_LANES), pl.BlockSpec((block, GROUP_LANES), lambda i: (i, 0))),
        ],
        cost=(0, 0, 0),
        after=after,
    )
    return context, ready


def attend_back_kernel(
    head,
    query_ref,
    key_ref,
    value_ref,
    context_ref,
    grad_ref,
    grad_query_ref,
    grad_key_ref,
    grad_value_ref,
    key_turned,
    key_total,
    value_total,
):
    step = pl.program_id(0)

    @pl.when(step == 0)
    def _():
        key_turned[...] = key_ref[...].T
        key_total[...] = jnp.zeros_like(key_total)
        value_total[...] = jnp.zeros_like(value_total)

    lanes = slice(head * HD, (head + 1) * HD)
    queries = query_ref[...]
    grad = grad_ref[:, lanes].astype(jnp.float32)
    row_term = jnp.sum(grad * context_ref[:, lanes].astype(jnp.float32), axis=1, keepdims=True)
    grad = jnp.concatenate([grad, jnp.zeros((grad.shape[0], LANES - HD), jnp.float32)], axis=1)
    grad = with_lanes(grad, HD, split_three(-row_term)).astype(LOW)
    soft = jnp.exp2(dot_nt(key_ref[...], queries))
    grad_soft = dot_nt(value_ref[...], grad)
    value_total[...] += dot_nn(soft.astype(LOW), grad)
    grad_scores = (soft * grad_soft).astype(LOW)
    key_total[...] += dot_nn(grad_scores, queries)
    grad_query = dot_nn(key_turned[...], grad_scores)
    grad_query_ref[...] = (grad_query * HD ** (-0.5)).T.astype(LOW)

    @pl.when(step == pl.num_programs(0) - 1)
    def _():
        grad_key_ref[...] = (key_total[...] * LN2).astype(LOW)
        grad_value_ref[...] = value_total[...].astype(LOW)


def attend_back(head, queries, pair, context, grad_context, held, after=()):
    rows = queries.shape[0]
    block = divisor(rows, GRAD_BLOCK)
    part = pl.BlockSpec((block, LANES), lambda i: (i, head))
    compact = pl.BlockSpec((block, GROUP_WIDTH), lambda i: (i, 0))
    out = like(rows, GROUP_LANES)
    whole = pl.BlockSpec((rows, LANES), lambda i: (0, head))
    return call(
        functools.partial(attend_back_kernel, head),
        (rows // block,),
        (),
        [
            (queries, part),
            (pair, whole),
            (pair, pl.BlockSpec((rows, LANES), lambda i: (0, GROUP_HEADS + head))),
            (context, compact),
            (grad_context, compact),
        ],
        [(out, part), (out, whole), (out, whole)],
        held,
        scratch=[
            pltpu.VMEM((LANES, rows), LOW),
            pltpu.VMEM((rows, LANES), jnp.float32),
            pltpu.VMEM((rows, LANES), jnp.float32),
        ],
        cost=(0, 0, 0),
        after=after,
    )


def entry_back_kernel(x_ref, query_ref, key_ref, value_ref, weight_ref, partial_ref, sums_ref):
    partial = dot_nn(query_ref[...], weight_ref[:GROUP_LANES, :])
    partial += dot_nn(key_ref[...], weight_ref[GROUP_LANES : 2 * GROUP_LANES, :])
    partial += dot_nn(value_ref[...], weight_ref[2 * GROUP_LANES :, :])
    partial_ref[...] = partial.astype(LOW)
    unit = unit_rows_of(x_ref[...].astype(jnp.float32))

    @pl.when(pl.program_id(0) == 0)
    def _():
        sums_ref[...] = jnp.zeros_like(sums_ref)

    sums_ref[0:1, :] += jnp.sum(partial * unit, axis=0, keepdims=True)
    sums_ref[1:2, :] += jnp.sum(partial, axis=0, keepdims=True)


def entry_back(number, x_block, grads, weight, after=()):
    tokens, width = x_block.shape
    block = divisor(tokens, TOKEN_BLOCK)
    steps = tokens // block
    spot = pl.BlockSpec((block, width), lambda i: (i, 0))
    return call(
        entry_back_kernel,
        (steps,),
        (),
        [(x_block, spot)]
        + [(grad, pl.BlockSpec((block, GROUP_LANES), lambda i: (number * steps + i, 0))) for grad in grads]
        + [(weight, whole_block(weight))],
        [(like(tokens, width), spot), (like(8, width, jnp.float32), pl.BlockSpec((8, width), lambda i: (0, 0)))],
        cost=(2 * tokens * weight.size, tokens * width * 8 + weight.size * 2, tokens),
        after=after,
    )


def widen_kernel(normed_ref, weight_ref, bias_ref, activated_ref, slope_ref):
    widened = dot_nt(normed_ref[...], weight_ref[...]) + bias_ref[...]
    below = 0.5 + 0.5 * lax.erf(widened * math.sqrt(0.5))
    activated_ref[...] = (widened * below).astype(LOW)
    density = jnp.exp2(widened * widened * (-0.5 * math.log2(math.e))) * (1.0 / math.sqrt(2.0 * math.pi))
    slope_ref[...] = (below + widened * density).astype(LOW)


def widen(number, normed, weight, bias, held, after=()):
    tokens, width = normed.shape
    units = weight.shape[0]
    block = divisor(units, UNIT_BLOCK)
    spot = pl.BlockSpec((tokens, block), lambda i: (number, i))
    out = like(2 * tokens, units)
    return call(
        widen_kernel,
        (units // block,),
        (),
        [
            (normed, whole_block(normed)),
            (weight, pl.BlockSpec((block, width), lambda i: (i, 0))),
            (bias.reshape(1, units), pl.BlockSpec((1, block), lambda i: (0, i))),
        ],
        [(out, spot), (out, spot)],
        held,
        cost=(0, 0, 0),
        after=after,
    )


def split_columns(piece, core, shards):
    rows, columns = piece.shape
    span = columns // shards // 2

    def body(core_ref, piece_ref, out_ref):
        for shard in range(shards):
            low = piece_ref[:, 2 * shard * span : (2 * shard + 1) * span]
            high = piece_ref[:, (2 * shard + 1) * span : (2 * shard + 2) * span]
            out_ref[:, shard * span : (shard + 1) * span] = jnp.where(core_ref[0] == 0, low, high)

    spec = pl.BlockSpec((rows, columns // 2), lambda *_: (0, 0))
    return call(body, (1,), (core.reshape(1),), [(piece, whole_block(piece))], [(like(rows, columns // 2), spec)])[0]


def merge_columns(mine, other, core, shards):
    rows, columns = mine.shape
    span = columns // shards

    def body(core_ref, mine_ref, other_ref, out_ref):
        for shard in range(shards):
            a = mine_ref[:, shard * span : (shard + 1) * span].astype(jnp.float32)
            b = other_ref[:, shard * span : (shard + 1) * span].astype(jnp.float32)
            first = core_ref[0] == 0
            out_ref[:, 2 * shard * span : (2 * shard + 1) * span] = jnp.where(first, a, b)
            out_ref[:, (2 * shard + 1) * span : (2 * shard + 2) * span] = jnp.where(first, b, a)

    spec = pl.BlockSpec((rows, 2 * columns), lambda *_: (0, 0))
    return call(
        body,
        (1,),
        (core.reshape(1),),
        [(mine, whole_block(mine)), (other, whole_block(other))],
        [(like(rows, 2 * columns, jnp.float32), spec)],
    )[0]


def normalise(values):
    center = values - jnp.mean(values, axis=-1, keepdims=True)
    spread = jnp.mean(center * center, axis=-1, keepdims=True)
    scale = lax.rsqrt(spread + EPSILON)
    return center * scale, scale


def norm_back(grad, gain, unit, scale):
    scaled = grad * gain
    return scale * (
        scaled
        - jnp.mean(scaled, axis=-1, keepdims=True)
        - unit * jnp.mean(scaled * unit, axis=-1, keepdims=True)
    )


def pick(blocks, index, axis=0):
    return lax.dynamic_index_in_dim(blocks, index, axis, keepdims=False)


def join_bit(held, came, place, mine):
    return jnp.where(
        mine == 1,
        jnp.concatenate([came, held], axis=place),
        jnp.concatenate([held, came], axis=place),
    )


def widen_bits(held, bits, first):
    for number, (axis, mask, mine) in enumerate(bits):
        held = join_bit(held, swap(held, axis, mask), first + number, mine)
    return held


def give(held, place, bit):
    axis, mask, mine = bit
    return swap(pick(held, 1 - mine, place), axis, mask)


def keep(held, came, place, bit):
    kept = pick(held, bit[2], place)
    return (kept.astype(jnp.float32) + came.astype(jnp.float32)).astype(LOW)


def reduce_bits(held, bits, place):
    for bit in bits:
        held = keep(held, give(held, place, bit), place, bit)
    return held


def reduce_last(held, bits):
    for place in reversed(range(len(bits))):
        held = keep(held, give(held, place, bits[place]), place, bits[place])
    return held


def gather_blocks(array, index):
    count = index.shape[0]

    def body(index_ref, source_ref, out_ref):
        for number in range(count):
            out_ref[number] = source_ref[index_ref[number]]

    shape = jax.ShapeDtypeStruct((count,) + array.shape[1:], array.dtype)
    return call(
        body,
        (1,),
        (index,),
        [(array, whole_block(array))],
        [(shape, whole_block(shape))],
        cost=(0, 0, 0),
    )[0]


def spread_heads(mine, other, core, index, rounds):
    copies, _, rows, width = mine.shape
    if rows % 8:
        blocks = jnp.stack([jnp.where(core == 0, mine, other), jnp.where(core == 0, other, mine)])
        picked = jnp.stack([pick(blocks, index[i], 2) for i in range(3 * rounds)])
        picked = picked.reshape(3 * GROUP_HEADS, HD, width)
        return jnp.pad(picked, ((0, 0), (0, LANES - HD), (0, 0))).reshape(3 * GROUP_LANES, width)

    def body(index_ref, mine_ref, other_ref, out_ref):
        for head in range(3 * GROUP_HEADS):
            out_ref[head * LANES + HD : (head + 1) * LANES, :] = jnp.zeros((LANES - HD, width), LOW)

        def fill(first, second):
            for unit in range(3 * rounds):
                slot = index_ref[unit]
                for part in range(2 * copies):
                    row = (2 * copies * unit + part) * rows
                    start = row // HD * LANES + row % HD
                    source = second if part // copies else first
                    out_ref[start : start + rows, :] = source[part % copies, slot]

        own = index_ref[3 * rounds]

        @pl.when(own == 0)
        def _():
            fill(mine_ref, other_ref)

        @pl.when(own == 1)
        def _():
            fill(other_ref, mine_ref)

    spec = pl.BlockSpec((3 * GROUP_LANES, width), lambda *_: (0, 0))
    return call(
        body,
        (1,),
        (jnp.concatenate([index, core.reshape(1)]),),
        [(mine, whole_block(mine)), (other, whole_block(other))],
        [(like(3 * GROUP_LANES, width), spec)],
        cost=(0, 0, 0),
    )[0]


def assemble_blocks(sources, targets, rows, width):
    each = len(targets) // len(sources)

    def body(start_ref, *refs):
        for number in range(len(targets)):
            place = number % each
            refs[-1][start_ref[number]] = refs[number // each][place * rows : (place + 1) * rows, :]

    shape = jax.ShapeDtypeStruct((len(targets), rows, width), LOW)
    return call(
        body,
        (1,),
        (jnp.stack(targets).astype(jnp.int32),),
        [(array, whole_block(array)) for array in sources],
        [(shape, whole_block(shape))],
        cost=(0, 0, 0),
    )[0]


def assemble(sources, targets, rows, shape, after=()):
    places = [(part, i) for part, source in enumerate(sources) for i in range(source.shape[0] // rows)]
    if rows % 16:
        out = jnp.zeros(shape, LOW)
        for (part, i), target in zip(places, targets, strict=True):
            out = lax.dynamic_update_slice(out, sources[part][i * rows : (i + 1) * rows], (target * rows, 0))
        return out

    def body(start_ref, *refs):
        for number, (part, i) in enumerate(places):
            start = pl.multiple_of(start_ref[number] * rows, 16)
            refs[-1][pl.ds(start, rows), :] = refs[part][i * rows : (i + 1) * rows, :]

    return call(
        body,
        (1,),
        (jnp.stack(targets).astype(jnp.int32),),
        [(array, whole_block(array)) for array in sources],
        [(like(*shape), pl.BlockSpec(shape, lambda *_: (0, 0)))],
        cost=(0, 0, 0),
        after=after,
    )[0]


def on_device(
    hidden_states,
    clip_lengths,
    norm_gains,
    norm_shifts,
    proj_biases,
    up_bias,
    in_proj,
    out_proj,
    up_proj,
    down_proj,
    cotangent,
):
    tokens_here, width = hidden_states.shape
    fsdp_count = lax.axis_size("fsdp")
    dp_count = lax.axis_size("dp")
    fsdp_index = lax.axis_index("fsdp")
    dp_index = lax.axis_index("dp")
    core = dp_index % 2
    copies = dp_count // 2
    copy_index = dp_index // 2
    region = (dp_index * fsdp_count + fsdp_index) // CLIP_DEV
    place = fsdp_index % CLIP_DEV
    length = lax.dynamic_index_in_dim(clip_lengths, region, keepdims=False)
    span = tokens_here * CLIP_DEV
    hidden_units = up_bias.shape[0]
    positions = jnp.arange(tokens_here, dtype=jnp.int32)
    row_valid = (place * tokens_here + positions < length).astype(jnp.float32)
    copy_levels = copies.bit_length() - 1
    fsdp_levels = fsdp_count.bit_length() - 1
    far_count = fsdp_count // 2
    half = width // 2

    core_bit = ("dp", 1, core)
    copy_bits = [("dp", 2 << level, copy_index >> level & 1) for level in reversed(range(copy_levels))]
    fsdp_bits = [("fsdp", 1 << level, fsdp_index >> level & 1) for level in reversed(range(fsdp_levels))]
    far_bits, near_bit = fsdp_bits[:-1], fsdp_bits[-1]
    lap_bits = fsdp_bits[:-2]
    orders = [[near_bit] + copy_bits, copy_bits + [near_bit]]
    stages = len(orders[0])
    token = jnp.zeros((8, LANES), jnp.float32)

    def by_core(first, second):
        return jnp.where(core == 0, first, second)

    def swap_stage(value, number):
        return swap_by_core(value, orders[0][number][:2], orders[1][number][:2])

    def own_bit(number):
        return by_core(orders[0][number][2], orders[1][number][2])

    def block_index(bits):
        indices = []
        for order in orders:
            near, copy = 0, 0
            for (axis, mask, _), bit in zip(order, bits, strict=True):
                near, copy = (bit, copy) if axis == "fsdp" else (near, copy + bit * (mask // 2))
            indices.append(near * copies + copy)
        return by_core(*indices)

    def all_bits(count):
        return [[number >> (count - 1 - i) & 1 for i in range(count)] for number in range(1 << count)]

    def gathered_targets(other_core):
        targets = []
        for differs in all_bits(len(far_bits) + stages):
            differs = differs[::-1]
            upper = 0
            for (_, mask, mine), bit in zip(far_bits, differs, strict=False):
                upper += (mine ^ bit) * (mask // 2)
            indices = []
            for order in orders:
                near, copy = 0, 0
                for (axis, mask, mine), bit in zip(order, differs[len(far_bits) :], strict=True):
                    near, copy = (mine ^ bit, copy) if axis == "fsdp" else (near, copy + (mine ^ bit) * (mask // 2))
                indices.append((2 * upper + near) * copies + copy)
            targets.append(by_core(*(indices[::-1] if other_core else indices)))
        return targets

    def stage_swap(value, number):
        if number < len(far_bits):
            return swap(value, *far_bits[number][:2])
        return swap_stage(value, number - len(far_bits))

    def first_blocks(grad):
        rest = all_bits(stages - 1)
        sent = [pick(grad, block_index([1 - own_bit(0)] + bits), 1) for bits in rest]
        kept = [pick(grad, block_index([own_bit(0)] + bits), 1) for bits in rest]
        return jnp.stack(sent, axis=1), kept

    def add_low(kept, came):
        return (kept.astype(jnp.float32) + came.astype(jnp.float32)).astype(LOW)

    def first_sum(kept, came):
        came = came if isinstance(came, list) else [came[:, i] for i in range(len(kept))]
        return jnp.stack([add_low(block, other) for block, other in zip(kept, came, strict=True)], axis=1)

    def next_start(held, number):
        pair = held.reshape(held.shape[:1] + (2, held.shape[1] // 2) + held.shape[2:])
        return pick(pair, own_bit(number), 1), swap_stage(pick(pair, 1 - own_bit(number), 1), number)

    def next_end(kept, came):
        held = add_low(kept, came)
        for number in range(2, stages):
            held = add_low(*next_start(held, number))
        return held.reshape(held.shape[:1] + held.shape[2:])

    out_rows = out_proj.shape[0] // dp_count
    shard_units = up_proj.shape[0]
    half_units = shard_units // 2
    up_rows = half_units // copies
    down_rows = down_proj.shape[0] // copies
    out_piece = pick(pick(out_proj.reshape(copies, 2, out_rows, width), copy_index), core)
    up_piece = pick(pick(up_proj.reshape(2, copies, up_rows, width), core), copy_index)
    up_held = jnp.concatenate([up_piece, out_piece])
    down_piece = pick(down_proj.reshape(copies, down_rows, hidden_units), copy_index)
    down_held = split_columns(down_piece, core, fsdp_count)
    far_stages = len(far_bits)

    def gather_stages(held, came, first, last):
        for number in range(first + 1, last + 1):
            held = jnp.concatenate([held, came])
            came = stage_swap(held, number)
        return held, came

    rounds = fsdp_count // CLIP_DEV
    unit_rows = in_proj.shape[0] // 3
    half_rows = unit_rows // 2
    piece_rows = unit_rows // dp_count
    pair_pairs, single_pairs, single_first = [], [], []
    slot_table = [[0] * (3 * rounds) for _ in range(CLIP_DEV)]
    pair_laps, single_laps = [0] * CLIP_DEV, [0] * CLIP_DEV
    for source in range(fsdp_count):
        keys = [divmod(3 * source + slot, fsdp_count) for slot in range(3)]
        owners = [spot // rounds for _, spot in keys]
        single = 0 if owners[0] != owners[1] else 2
        single_first.append(single == 0)
        twins = [1, 2] if single == 0 else [0, 1]
        place_of = owners[twins[0]]
        pair_pairs.append((source, pair_laps[place_of] * CLIP_DEV + place_of))
        for number, slot in enumerate(twins):
            kind, spot = keys[slot]
            slot_table[place_of][kind * rounds + spot % rounds] = pair_laps[place_of] * 3 + number
        pair_laps[place_of] += 1
        place_of = owners[single]
        single_pairs.append((source, single_laps[place_of] * CLIP_DEV + place_of))
        kind, spot = keys[single]
        slot_table[place_of][kind * rounds + spot % rounds] = single_laps[place_of] * 3 + 2
        single_laps[place_of] += 1
    single_leads = pick(jnp.array(single_first, jnp.int32), fsdp_index)
    slot_row = pick(jnp.array(slot_table, jnp.int32), place)
    key_table = [[row.index(slot) for slot in range(3 * rounds)] for row in slot_table]
    key_row = pick(jnp.array(key_table, jnp.int32), place)

    with jax.named_scope("gather_in_proj"):
        units = pick(pick(in_proj.reshape(3, 2, copies, piece_rows, width), core, 1), copy_index, 1)
        twins = lax.ppermute(lax.dynamic_slice_in_dim(units, single_leads, 2, 0), "fsdp", pair_pairs)
        single = lax.ppermute(lax.dynamic_slice_in_dim(units, 2 - 2 * single_leads, 1, 0), "fsdp", single_pairs)
    token, twins, single, own_x, own_grad = fence(token, [], twins, single, hidden_states, cotangent)

    with jax.named_scope("gather_tokens"):
        near = swap(own_x, "fsdp", 1)
        far = swap(own_x, "fsdp", 2)
    with jax.named_scope("gather_in_proj"):
        units = jnp.concatenate([twins, single])
        units = widen_bits(units.reshape((1,) * len(lap_bits) + units.shape), lap_bits, 0)
        units = units.reshape((1,) * copy_levels + (3 * rounds, piece_rows, width))
        units = widen_bits(units, copy_bits, 0).reshape(copies, 3 * rounds, piece_rows, width)
    token, units, near, far, own_grad, up_held, down_held = fence(
        token, [], units, near, far, own_grad, up_held, down_held
    )

    with jax.named_scope("gather_in_proj"):
        core_came = swap(units, *core_bit[:2])
    with jax.named_scope("gather_tokens"):
        both = swap(far, "fsdp", 1)
    with jax.named_scope("gather_up_and_out_proj"):
        up_came = stage_swap(up_held, 0)
    with jax.named_scope("gather_in_proj"):
        weight_in = spread_heads(units, core_came, core, slot_row, rounds)
    clip_blocks = [hidden_states, near, far, None]

    padded_width = 3 * GROUP_LANES
    zeros = jnp.zeros((width,), jnp.float32)
    group_bias = jnp.stack([proj_biases[0] * SCORE_SCALE, zeros, proj_biases[1]])
    group_bias = pick(group_bias.reshape(3, CLIP_DEV, GROUP_HEADS, HD), place, 1)
    group_bias = jnp.pad(group_bias, ((0, 0), (0, 0), (0, LANES - HD)))
    lane = jnp.arange(LANES)
    spare = jnp.stack(
        [
            lane == HD,
            (lane > HD) & (lane <= HD + 3),
            (lane >= HD) & (lane < HD + 3),
        ]
    ).astype(jnp.float32)
    columns = (group_bias + spare[:, None]).reshape(1, padded_width)

    def project_block(number, held, after):
        limit = (length - (place ^ number) * tokens_here).reshape(1)
        return project(
            number, clip_blocks[number], weight_in, norm_gains[0:1], norm_shifts[0:1], columns, limit, held, after
        )

    held = project_block(0, None, [token])
    held = project_block(1, held, [token])
    token, up_came, own_grad, down_held = fence(token, [held[0]], up_came, own_grad, down_held)
    with jax.named_scope("gather_down_proj"):
        down_came = stage_swap(down_held, 0)
    with jax.named_scope("gather_up_and_out_proj"):
        up_held, up_came = gather_stages(up_held, up_came, 0, far_stages - 1)
    with jax.named_scope("gather_tokens"):
        grad_other = swap(own_grad, "dp", 1)
    held = project_block(2, held, [token])
    token, both, grad_other = fence(token, [held[0]], both, grad_other)
    clip_blocks[3] = both
    queries, pair, normed_one = project_block(3, held, [token])
    token, pair, up_came = fence(token, [], pair, up_came)
    with jax.named_scope("gather_up_and_out_proj"):
        up_held, up_came = gather_stages(up_held, up_came, far_stages - 1, far_stages)
    contexts, ready = [None] * CLIP_DEV, [None] * CLIP_DEV
    contexts[1], ready[1] = attend(1, queries, pair, [token])
    token, contexts[1], down_came = fence(token, [], contexts[1], down_came)
    with jax.named_scope("context_back"):
        sent_one = swap(contexts[1], "fsdp", 1)
    with jax.named_scope("gather_down_proj"):
        down_held, down_came = gather_stages(down_held, down_came, 0, far_stages - 1)
    contexts[3], ready[3] = attend(3, queries, pair, [token])
    token, contexts[3], sent_one, up_came = fence(token, [], contexts[3], sent_one, up_came)
    with jax.named_scope("context_back"):
        sent_three = swap(contexts[3], "fsdp", 3)
    with jax.named_scope("gather_out_proj"):
        up_held, up_came = gather_stages(up_held, up_came, far_stages, far_stages + stages - 2)
        blocks = jnp.concatenate([up_held, up_came]).reshape(-1, up_rows + out_rows, width)
        up_held = blocks[:, :up_rows].reshape(-1, width)
        out_held = blocks[:, up_rows:].reshape(-1, width)
        out_came = stage_swap(out_held, far_stages + stages - 1)
    contexts[2], ready[2] = attend(2, queries, pair, [token])
    token, contexts[2], sent_three, out_came, up_held, down_came = fence(
        token, [], contexts[2], sent_three, out_came, up_held, down_came
    )
    with jax.named_scope("context_back"):
        sent_two = swap(contexts[2], "fsdp", 2)
    with jax.named_scope("gather_up_proj"):
        rows = up_held.shape[0] // 2
        up_came = [stage_swap(up_held[i * rows : (i + 1) * rows], far_stages + stages - 1) for i in range(2)]
    with jax.named_scope("gather_out_proj"):
        out_blocks = jnp.concatenate([out_held, out_came])
        out_other = swap(out_blocks, *core_bit[:2])
    contexts[0], ready[0] = attend(0, queries, pair, [token])
    token, sent_two, out_other, down_came, up_came[0] = fence(
        token, [contexts[0]], sent_two, out_other, down_came, up_came[0]
    )
    with jax.named_scope("gather_out_proj"):
        targets, others = gathered_targets(False), gathered_targets(True)
        homes = [2 * t + core for t in targets] + [2 * t + 1 - core for t in others]
        out_full = assemble_blocks([out_blocks, out_other], homes, out_rows, width).reshape(width, width)
    with jax.named_scope("context_back"):
        parts = jnp.stack([contexts[0], sent_one, sent_two, sent_three])
        context_low = jnp.concatenate([pick(parts, place ^ group) for group in range(CLIP_DEV)], axis=1)
    context_heads = jnp.concatenate(contexts)
    queries_ready = jnp.concatenate(ready)
    with jax.named_scope("gather_down_proj"):
        down_held, down_came = gather_stages(down_held, down_came, far_stages - 1, far_stages)
    with jax.named_scope("gather_up_proj"):
        up_half = assemble([up_held, *up_came], targets, up_rows, (hidden_units // 2, width))

    inputs = hidden_states.astype(jnp.float32)
    grad_pair = jnp.concatenate([cotangent, grad_other])
    attention = dot_nt(context_low, out_full) + proj_biases[2]
    middle = inputs + attention
    unit_two, scale_two = normalise(middle)
    normed_two = (unit_two * norm_gains[1] + norm_shifts[1]).astype(LOW)
    normed_other = swap(normed_two, "dp", 1)
    half_bias = pick(up_bias.reshape(fsdp_count, 2, half_units), core, 1).reshape(hidden_units // 2)
    token, normed_two, down_came = fence(token, [], normed_two, down_came)
    held = list(widen(0, normed_two, up_half, half_bias, None, [token]))
    with jax.named_scope("gather_down_proj"):
        down_held, down_came = gather_stages(down_held, down_came, far_stages, far_stages + stages - 1)
    activated, slope = widen(1, normed_other, up_half, half_bias, held)
    normed_pair = jnp.concatenate([normed_two, normed_other])
    grad_down = dot_tn(grad_pair, activated).astype(LOW)
    with jax.named_scope("reduce_down_proj"):
        grad = grad_down.reshape(far_count, 2 * copies, down_rows, hidden_units // 2)
        sent, down_kept = first_blocks(grad)
        sent = [sent[:, i] for i in range(len(down_kept))]
    token, slope, down_came, *sent = fence(token, [], slope, down_came, *sent)

    with jax.named_scope("reduce_down_proj"):
        down_first = [swap_stage(block, 0) for block in sent]
    with jax.named_scope("gather_down_proj"):
        down_half = assemble([down_held, down_came], targets, down_rows, (width, hidden_units // 2), [token])
    grad_activated = dot_nn(grad_pair, down_half)
    grad_widened = (grad_activated * slope.astype(jnp.float32)).astype(LOW)
    token, grad_widened, down_first[0] = fence(token, [], grad_widened, down_first[0])

    def over_cores(rows, product):
        sent = product(rows[tokens_here:]).astype(LOW)
        return product(rows[:tokens_here]) + swap(sent, "dp", 1).astype(jnp.float32)

    grad_normed_two = over_cores(grad_widened, lambda rows: dot_nn(rows, up_half))
    grad_out = cotangent.astype(jnp.float32)
    grad_middle = grad_out + norm_back(grad_normed_two, norm_gains[1], unit_two, scale_two)
    grad_attention = grad_middle.astype(LOW)
    grad_context = dot_nn(grad_attention, out_full).astype(LOW)
    token, grad_context, grad_widened, *down_first = fence(token, [], grad_context, grad_widened, *down_first)

    with jax.named_scope("grad_context_to_heads"):
        groups = [grad_context[:, i * GROUP_WIDTH : (i + 1) * GROUP_WIDTH] for i in range(CLIP_DEV)]
        groups = jnp.stack(groups)
        sends = [pick(groups, place ^ j) for j in range(CLIP_DEV)]
        grad_came = [swap(sends[j], "fsdp", j) for j in range(1, CLIP_DEV)]
    grad_up = dot_tn(grad_widened, normed_pair).astype(LOW)
    grad_exit = dot_tn(grad_attention, context_low).astype(LOW)
    feedforward = over_cores(activated, lambda rows: dot_nt(rows, down_half)) + proj_biases[3]
    outputs = (middle + feedforward).astype(LOW)
    stat_terms = jnp.stack(
        [
            jnp.sum(row_valid * jnp.sum(middle * middle, axis=1)),
            jnp.sum(row_valid * jnp.sum(attention * attention, axis=1)),
            jnp.sum(row_valid * jnp.sum(feedforward * feedforward, axis=1)),
        ]
    )
    with jax.named_scope("small_sums"):
        half_up = jnp.sum(grad_widened.astype(jnp.float32), axis=0).reshape(fsdp_count, half_units)
        up_terms = jnp.zeros((fsdp_count, 2, half_units), jnp.float32)
        up_terms = lax.dynamic_update_index_in_dim(up_terms, half_up, core, 1).reshape(hidden_units // width, width)
        early = jnp.concatenate(
            [
                jnp.stack(
                    [
                        jnp.sum(grad_normed_two * unit_two, axis=0),
                        jnp.sum(grad_normed_two, axis=0),
                        jnp.sum(grad_attention.astype(jnp.float32), axis=0),
                        jnp.sum(grad_out, axis=0),
                        jnp.pad(stat_terms, (0, width - 3)),
                    ]
                ),
                up_terms,
            ]
        )
    token, *grad_came, grad_up, grad_exit, down_first[0] = fence(
        token, [], *grad_came, grad_up, grad_exit, down_first[0]
    )

    grad_heads = jnp.concatenate([sends[0], *grad_came])
    far_split = (2,) * len(far_bits)
    with jax.named_scope("reduce_up_proj"):
        exit_grad = grad_exit.reshape(far_count * 2 * copies, 2, out_rows, width)
        exit_came = give(exit_grad, 1, core_bit)
        sent, up_kept = first_blocks(grad_up.reshape(far_count, 2 * copies, up_rows, width))
        up_first = swap_stage(sent, 0)
    with jax.named_scope("reduce_down_proj"):
        down_kept, down_came = next_start(first_sum(down_kept, down_first), 1)
    held = attend_back(0, queries_ready, pair, context_heads, grad_heads, None, [token])
    token, exit_came = fence(token, [held[0]], exit_came)

    with jax.named_scope("reduce_up_proj"):
        exit_grad = keep(exit_grad, exit_came, 1, core_bit).reshape(far_count, 2 * copies, out_rows, width)
        sent, exit_kept = first_blocks(exit_grad)
        exit_first = swap_stage(sent, 0)
    held = attend_back(1, queries_ready, pair, context_heads, grad_heads, held, [token])
    token, down_came = fence(token, [held[0]], down_came)

    with jax.named_scope("reduce_down_proj"):
        down_sum = next_end(down_kept, down_came)
        down_sum = down_sum.reshape(far_split + down_sum.shape[1:])
        down_came = give(down_sum, far_stages - 1, far_bits[-1])
    held = attend_back(2, queries_ready, pair, context_heads, grad_heads, held, [token])
    token, up_first, exit_first, down_came = fence(token, [held[0]], up_first, exit_first, down_came)

    with jax.named_scope("reduce_up_proj"):
        up_second = jnp.concatenate([first_sum(up_kept, up_first), first_sum(exit_kept, exit_first)], axis=2)
        up_kept, up_came = next_start(up_second, 1)
    with jax.named_scope("reduce_down_proj"):
        down_sum = keep(down_sum, down_came, far_stages - 1, far_bits[-1])
        if far_stages > 2:
            down_sum = reduce_last(down_sum, far_bits[1:-1])
        down_came = give(down_sum, 0, far_bits[0])
    kinds = attend_back(3, queries_ready, pair, context_heads, grad_heads, held, [token])
    token, *kinds, up_came, down_came = fence(token, [], *kinds, up_came, down_came)

    grad_query, grad_key, grad_value = kinds
    with jax.named_scope("reduce_up_proj"):
        up_second = next_end(up_kept, up_came)
        up_second = up_second.reshape(far_split + up_second.shape[1:])
        up_came = give(up_second, far_stages - 1, far_bits[-1])
    with jax.named_scope("reduce_in_proj"):
        entry = jnp.stack([dot_tn(grad, normed_one).astype(LOW) for grad in kinds])
        entry = entry.reshape(3, GROUP_HEADS, LANES, width)[:, :, :HD]
        entry = entry.reshape((3 * rounds, 2) + (2,) * copy_levels + (piece_rows, width))
    with jax.named_scope("reduce_down_proj"):
        down_sum = keep(down_sum, down_came, 0, far_bits[0])
        down_sum = down_sum.reshape((1,) * copy_levels + down_sum.shape)
        down_came = swap(down_sum, *copy_bits[0][:2])
    token, entry, down_came = fence(token, [], entry, down_came)
    with jax.named_scope("reduce_in_proj"):
        entry_came = give(entry, 1, core_bit)
    with jax.named_scope("reduce_down_proj"):
        down_sum = join_bit(down_sum, down_came, 0, copy_bits[0][2])
        down_sum = widen_bits(down_sum, copy_bits[1:], 1).reshape(down_rows * copies, hidden_units // 2)
        down_other = swap(down_sum, *core_bit[:2])
    partial, sums = [None] * CLIP_DEV, [None] * CLIP_DEV
    partial[3], sums[3] = entry_back(3, clip_blocks[3], kinds, weight_in, [token])
    token, partial[3], entry_came = fence(token, [], partial[3], entry_came)
    with jax.named_scope("reduce_tokens"):
        both_came = swap(partial[3], "fsdp", 1)
    with jax.named_scope("reduce_in_proj"):
        entry = keep(entry, entry_came, 1, core_bit).reshape(3 * rounds, half_rows, width)
        entry = gather_blocks(entry, key_row)
        entry = entry.reshape((2,) * len(lap_bits) + (3, half_rows, width))
        if len(lap_bits) > 1:
            entry = reduce_last(entry, lap_bits[1:])
        entry_came = give(entry, 0, lap_bits[0])
    partial[1], sums[1] = entry_back(1, clip_blocks[1], kinds, weight_in, [token])
    token, partial[1], up_came = fence(token, [], partial[1], up_came)
    with jax.named_scope("reduce_tokens"):
        near_came = swap(partial[1], "fsdp", 1)
    partial[2], sums[2] = entry_back(2, clip_blocks[2], kinds, weight_in, [token])
    partial[0], sums[0] = entry_back(0, clip_blocks[0], kinds, weight_in, [token])
    token, partial[2], partial[0], sums[0], entry_came, down_other, both_came, up_came = fence(
        token, [], partial[2], partial[0], sums[0], entry_came, down_other, both_came, up_came
    )
    with jax.named_scope("reduce_tokens"):
        far_came = swap(add_low(partial[2], both_came), "fsdp", 2)
    with jax.named_scope("reduce_in_proj"):
        entry = keep(entry, entry_came, 0, lap_bits[0])
        entry = entry.reshape((3,) + (2,) * copy_levels + (piece_rows, width))
        entry_came = give(entry, 1, copy_bits[0])
    with jax.named_scope("reduce_up_proj"):
        sums_up = keep(up_second, up_came, far_stages - 1, far_bits[-1])
        if far_stages > 2:
            sums_up = reduce_last(sums_up, far_bits[1:-1])
        up_came = give(sums_up, 0, far_bits[0])
    down_out = merge_columns(down_sum, down_other, core, fsdp_count)
    token, entry_came = fence(token, [], entry_came)
    with jax.named_scope("reduce_in_proj"):
        entry = keep(entry, entry_came, 1, copy_bits[0])
        entry = reduce_bits(entry, copy_bits[1:], 1)
        twins = lax.ppermute(entry[:2], "fsdp", [(target, source) for source, target in pair_pairs])
        single = lax.ppermute(entry[2:], "fsdp", [(target, source) for source, target in single_pairs])
    def place_heads(grads):
        columns = jnp.sum(grads.astype(jnp.float32), axis=0).reshape(GROUP_HEADS, LANES)[:, :HD]
        rows = jnp.zeros((CLIP_DEV, GROUP_WIDTH), jnp.float32)
        return lax.dynamic_update_index_in_dim(rows, columns.reshape(GROUP_WIDTH), place, 0).reshape(width)

    with jax.named_scope("small_sums"):
        late = jnp.concatenate(
            [
                sums[0] + sums[1] + sums[2] + sums[3],
                jnp.stack([place_heads(grad_query), place_heads(grad_value)]),
                early,
            ]
        )
        for level in range(dp_count.bit_length() - 1):
            late = late + swap(late, "dp", 1 << level)
        late = late + swap(late, "fsdp", 1)
    token, twins, single, near_came, far_came, late, up_came = fence(
        token, [], twins, single, near_came, far_came, late, up_came
    )
    with jax.named_scope("reduce_up_proj"):
        sums_up = keep(sums_up, up_came, 0, far_bits[0])
        ends = widen_bits(sums_up.reshape((1,) * copy_levels + sums_up.shape), copy_bits, 0)
        ends = widen_bits(ends[None], [core_bit], 0).reshape(2, copies, -1, width)
        up_sum = ends[:, :, :up_rows].reshape(up_proj.shape).astype(jnp.float32)
        exit_sum = jnp.moveaxis(ends[:, :, up_rows : up_rows + out_rows], 0, 1)
        exit_sum = exit_sum.reshape(out_proj.shape).astype(jnp.float32)
    with jax.named_scope("reduce_in_proj"):
        entry = jnp.where(
            single_leads == 1, jnp.concatenate([single, twins]), jnp.concatenate([twins, single])
        ).reshape(3 * piece_rows, width)
        entry = widen_bits(entry.reshape((1,) * (1 + copy_levels) + entry.shape), copy_bits, 1)
        entry = widen_bits(entry, [core_bit], 0).reshape(dp_count, 3, piece_rows, width)
        entry_sum = jnp.moveaxis(entry, 1, 0).reshape(in_proj.shape).astype(jnp.float32)

    with jax.named_scope("small_sums"):
        for level in range(1, fsdp_levels):
            late = late + swap(late, "fsdp", 1 << level)
    grad_normed_one = partial[0].astype(jnp.float32) + near_came.astype(jnp.float32) + far_came.astype(jnp.float32)
    unit_one, scale_one = normalise(inputs)
    grad_hidden = grad_middle + norm_back(grad_normed_one, norm_gains[0], unit_one, scale_one)
    valid_count = jnp.sum(clip_lengths).astype(jnp.float32) * width
    root_means = jnp.sqrt(late[14, :3] / valid_count)
    return (
        outputs,
        grad_hidden.astype(LOW),
        entry_sum,
        exit_sum,
        up_sum,
        down_out,
        jnp.stack([late[0], late[10]]),
        jnp.stack([late[1], late[11]]),
        jnp.stack([late[8], late[9], late[12], late[13]]),
        late[15 : 15 + hidden_units // width].reshape(hidden_units),
        root_means,
    )


def solution(mesh):
    in_specs = (
        P(("dp", "fsdp"), None),
        P(),
        P(),
        P(),
        P(),
        P(),
        P("fsdp", None),
        P("fsdp", None),
        P("fsdp", None),
        P("fsdp", None),
        P(("dp", "fsdp"), None),
    )
    out_specs = (
        P(("dp", "fsdp"), None),
        P(("dp", "fsdp"), None),
        P("fsdp", None),
        P("fsdp", None),
        P("fsdp", None),
        P("fsdp", None),
        P(),
        P(),
        P(),
        P(),
        P(),
    )
    return jax.shard_map(
        on_device, mesh=mesh, in_specs=in_specs, out_specs=out_specs, check_vma=False
    )
```

time: 769 us -> 650 us (0.85)
  waiting for transfers between devices: 201 us -> 120 us
  starting transfers between devices: 107 us -> 57.7 us
  matrix products: 79.1 us -> 93.9 us
  Pallas kernels: 206 us -> 197 us
    ppermute x63 -> x43, waiting for transfers between devices: 154 us -> 85.3 us  [swap(): return lax.ppermute(value, axis, pairs)]
    ppermute x63 -> x43, starting transfers between devices: 82.3 us -> 43.7 us  [swap(): return lax.ppermute(value, axis, pairs)]
    unnamed x192 -> x274, local copies, waits for them, and re-layouts: 19.5 us -> 33.8 us
    ppermute x12 -> x16, waiting for transfers between devices: 46.7 us -> 34.6 us  [the longest x12 27.5 us: swap_by_core(): return lax.ppermute(value, ('dp', 'fsdp'), pairs)]
    ppermute x12 -> x16, starting transfers between devices: 25 us -> 14 us  [the longest x12 6.39 us: swap_by_core(): return lax.ppermute(value, ('dp', 'fsdp'), pairs)]
    pallas_call x22 -> x25, Pallas kernels: 206 us -> 197 us  [call(): pl.pallas_call(kernel, grid_spec=pltpu.PrefetchScalarGridSpec(num_scalar_...]
    dot_general x4, matrix products: 29 us -> 37.1 us  [dot_nn(): return jnp.dot(lhs, rhs, preferred_element_type=jnp.float32)]
    convert_element_type x21 -> x13, other arithmetic: 30 us -> 22.2 us  [the longest x5 12.3 us: add_low(): return (kept.astype(jnp.float32) + came.astype(jnp.float32)).astype(LOW)]
  transfers between devices with their start and end apart: 75 -> 59, of which waited for: 21 -> 23; matrix products, arithmetic and copies ran while one was open for 25% -> 29% of each run, Pallas kernels for 26% -> 31%
where the time goes in v3:
time: 650 us; the launch traced here: 642 us
  Pallas kernels  197 us (30%)
  waiting for transfers between devices  120 us (18%)
  matrix products  93.9 us (14%)
  local copies, waits for them, and re-layouts  82.8 us (13%)
  other arithmetic  81.1 us (12%)
  starting transfers between devices  57.7 us (9%)
  between operations  9.2 us (1%)
    pallas_call x25, Pallas kernels, call(): pl.pallas_call(kernel, grid_spec=pltpu.PrefetchScalarGridSpec(num_scalar_...  197 us
    ppermute x43, waiting for transfers between devices, swap(): return lax.ppermute(value, axis, pairs)  85.3 us
    ppermute x43, starting transfers between devices, swap(): return lax.ppermute(value, axis, pairs)  43.7 us
    dot_general x4, matrix products, dot_nn(): return jnp.dot(lhs, rhs, preferred_element_type=jnp.float32)  37.1 us
    dot_general x6, matrix products, dot_tn(): lax.dot_general(lhs, rhs, (((0,), (0,)), ((), ())), preferred_element_typ...  34.5 us
    unnamed x274, local copies, waits for them, and re-layouts  33.8 us
    ppermute x12, waiting for transfers between devices, swap_by_core(): return lax.ppermute(value, ('dp', 'fsdp'), pairs)  27.5 us
    dot_general x3, matrix products, dot_nt(): lax.dot_general(lhs, rhs, (((1,), (1,)), ((), ())), preferred_element_typ...  22.3 us
  transfers between devices with their start and end apart: 59, of which 23 were waited for; matrix products, arithmetic and copies ran while one was open for 29% of the time, Pallas kernels for 31%

profile of v3, /device:TPU:3, one launch (start us, length us, event | category | flops | bytes accessed | tf_op | source)
XLA Modules:
  0.0 641.6 jit_solution(3270643509281122156)
XLA Ops:
  23.2 9.3 %collective-permute-done.2 = bf16[1,3,40,1280]{3,2,1,0:T(8,128)(2,1)S(1)} collective-permute-done((bf16[1,3,40,1280]{3,2,1,0:T(8,128)(2,1)S(1)}, bf16[1,3,40,1280]{3,2,1,0:T(8,128)(2,1)S(1)}, u32[]{:S(2)}, u32[]{:S(2)}) %collective-permute-start.2) | collective-permute-done | bytes 307232 | tf_op jit(solution)/shard_map/gather_in_proj/ppermute | solution.py:31
  105.4 8.9 %collective-permute-done.10.refs_2_ = bf16[400,1280]{1,0:T(8,128)(2,1)S(1)} collective-permute-done((bf16[400,1280]{1,0:T(8,128)(2,1)}, bf16[400,1280]{1,0:T(8,128)(2,1)S(1)}, u32[]{:S(2)}, u32[]{:S(2)}) %collective-permute-start.10) | collective-permute-done | bytes 1024032 | tf_op jit(solution)/shard_map/gather_up_and_out_proj/ppermute | solution.py:31
  120.6 9.4 %shard_map.231 = (bf16[512,320]{1,0:T(8,128)(2,1)}, bf16[512,512]{1,0:T(8,128)(2,1)}) custom-call(bf16[2048,512]{1,0:T(8,128)(2,1)} %get-tuple-element.182.refs_0_, bf16[2048,1024]{1,0:T(8,128)(2,1)} %get-tuple-element.185.refs_1_.refs_2_, f32[8,128]{1,0:T(8,128)} %get-tuple-element.186.refs_2_.refs_0_), custom_call_target="tpu_custom_call" | custom-call | tf_op jit(solution)/shard_map/pallas_call | solution.py:95
  130.0 11.3 %collective-permute-done.11.refs_2_ = bf16[80,2560]{1,0:T(8,128)(2,1)S(1)} collective-permute-done((bf16[80,2560]{1,0:T(8,128)(2,1)S(1)}, bf16[80,2560]{1,0:T(8,128)(2,1)S(1)}, u32[]{:S(2)}, u32[]{:S(2)}) %collective-permute-start.11) | collective-permute-done | bytes 409632 | tf_op jit(solution)/shard_map/gather_down_proj/ppermute | solution.py:31
  145.7 9.8 %shard_map.233 = (bf16[512,320]{1,0:T(8,128)(2,1)}, bf16[512,512]{1,0:T(8,128)(2,1)}) custom-call(bf16[2048,512]{1,0:T(8,128)(2,1)} %get-tuple-element.182.refs_0_, bf16[2048,1024]{1,0:T(8,128)(2,1)} %get-tuple-element.185.refs_1_.refs_2_, f32[8,128]{1,0:T(8,128)} %get-tuple-element.189.refs_2_.refs_0_), custom_call_target="tpu_custom_call" | custom-call | tf_op jit(solution)/shard_map/pallas_call | solution.py:95
  163.2 9.4 %shard_map.235 = (bf16[512,320]{1,0:T(8,128)(2,1)}, bf16[512,512]{1,0:T(8,128)(2,1)}) custom-call(bf16[2048,512]{1,0:T(8,128)(2,1)} %get-tuple-element.182.refs_0_, bf16[2048,1024]{1,0:T(8,128)(2,1)} %get-tuple-element.185.refs_1_.refs_2_, f32[8,128]{1,0:T(8,128)} %get-tuple-element.193.refs_2_.refs_0_), custom_call_target="tpu_custom_call" | custom-call | tf_op jit(solution)/shard_map/pallas_call | solution.py:95
  186.8 9.6 %shard_map.237 = (bf16[512,320]{1,0:T(8,128)(2,1)}, bf16[512,512]{1,0:T(8,128)(2,1)}) custom-call(bf16[2048,512]{1,0:T(8,128)(2,1)} %get-tuple-element.182.refs_0_, bf16[2048,1024]{1,0:T(8,128)(2,1)} %get-tuple-element.185.refs_1_.refs_2_, f32[8,128]{1,0:T(8,128)} %get-tuple-element.198.refs_2_.refs_0_), custom_call_target="tpu_custom_call" | custom-call | tf_op jit(solution)/shard_map/pallas_call | solution.py:95
  196.4 7.0 %collective-permute-done.19.refs_4_ = bf16[640,1280]{1,0:T(8,128)(2,1)} collective-permute-done((bf16[640,1280]{1,0:T(8,128)(2,1)}, bf16[640,1280]{1,0:T(8,128)(2,1)}, u32[]{:S(2)}, u32[]{:S(2)}) %collective-permute-start.19) | collective-permute-done | bytes 1638432 | tf_op jit(solution)/shard_map/gather_up_proj/ppermute | solution.py:42
  232.9 11.0 %collective-permute-done.21.refs_3_ = bf16[640,1280]{1,0:T(8,128)(2,1)} collective-permute-done((bf16[640,1280]{1,0:T(8,128)(2,1)}, bf16[640,1280]{1,0:T(8,128)(2,1)}, u32[]{:S(2)}, u32[]{:S(2)}) %collective-permute-start.21) | collective-permute-done | bytes 1638432 | tf_op jit(solution)/shard_map/gather_up_proj/ppermute | solution.py:42
  250.6 8.9 %shard_map.240 = (bf16[1024,2560]{1,0:T(8,128)(2,1)}, bf16[1024,2560]{1,0:T(8,128)(2,1)}) custom-call(bf16[512,1280]{1,0:T(8,128)(2,1)} %get-tuple-element.211.refs_0_, bf16[2560,1280]{1,0:T(8,128)(2,1)} %gather_up_proj.1.refs_1_, f32[1,2560]{1,0:T(1,128)} %reshape_reshape.4.refs_2_, f32[8,128]{1,0:T(8,128)} %get-tuple-element.212.refs_3_.refs_0_), custom_call_target="tpu_custom_call" | custom-call | tf_op jit(solution)/shard_map/pallas_call | solution.py:95
  259.5 9.0 %shard_map.241 = (bf16[1024,2560]{1,0:T(8,128)(2,1)}, bf16[1024,2560]{1,0:T(8,128)(2,1)}) custom-call(bf16[512,1280]{1,0:T(8,128)(2,1)} %copy-done.88, bf16[2560,1280]{1,0:T(8,128)(2,1)} %gather_up_proj.1.refs_1_, f32[1,2560]{1,0:T(1,128)} %reshape_reshape.4.refs_2_, ...), custom_call_target="tpu_custom_call", output_to_operand_aliasing={{0}: (3, {}), {1}: (4, {})} | custom-call | tf_op jit(solution)/shard_map/pallas_call | solution.py:95
  268.5 9.7 %convolution_convert_fusion.1 = bf16[1280,2560]{1,0:T(8,128)(2,1)S(1)} fusion(bf16[1024,1280]{1,0:T(8,128)(2,1)S(1)} %constant_dynamic-update-slice_fusion.4, bf16[1024,2560]{1,0:T(8,128)(2,1)} %get-tuple-element.215), kind=kOutput, calls=%fused_computation.1 | convolution fusion | flops 6714163200 | bytes 14417920 | tf_op jit(solution)/shard_map/dot_general | solution.py:56
  290.2 12.7 %multiply_convert_fusion.refs_1_ = bf16[1024,2560]{1,0:T(8,128)(2,1)} fusion(bf16[1024,2560]{1,0:T(8,128)(2,1)} %get-tuple-element.221, bf16[1024,1280]{1,0:T(8,128)(2,1)S(1)} %copy-done.97, bf16[1280,2560]{1,0:T(8,128)(2,1)} %gather_down_proj.1), kind=kOutput, calls=%fused_computation.3 | convolution fusion | flops 6718750720 | bytes 19660800 | tf_op jit(solution)/shard_map/dot_general | solution.py:52
  304.2 8.3 %convolution_convert_fusion.7 = bf16[512,1280]{1,0:T(8,128)(2,1)} fusion(bf16[2560,1280]{1,0:T(8,128)(2,1)} %gather_up_proj.1.refs_1_, bf16[1024,2560]{1,0:T(8,128)(2,1)} %get-tuple-element.223.refs_2_), kind=kOutput, calls=%fused_computation.39 | convolution fusion | flops 3356098560 | bytes 10485760 | tf_op jit(solution)/shard_map/dot_general | solution.py:52
  314.3 7.4 %convolution_convert_fusion.8 = bf16[512,1280]{1,0:T(8,128)(2,1)S(1)} fusion(bf16[1280,2560]{1,0:T(8,128)(2,1)} %gather_down_proj.1, bf16[1024,2560]{1,0:T(8,128)(2,1)} %get-tuple-element.215), kind=kOutput, calls=%fused_computation.40 | convolution fusion | flops 3356098560 | bytes 10485760 | tf_op jit(solution)/shard_map/dot_general | solution.py:46
  323.1 10.2 %multiply_reduce_fusion.3 = (f32[1280]{0:T(1024)}, f32[512]{0:T(512)S(1)}, f32[512]{0:T(512)S(1)}, f32[512]{0:T(512)S(1)}, f32[1280]{0:T(1024)}, /*index=5*/f32[512,1280]{1,0:T(8,128)}) fusion(f32[512,1280]{1,0:T(8,128)S(1)} %copy-done.33, f32[512]{0:T(512)S(1)} %add_rsqrt_fusion.1, f32[512]{0:T(512)S(1)} %broadcast_multiply_fusion.5, ...), kind=kOutput, calls=%fused_computation.57 | convolution fusion | flops 3363958784 | bytes 15757312 | tf_op jit(solution)/shard_map/dot_general | solution.py:52
  333.4 9.6 %multiply_reduce_fusion = (f32[512]{0:T(512)S(1)}, bf16[512,1280]{1,0:T(8,128)(2,1)}, f32[1280]{0:T(1024)S(1)}, f32[512,1280]{1,0:T(8,128)}, f32[1280]{0:T(1024)}) fusion(f32[512,1280]{1,0:T(8,128)S(1)} %copy-done.33, f32[512]{0:T(512)S(1)} %broadcast_multiply_fusion.3, f32[512]{0:T(512)S(1)} %broadcast_multiply_fusion.5, ...), kind=kOutput, calls=%fused_computation.53 | convolution fusion | flops 3368547328 | bytes 21002240 | tf_op jit(solution)/shard_map/dot_general | solution.py:46
  355.9 9.0 %convolution_convert_fusion.refs_4_ = bf16[2560,1280]{1,0:T(8,128)(2,1)} fusion(bf16[1024,2560]{1,0:T(8,128)(2,1)S(1)} %copy-done.6, bf16[512,1280]{1,0:T(8,128)(2,1)S(1)} %copy-done.89, bf16[512,1280]{1,0:T(8,128)(2,1)S(1)} %copy-done.31), kind=kOutput, calls=%fused_computation | convolution fusion | flops 6719406080 | bytes 14417920 | tf_op jit(solution)/shard_map/dot_general | solution.py:56
  390.1 14.4 %shard_map.246 = (bf16[2048,512]{1,0:T(8,128)(2,1)}, bf16[2048,512]{1,0:T(8,128)(2,1)}, bf16[2048,512]{1,0:T(8,128)(2,1)}) custom-call(bf16[2048,512]{1,0:T(8,128)(2,1)} %copy-done.10, bf16[2048,1024]{1,0:T(8,128)(2,1)} %get-tuple-element.185.refs_1_.refs_2_, bf16[2048,1024]{1,0:T(8,128)(2,1)} %get-tuple-element.185.refs_1_.refs_2_, ...), custom_call_target="tpu_custom_call" | custom-call | tf_op jit(solution)/shard_map/pallas_call | solution.py:95
  404.5 14.3 %shard_map.248 = (bf16[2048,512]{1,0:T(8,128)(2,1)}, bf16[2048,512]{1,0:T(8,128)(2,1)}, bf16[2048,512]{1,0:T(8,128)(2,1)}) custom-call(bf16[2048,512]{1,0:T(8,128)(2,1)} %copy-done.10, bf16[2048,1024]{1,0:T(8,128)(2,1)} %get-tuple-element.185.refs_1_.refs_2_, ...), custom_call_target="tpu_custom_call", output_to_operand_aliasing={{0}: (5, {}), {1}: (6, {}), {2}: (7, {})} | custom-call | tf_op jit(solution)/shard_map/pallas_call | solution.py:95
  427.8 14.2 %shard_map.250 = (bf16[2048,512]{1,0:T(8,128)(2,1)}, bf16[2048,512]{1,0:T(8,128)(2,1)}, bf16[2048,512]{1,0:T(8,128)(2,1)}) custom-call(bf16[2048,512]{1,0:T(8,128)(2,1)} %copy-done.10, bf16[2048,1024]{1,0:T(8,128)(2,1)} %get-tuple-element.185.refs_1_.refs_2_, ...), custom_call_target="tpu_custom_call", output_to_operand_aliasing={{0}: (5, {}), {1}: (6, {}), {2}: (7, {})} | custom-call | tf_op jit(solution)/shard_map/pallas_call | solution.py:95
  469.5 14.3 %shard_map.252 = (bf16[2048,512]{1,0:T(8,128)(2,1)}, bf16[2048,512]{1,0:T(8,128)(2,1)}, bf16[2048,512]{1,0:T(8,128)(2,1)}) custom-call(bf16[2048,512]{1,0:T(8,128)(2,1)} %copy-done.10, bf16[2048,1024]{1,0:T(8,128)(2,1)} %get-tuple-element.185.refs_1_.refs_2_, ...), custom_call_target="tpu_custom_call", output_to_operand_aliasing={{0}: (5, {}), {1}: (6, {}), {2}: (7, {})} | custom-call | tf_op jit(solution)/shard_map/pallas_call | solution.py:95
  588.5 14.8 %collective-permute-done.52.refs_6_ = bf16[200,1280]{1,0:T(8,128)(2,1)S(1)} collective-permute-done((bf16[200,1280]{1,0:T(8,128)(2,1)}, bf16[200,1280]{1,0:T(8,128)(2,1)S(1)}, u32[]{:S(2)}, u32[]{:S(2)}) %collective-permute-start.52) | collective-permute-done | bytes 512032 | tf_op jit(solution)/shard_map/reduce_up_proj/ppermute | solution.py:31
  603.3 7.1 %collective-permute-done.45.refs_1_ = bf16[2,40,1280]{2,1,0:T(8,128)(2,1)S(1)} collective-permute-done((bf16[2,40,1280]{2,1,0:T(8,128)(2,1)S(1)}, bf16[2,40,1280]{2,1,0:T(8,128)(2,1)S(1)}, u32[]{:S(2)}, u32[]{:S(2)}) %collective-permute-start.45) | collective-permute-done | bytes 204832 | tf_op jit(solution)/shard_map/reduce_in_proj/ppermute | solution.py:983
  (581 shorter events, 382.6 us)
Async XLA Ops:
  20.3 30.8 %collective-permute-start.4 = (bf16[512,1280]{1,0:T(8,128)(2,1)}, bf16[512,1280]{1,0:T(8,128)(2,1)S(1)}, u32[]{:S(2)}, u32[]{:S(2)}) collective-permute-start(bf16[512,1280]{1,0:T(8,128)(2,1)} %get-tuple-element.160), channel_id=1, source_target_pairs={{0,1},{1,0},{2,3},{3,2},{4,5},{5,4},{6,7},{7,6},{8,9},{9,8},{10,11... | collective-permute-start | bytes 3932168 | tf_op jit(solution)/shard_map/gather_tokens/ppermute | solution.py:31
  23.2 33.9 %collective-permute-start.5 = (bf16[512,1280]{1,0:T(8,128)(2,1)}, bf16[512,1280]{1,0:T(8,128)(2,1)S(1)}, u32[]{:S(2)}, u32[]{:S(2)}) collective-permute-start(bf16[512,1280]{1,0:T(8,128)(2,1)} %get-tuple-element.160), channel_id=1, source_target_pairs={{0,2},{1,3},{2,0},{3,1},{4,6},{5,7},{6,4},{7,5},{8,10},{9,11},{10,... | collective-permute-start | bytes 3932168 | tf_op jit(solution)/shard_map/gather_tokens/ppermute | solution.py:31
  61.9 24.8 %collective-permute-start.6 = (bf16[200,1280]{1,0:T(8,128)(2,1)}, bf16[200,1280]{1,0:T(8,128)(2,1)S(1)}, u32[]{:S(2)}, u32[]{:S(2)}) collective-permute-start(bf16[200,1280]{1,0:T(8,128)(2,1)} %get-tuple-element.163), channel_id=1, source_target_pairs={{0,4},{1,5},{2,6},{3,7},{4,0},{5,1},{6,2},{7,3},{8,12},{9,13},{10,... | collective-permute-start | bytes 1536008 | tf_op jit(solution)/shard_map/gather_up_and_out_proj/ppermute | solution.py:31
  64.3 33.5 %collective-permute-start.8 = (bf16[512,1280]{1,0:T(8,128)(2,1)}, bf16[512,1280]{1,0:T(8,128)(2,1)S(1)}, u32[]{:S(2)}, u32[]{:S(2)}) collective-permute-start(bf16[512,1280]{1,0:T(8,128)(2,1)} %get-tuple-element.173.refs_1_.refs_0_), channel_id=1, source_target_pairs={{0,1},{1,0},{2,3},{3,2},{4,5},{5,4},{6,7},{7,6},{8,9},{9,8},{10,11... | collective-permute-start | bytes 3932168 | tf_op jit(solution)/shard_map/gather_tokens/ppermute | solution.py:31
  90.0 24.4 %collective-permute-start.10 = (bf16[400,1280]{1,0:T(8,128)(2,1)}, bf16[400,1280]{1,0:T(8,128)(2,1)S(1)}, u32[]{:S(2)}, u32[]{:S(2)}) collective-permute-start(bf16[400,1280]{1,0:T(8,128)(2,1)} %pad_maximum_fusion.10), channel_id=1, source_target_pairs={{0,2},{1,3},{2,0},{3,1},{4,6},{5,7},{6,4},{7,5},{8,10},{9,11},{10,... | collective-permute-start | bytes 3072008 | tf_op jit(solution)/shard_map/gather_up_and_out_proj/ppermute | solution.py:31
  119.0 36.5 %collective-permute-start.13 = (bf16[800,1280]{1,0:T(8,128)(2,1)}, bf16[800,1280]{1,0:T(8,128)(2,1)}, u32[]{:S(2)}, u32[]{:S(2)}) collective-permute-start(bf16[800,1280]{1,0:T(8,128)(2,1)} %pad_maximum_fusion.4), channel_id=1, source_target_pairs={{0,1},{1,0},{2,3},{3,2},{4,5},{5,4},{6,7},{7,6},{8,24},{9,25},{10,... | collective-permute-start | bytes 6144008 | tf_op jit(solution)/shard_map/gather_up_and_out_proj/ppermute | solution.py:42
  120.3 21.0 %collective-permute-start.11 = (bf16[80,2560]{1,0:T(8,128)(2,1)S(1)}, bf16[80,2560]{1,0:T(8,128)(2,1)S(1)}, u32[]{:S(2)}, u32[]{:S(2)}) collective-permute-start(bf16[80,2560]{1,0:T(8,128)(2,1)S(1)} %copy-done.15), channel_id=1, source_target_pairs={{0,4},{1,5},{2,6},{3,7},{4,0},{5,1},{6,2},{7,3},{8,12},{9,13},{10,... | collective-permute-start | bytes 1228808 | tf_op jit(solution)/shard_map/gather_down_proj/ppermute | solution.py:31
  145.7 27.0 %collective-permute-start.16 = (bf16[160,2560]{1,0:T(8,128)(2,1)}, bf16[160,2560]{1,0:T(8,128)(2,1)S(1)}, u32[]{:S(2)}, u32[]{:S(2)}) collective-permute-start(bf16[160,2560]{1,0:T(8,128)(2,1)} %pad_maximum_fusion.11), channel_id=1, source_target_pairs={{0,2},{1,3},{2,0},{3,1},{4,6},{5,7},{6,4},{7,5},{8,10},{9,11},{10,... | collective-permute-start | bytes 2457608 | tf_op jit(solution)/shard_map/gather_down_proj/ppermute | solution.py:31
  230.0 52.1 %collective-permute-start.23 = (bf16[640,2560]{1,0:T(8,128)(2,1)}, bf16[640,2560]{1,0:T(8,128)(2,1)}, u32[]{:S(2)}, u32[]{:S(2)}) collective-permute-start(bf16[640,2560]{1,0:T(8,128)(2,1)} %constant_dynamic-update-slice_fusion.refs_1_), channel_id=1, source_target_pairs={{0,16},{1,17},{2,18},{3,19},{4,20},{5,21},{6,22},{7,23},{8,9},{9,8... | collective-permute-start | bytes 9830408 | tf_op jit(solution)/shard_map/gather_down_proj/ppermute | solution.py:42
  282.0 20.9 %collective-permute-start.25 = (bf16[4,80,2560]{2,1,0:T(8,128)(2,1)}, bf16[4,80,2560]{2,1,0:T(8,128)(2,1)S(1)}, u32[]{:S(2)}, u32[]{:S(2)}) collective-permute-start(bf16[4,80,2560]{2,1,0:T(8,128)(2,1)} %get-tuple-element.222), channel_id=1, source_target_pairs={{0,1},{1,0},{2,3},{3,2},{4,5},{5,4},{6,7},{7,6},{8,24},{9,25},{10,... | collective-permute-start | bytes 4915208 | tf_op jit(solution)/shard_map/reduce_down_proj/ppermute | solution.py:42
  321.8 27.0 %collective-permute-start.27 = (bf16[4,80,2560]{2,1,0:T(8,128)(2,1)S(1)}, bf16[4,80,2560]{2,1,0:T(8,128)(2,1)S(1)}, u32[]{:S(2)}, u32[]{:S(2)}) collective-permute-start(bf16[4,80,2560]{2,1,0:T(8,128)(2,1)S(1)} %copy-done.48), channel_id=1, source_target_pairs={{0,1},{1,0},{2,3},{3,2},{4,5},{5,4},{6,7},{7,6},{8,24},{9,25},{10,... | collective-permute-start | bytes 4915208 | tf_op jit(solution)/shard_map/reduce_down_proj/ppermute | solution.py:42
  376.7 27.8 %collective-permute-start.31 = (bf16[16,40,1280]{2,1,0:T(8,128)(2,1)}, bf16[16,40,1280]{2,1,0:T(8,128)(2,1)}, u32[]{:S(2)}, u32[]{:S(2)}) collective-permute-start(bf16[16,40,1280]{2,1,0:T(8,128)(2,1)} %dynamic-slice_bitcast_fusion), channel_id=1, source_target_pairs={{0,8},{8,0},{16,24},{24,16},{1,9},{9,1},{17,25},{25,17},{2,10},{10... | collective-permute-start | bytes 4915208 | tf_op jit(solution)/shard_map/reduce_up_proj/ppermute | solution.py:31
  381.9 37.0 %collective-permute-start.32 = (bf16[4,1,80,2560]{3,2,1,0:T(8,128)(2,1)}, bf16[4,1,80,2560]{3,2,1,0:T(8,128)(2,1)}, u32[]{:S(2)}, u32[]{:S(2)}) collective-permute-start(bf16[4,1,80,2560]{3,2,1,0:T(8,128)(2,1)} %fusion.26), channel_id=1, source_target_pairs={{0,16},{1,17},{2,18},{3,19},{4,20},{5,21},{6,22},{7,23},{8,9},{9,8... | collective-permute-start | bytes 4915208 | tf_op jit(solution)/shard_map/reduce_down_proj/ppermute | solution.py:42
  387.6 59.0 %collective-permute-start.33 = (bf16[4,2,160,1280]{3,2,1,0:T(8,128)(2,1)}, bf16[4,2,160,1280]{3,2,1,0:T(8,128)(2,1)}, u32[]{:S(2)}, u32[]{:S(2)}) collective-permute-start(bf16[4,2,160,1280]{3,2,1,0:T(8,128)(2,1)} %pad_maximum_fusion.1), channel_id=1, source_target_pairs={{0,1},{1,0},{2,3},{3,2},{4,5},{5,4},{6,7},{7,6},{8,24},{9,25},{10,... | collective-permute-start | bytes 9830408 | tf_op jit(solution)/shard_map/reduce_up_proj/ppermute | solution.py:42
  455.3 28.4 %collective-permute-start.36 = (bf16[4,1,200,1280]{3,2,1,0:T(8,128)(2,1)}, bf16[4,1,200,1280]{3,2,1,0:T(8,128)(2,1)}, u32[]{:S(2)}, u32[]{:S(2)}) collective-permute-start(bf16[4,1,200,1280]{3,2,1,0:T(8,128)(2,1)} %constant_dynamic-slice_fusion.1), channel_id=1, source_target_pairs={{0,16},{1,17},{2,18},{3,19},{4,20},{5,21},{6,22},{7,23},{8,9},{9,8... | collective-permute-start | bytes 6144008 | tf_op jit(solution)/shard_map/reduce_up_proj/ppermute | solution.py:42
  461.6 22.2 %collective-permute-start.37 = (bf16[80,2560]{1,0:T(8,128)(2,1)S(1)}, bf16[80,2560]{1,0:T(8,128)(2,1)S(1)}, u32[]{:S(2)}, u32[]{:S(2)}) collective-permute-start(bf16[80,2560]{1,0:T(8,128)(2,1)S(1)} %dynamic-slice_bitcast_fusion.9), channel_id=1, source_target_pairs={{0,4},{1,5},{2,6},{3,7},{4,0},{5,1},{6,2},{7,3},{8,12},{9,13},{10,... | collective-permute-start | bytes 1228808 | tf_op jit(solution)/shard_map/reduce_down_proj/ppermute | solution.py:31
  508.3 28.7 %collective-permute-start.40 = (bf16[2,200,1280]{2,1,0:T(8,128)(2,1)}, bf16[2,200,1280]{2,1,0:T(8,128)(2,1)S(1)}, u32[]{:S(2)}, u32[]{:S(2)}) collective-permute-start(bf16[2,200,1280]{2,1,0:T(8,128)(2,1)} %dynamic-slice_bitcast_fusion.4), channel_id=1, source_target_pairs={{0,2},{1,3},{2,0},{3,1},{4,6},{5,7},{6,4},{7,5},{8,10},{9,11},{10,... | collective-permute-start | bytes 3072008 | tf_op jit(solution)/shard_map/reduce_up_proj/ppermute | solution.py:31
  510.3 41.6 %collective-permute-start.42 = (bf16[160,2560]{1,0:T(8,128)(2,1)}, bf16[160,2560]{1,0:T(8,128)(2,1)}, u32[]{:S(2)}, u32[]{:S(2)}) collective-permute-start(bf16[160,2560]{1,0:T(8,128)(2,1)} %bitcast.119.refs_1_), channel_id=1, source_target_pairs={{0,8},{8,0},{16,24},{24,16},{1,9},{9,1},{17,25},{25,17},{2,10},{10... | collective-permute-start | bytes 2457608 | tf_op jit(solution)/shard_map/reduce_down_proj/ppermute | solution.py:31
  518.2 38.3 %collective-permute-start.43 = (bf16[512,1280]{1,0:T(8,128)(2,1)}, bf16[512,1280]{1,0:T(8,128)(2,1)}, u32[]{:S(2)}, u32[]{:S(2)}) collective-permute-start(bf16[512,1280]{1,0:T(8,128)(2,1)} %get-tuple-element.281), channel_id=1, source_target_pairs={{0,1},{1,0},{2,3},{3,2},{4,5},{5,4},{6,7},{7,6},{8,9},{9,8},{10,11... | collective-permute-start | bytes 3932168 | tf_op jit(solution)/shard_map/reduce_tokens/ppermute | solution.py:31
  527.0 29.5 %collective-permute-start.41 = (bf16[3,80,1280]{2,1,0:T(8,128)(2,1)}, bf16[3,80,1280]{2,1,0:T(8,128)(2,1)S(1)}, u32[]{:S(2)}, u32[]{:S(2)}) collective-permute-start(bf16[3,80,1280]{2,1,0:T(8,128)(2,1)} %dynamic-slice_bitcast_fusion.7), channel_id=1, source_target_pairs={{0,4},{1,5},{2,6},{3,7},{4,0},{5,1},{6,2},{7,3},{8,12},{9,13},{10,... | collective-permute-start | bytes 1843208 | tf_op jit(solution)/shard_map/reduce_in_proj/ppermute | solution.py:31
  538.0 50.5 %collective-permute-start.47 = (bf16[512,1280]{1,0:T(8,128)(2,1)}, bf16[512,1280]{1,0:T(8,128)(2,1)S(1)}, u32[]{:S(2)}, u32[]{:S(2)}) collective-permute-start(bf16[512,1280]{1,0:T(8,128)(2,1)} %get-tuple-element.288), channel_id=1, source_target_pairs={{0,1},{1,0},{2,3},{3,2},{4,5},{5,4},{6,7},{7,6},{8,9},{9,8},{10,11... | collective-permute-start | bytes 3932168 | tf_op jit(solution)/shard_map/reduce_tokens/ppermute | solution.py:31
  563.7 46.8 %collective-permute-start.48 = (bf16[512,1280]{1,0:T(8,128)(2,1)}, bf16[512,1280]{1,0:T(8,128)(2,1)S(1)}, u32[]{:S(2)}, u32[]{:S(2)}) collective-permute-start(bf16[512,1280]{1,0:T(8,128)(2,1)} %add_convert_fusion.4), channel_id=1, source_target_pairs={{0,2},{1,3},{2,0},{3,1},{4,6},{5,7},{6,4},{7,5},{8,10},{9,11},{10,... | collective-permute-start | bytes 3932168 | tf_op jit(solution)/shard_map/reduce_tokens/ppermute | solution.py:31
  567.8 35.5 %collective-permute-start.52 = (bf16[200,1280]{1,0:T(8,128)(2,1)}, bf16[200,1280]{1,0:T(8,128)(2,1)S(1)}, u32[]{:S(2)}, u32[]{:S(2)}) collective-permute-start(bf16[200,1280]{1,0:T(8,128)(2,1)} %dynamic-slice_bitcast_fusion.8), channel_id=1, source_target_pairs={{0,4},{1,5},{2,6},{3,7},{4,0},{5,1},{6,2},{7,3},{8,12},{9,13},{10,... | collective-permute-start | bytes 1536008 | tf_op jit(solution)/shard_map/reduce_up_proj/ppermute | solution.py:31
  580.2 30.3 %collective-permute-start.45 = (bf16[2,40,1280]{2,1,0:T(8,128)(2,1)S(1)}, bf16[2,40,1280]{2,1,0:T(8,128)(2,1)S(1)}, u32[]{:S(2)}, u32[]{:S(2)}) collective-permute-start(bf16[2,40,1280]{2,1,0:T(8,128)(2,1)S(1)} %slice.170), channel_id=1, source_target_pairs={{0,0},{2,1},{3,2},{1,3},{6,4},{4,5},{5,6},{7,7},{8,8},{10,9},{11,1... | collective-permute-start | bytes 614408 | tf_op jit(solution)/shard_map/reduce_in_proj/ppermute | solution.py:983
  (166 other events, 1088.3 us)
